TPU v7x, 32 devices: a whole 2x2x4 slice. The times are simulated.
32 devices in a mesh: dp: 32 (over z, y, x, core).
Axes of the slice: x: 2, y: 2, z: 4, core: 2. Of those that a mesh axis runs over, the one named last changes fastest.
Arguments:
- tokens: bfloat16 [32768, 768], P('dp'), may hold values from -12 to 12
- cotangent: bfloat16 [32768, 768], P('dp'), may hold values from -12 to 12
- lengths: int32 [32, 8], P('dp'), may hold values from 0 to 512, as said below
- w_qkv: bfloat16 [768, 2304], P('dp'), may hold values from -0.21875 to 0.21875
- w_out: bfloat16 [768, 768], P('dp'), may hold values from -0.875 to 0.875
- w_up: bfloat16 [768, 3072], P('dp'), may hold values from -0.21875 to 0.21875
- w_down: bfloat16 [3072, 768], P('dp'), may hold values from -0.109375 to 0.109375
- bias_q: bfloat16 [768], P('dp'), may hold values from -1.75 to 1.75
- bias_v: bfloat16 [768], P('dp'), may hold values from -1.75 to 1.75
- bias_out: bfloat16 [768], P('dp'), may hold values from -1.75 to 1.75
- gain_one: bfloat16 [768], P('dp'), may hold values from 0.5 to 1.5
- shift_one: bfloat16 [768], P('dp'), may hold values from -1.75 to 1.75
- bias_up: bfloat16 [3072], P('dp'), may hold values from -3 to 3
- bias_down: bfloat16 [768], P('dp'), may hold values from -1.75 to 1.75
- gain_two: bfloat16 [768], P('dp'), may hold values from 0.5 to 1.5
- shift_two: bfloat16 [768], P('dp'), may hold values from -1.75 to 1.75
Outputs:
- output: bfloat16 [32768, 768], P('dp')
- grad_tokens: float32 [32768, 768], P('dp')
- grad_w_qkv: float32 [768, 2304], P('dp')
- grad_w_out: float32 [768, 768], P('dp')
- grad_w_up: float32 [768, 3072], P('dp')
- grad_w_down: float32 [3072, 768], P('dp')
- grad_bias_q: float32 [768], P('dp')
- grad_bias_v: float32 [768], P('dp')
- grad_bias_out: float32 [768], P('dp')
- grad_gain_one: float32 [768], P('dp')
- grad_shift_one: float32 [768], P('dp')
- grad_bias_up: float32 [3072], P('dp')
- grad_bias_down: float32 [768], P('dp')
- grad_gain_two: float32 [768], P('dp')
- grad_shift_two: float32 [768], P('dp')
Inputs may be any that keep to these rules, and one draw needn't show every extreme that they name: Row d lists the lengths of the sequences packed on device d, laid end to end from its first row and followed by padding; its nonzero entries come first and are 128 or more, and they sum to at most 1024; some device holds exactly 2 sequences of 512 tokens.
All inputs are finite; a program needn't handle non-finite values.
Results may differ from a plain program's by a relative error of at most 0.014.
Values may be sent and summed in bfloat16 or wider, within the bound.
No kernel may reach another device: no remote copies, remote signals or barrier semaphores. Data moves between devices by JAX's collectives and lax.ppermute only.
A program may use at most 192 MiB of HBM per device.

v0:
```python
import math

import jax
import jax.numpy as jnp
from jax import lax
from jax.sharding import PartitionSpec as P

HD = 64


norm_eps = 1e-06


def normalize(values, gain, shift):
    center = jnp.mean(values, axis=-1, keepdims=True)
    centered = values - center
    spread = jnp.mean(centered * centered, axis=-1, keepdims=True)
    return centered * lax.rsqrt(spread + norm_eps) * gain + shift


def gelu_exact(values):
    return jax.nn.gelu(values, approximate=False)


def segments(length_row, row_count):
    bounds = jnp.cumsum(length_row)
    position = jnp.arange(row_count, dtype=jnp.int32)
    member = jnp.sum((position[:, None] >= bounds[None, :]).astype(jnp.int32), axis=1)
    valid = position < bounds[-1]
    return (jnp.where(valid, member, position + length_row.shape[0]), valid)


def split_heads(matrix):
    return matrix.reshape(matrix.shape[0], -1, HD).transpose(1, 0, 2)


def merge_heads(stacked):
    return stacked.transpose(1, 0, 2).reshape(stacked.shape[1], -1)


def attend_forward(query_h, keys_h, values_h, segment, scale_factor):
    row_count = query_h.shape[1]
    block_rows = min(512, row_count)
    block_count = row_count // block_rows
    segment_blocks = segment.reshape(block_count, block_rows)

    def one_head(operands):
        query_one, keys_one, values_one = operands

        def one_block(paired):
            query_part, segment_part = paired
            scores = (
                jnp.einsum("qd,kd->qk", query_part, keys_one, preferred_element_type=jnp.float32)
                * scale_factor
            )
            scores = jnp.where(segment_part[:, None] == segment[None, :], scores, -1000000000.0)
            highest = jnp.max(scores, axis=1, keepdims=True)
            weights = jnp.exp(scores - highest)
            totals = jnp.sum(weights, axis=1, keepdims=True)
            probs_low = (weights / totals).astype(jnp.bfloat16)
            mixed = jnp.dot(probs_low, values_one, preferred_element_type=jnp.float32)
            return (mixed, (highest + jnp.log(totals))[:, 0])

        mixed, log_total = lax.map(
            one_block, (query_one.reshape(block_count, block_rows, HD), segment_blocks)
        )
        return (mixed.reshape(row_count, HD), log_total.reshape(row_count))

    return lax.map(one_head, (query_h, keys_h, values_h))


def attend_backward(query_h, keys_h, values_h, grad_mixed_h, log_total, segment, scale_factor):
    row_count = query_h.shape[1]
    block_rows = min(512, row_count)
    block_count = row_count // block_rows
    segment_blocks = segment.reshape(block_count, block_rows)

    def one_head(operands):
        query_one, keys_one, values_one, grad_one, lse_one = operands

        def one_block(carry, items):
            grad_keys, grad_values = carry
            query_part, grad_part, lse_part, segment_part = items
            scores = (
                jnp.einsum("qd,kd->qk", query_part, keys_one, preferred_element_type=jnp.float32)
                * scale_factor
            )
            scores = jnp.where(segment_part[:, None] == segment[None, :], scores, -1000000000.0)
            probs = jnp.exp(scores - lse_part[:, None])
            grad_probs = jnp.einsum(
                "qd,kd->qk", grad_part, values_one, preferred_element_type=jnp.float32
            )
            inner_sum = jnp.sum(probs * grad_probs, axis=1, keepdims=True)
            grad_scores = (probs * (grad_probs - inner_sum)).astype(jnp.bfloat16)
            grad_query = (
                jnp.dot(grad_scores, keys_one, preferred_element_type=jnp.float32) * scale_factor
            )
            grad_keys = (
                grad_keys
                + jnp.einsum(
                    "qk,qd->kd", grad_scores, query_part, preferred_element_type=jnp.float32
                )
                * scale_factor
            )
            grad_values = grad_values + jnp.einsum(
                "qk,qd->kd",
                probs.astype(jnp.bfloat16),
                grad_part,
                preferred_element_type=jnp.float32,
            )
            return ((grad_keys, grad_values), grad_query)

        zeros_init = jnp.zeros((row_count, HD), jnp.float32)
        items = (
            query_one.reshape(block_count, block_rows, HD),
            grad_one.reshape(block_count, block_rows, HD),
            lse_one.reshape(block_count, block_rows),
            segment_blocks,
        )
        (grad_keys, grad_values), grad_query = lax.scan(one_block, (zeros_init, zeros_init), items)
        return (grad_query.reshape(row_count, HD), grad_keys, grad_values)

    return lax.map(one_head, (query_h, keys_h, values_h, grad_mixed_h, log_total))


def body(
    tokens,
    cotangent,
    lengths,
    w_qkv,
    w_out,
    w_up,
    w_down,
    bias_q,
    bias_v,
    bias_out,
    gain_one,
    shift_one,
    bias_up,
    bias_down,
    gain_two,
    shift_two,
):
    row_count = tokens.shape[0]
    segment, valid = segments(lengths[0], row_count)
    scale_factor = 1.0 / math.sqrt(HD)
    full_qkv, full_out, full_bias_q, full_bias_v, full_bias_out, full_gain_one, full_shift_one = (
        lax.all_gather(w_qkv, "dp", axis=0, tiled=True),
        lax.all_gather(w_out, "dp", axis=0, tiled=True),
        lax.all_gather(bias_q, "dp", axis=0, tiled=True),
        lax.all_gather(bias_v, "dp", axis=0, tiled=True),
        lax.all_gather(bias_out, "dp", axis=0, tiled=True),
        lax.all_gather(gain_one, "dp", axis=0, tiled=True),
        lax.all_gather(shift_one, "dp", axis=0, tiled=True),
    )
    width = full_out.shape[0]
    projected = jnp.dot(tokens, full_qkv, preferred_element_type=jnp.float32)
    query = (projected[:, :width] + full_bias_q).astype(jnp.bfloat16)
    keys = projected[:, width : 2 * width].astype(jnp.bfloat16)
    values = (projected[:, 2 * width :] + full_bias_v).astype(jnp.bfloat16)
    query_h = split_heads(query)
    keys_h = split_heads(keys)
    values_h = split_heads(values)
    mixed_h, log_total = attend_forward(query_h, keys_h, values_h, segment, scale_factor)
    mixed = merge_heads(mixed_h).astype(jnp.bfloat16)
    pre_one = (
        tokens.astype(jnp.float32)
        + jnp.dot(mixed, full_out, preferred_element_type=jnp.float32)
        + full_bias_out
    )
    hidden, norm_one_back = jax.vjp(
        normalize, pre_one, full_gain_one.astype(jnp.float32), full_shift_one.astype(jnp.float32)
    )
    full_up, full_down, full_bias_up, full_bias_down, full_gain_two, full_shift_two = (
        lax.all_gather(w_up, "dp", axis=0, tiled=True),
        lax.all_gather(w_down, "dp", axis=0, tiled=True),
        lax.all_gather(bias_up, "dp", axis=0, tiled=True),
        lax.all_gather(bias_down, "dp", axis=0, tiled=True),
        lax.all_gather(gain_two, "dp", axis=0, tiled=True),
        lax.all_gather(shift_two, "dp", axis=0, tiled=True),
    )
    hidden_low = hidden.astype(jnp.bfloat16)
    up_pre = jnp.dot(hidden_low, full_up, preferred_element_type=jnp.float32) + full_bias_up
    active, gelu_back = jax.vjp(gelu_exact, up_pre)
    active_low = active.astype(jnp.bfloat16)
    pre_two = (
        hidden + jnp.dot(active_low, full_down, preferred_element_type=jnp.float32) + full_bias_down
    )
    normed, norm_two_back = jax.vjp(
        normalize, pre_two, full_gain_two.astype(jnp.float32), full_shift_two.astype(jnp.float32)
    )
    output = jnp.where(valid[:, None], normed, 0.0).astype(jnp.bfloat16)
    back_up, back_down = (
        lax.all_gather(w_up, "dp", axis=0, tiled=True),
        lax.all_gather(w_down, "dp", axis=0, tiled=True),
    )
    grad_out = jnp.where(valid[:, None], cotangent.astype(jnp.float32), 0.0)
    grad_pre_two, grad_gain_two, grad_shift_two = norm_two_back(grad_out)
    grad_branch = grad_pre_two.astype(jnp.bfloat16)
    grad_bias_down = jnp.sum(grad_branch, axis=0, dtype=jnp.float32)
    grad_w_down = jnp.einsum(
        "tf,td->fd", active_low, grad_branch, preferred_element_type=jnp.float32
    )
    grad_active = jnp.einsum(
        "td,fd->tf", grad_branch, back_down, preferred_element_type=jnp.float32
    )
    (grad_up_pre,) = gelu_back(grad_active)
    grad_up = grad_up_pre.astype(jnp.bfloat16)
    grad_bias_up = jnp.sum(grad_up, axis=0, dtype=jnp.float32)
    grad_w_up = jnp.einsum("td,tf->df", hidden_low, grad_up, preferred_element_type=jnp.float32)
    grad_hidden = grad_pre_two + jnp.einsum(
        "tf,df->td", grad_up, back_up, preferred_element_type=jnp.float32
    )
    mlp_grads = (
        lax.psum_scatter(grad_w_up, "dp", scatter_dimension=0, tiled=True),
        lax.psum_scatter(grad_w_down, "dp", scatter_dimension=0, tiled=True),
        lax.psum_scatter(grad_bias_up, "dp", scatter_dimension=0, tiled=True),
        lax.psum_scatter(grad_bias_down, "dp", scatter_dimension=0, tiled=True),
        lax.psum_scatter(grad_gain_two, "dp", scatter_dimension=0, tiled=True),
        lax.psum_scatter(grad_shift_two, "dp", scatter_dimension=0, tiled=True),
    )
    grad_pre_one, grad_gain_one, grad_shift_one = norm_one_back(grad_hidden)
    back_qkv, back_out = (
        lax.all_gather(w_qkv, "dp", axis=0, tiled=True),
        lax.all_gather(w_out, "dp", axis=0, tiled=True),
    )
    grad_attn = grad_pre_one.astype(jnp.bfloat16)
    grad_bias_out = jnp.sum(grad_attn, axis=0, dtype=jnp.float32)
    grad_w_out = jnp.einsum("td,te->de", mixed, grad_attn, preferred_element_type=jnp.float32)
    grad_mixed = jnp.einsum(
        "te,de->td", grad_attn, back_out, preferred_element_type=jnp.float32
    ).astype(jnp.bfloat16)
    grad_query_h, grad_keys_h, grad_values_h = attend_backward(
        query_h, keys_h, values_h, split_heads(grad_mixed), log_total, segment, scale_factor
    )
    grad_qkv = jnp.concatenate(
        [merge_heads(grad_query_h), merge_heads(grad_keys_h), merge_heads(grad_values_h)], axis=1
    ).astype(jnp.bfloat16)
    grad_bias_q = jnp.sum(grad_qkv[:, :width], axis=0, dtype=jnp.float32)
    grad_bias_v = jnp.sum(grad_qkv[:, 2 * width :], axis=0, dtype=jnp.float32)
    grad_w_qkv = jnp.einsum("td,te->de", tokens, grad_qkv, preferred_element_type=jnp.float32)
    grad_tokens = grad_pre_one + jnp.einsum(
        "te,de->td", grad_qkv, back_qkv, preferred_element_type=jnp.float32
    )
    attn_grads = (
        lax.psum_scatter(grad_w_qkv, "dp", scatter_dimension=0, tiled=True),
        lax.psum_scatter(grad_w_out, "dp", scatter_dimension=0, tiled=True),
        lax.psum_scatter(grad_bias_q, "dp", scatter_dimension=0, tiled=True),
        lax.psum_scatter(grad_bias_v, "dp", scatter_dimension=0, tiled=True),
        lax.psum_scatter(grad_bias_out, "dp", scatter_dimension=0, tiled=True),
        lax.psum_scatter(grad_gain_one, "dp", scatter_dimension=0, tiled=True),
        lax.psum_scatter(grad_shift_one, "dp", scatter_dimension=0, tiled=True),
    )
    return (
        output,
        grad_tokens,
        attn_grads[0],
        attn_grads[1],
        mlp_grads[0],
        mlp_grads[1],
        attn_grads[2],
        attn_grads[3],
        attn_grads[4],
        attn_grads[5],
        attn_grads[6],
        mlp_grads[2],
        mlp_grads[3],
        mlp_grads[4],
        mlp_grads[5],
    )


def solution(mesh):
    in_specs = (
        P("dp", None),
        P("dp", None),
        P("dp", None),
        P("dp", None),
        P("dp", None),
        P("dp", None),
        P("dp", None),
        P("dp"),
        P("dp"),
        P("dp"),
        P("dp"),
        P("dp"),
        P("dp"),
        P("dp"),
        P("dp"),
        P("dp"),
    )
    out_specs = (
        P("dp", None),
        P("dp", None),
        P("dp", None),
        P("dp", None),
        P("dp", None),
        P("dp", None),
        P("dp"),
        P("dp"),
        P("dp"),
        P("dp"),
        P("dp"),
        P("dp"),
        P("dp"),
        P("dp"),
        P("dp"),
    )
    return jax.shard_map(body, mesh=mesh, in_specs=in_specs, out_specs=out_specs, check_vma=False)
```

profile of v0, /device:TPU:0, one launch (start us, length us, event | category | flops | bytes accessed | tf_op | source)
XLA Modules:
  0.0 1058.7 jit_solution(10867048414736670059)
XLA Ops:
  21.0 42.5 %all-reduce.19 = (bf16[768]{0:T(1024)(128)(2,1)S(1)}, bf16[768]{0:T(1024)(128)(2,1)S(1)}, bf16[768]{0:T(1024)(128)(2,1)S(1)}, bf16[768]{0:T(1024)(128)(2,1)S(1)}...) all-reduce(bf16[768]{0:T(1024)(128)(2,1)S(1)} %dynamic-update-slice, ...), channel_id=1, replica_groups=mesh['dp'=32] {'dp'}, use_global_device_ids=true, to_apply=%add | all-reduce | flops 9216 | bytes 36864
  96.6 94.8 %while.54 = (s32[]{:T(128)}, bf16[12,1024,64]{1,2,0:T(8,128)(2,1)}, f32[12,1024]{1,0:T(8,128)}, bf16[12,1024,64]{2,1,0:T(8,128)(2,1)}, bf16[12,1024,64]{2,1,0:T(...) while((s32[]{:T(128)}, bf16[12,1024,64]{1,2,0:T(8,128)(2,1)}, ...), condition=%wide.region_7.8_spmd, body=%wide.region_2.7_spmd.sunk | while | flops 138935808 | bytes 8698702 | solution.py:69
  195.8 38.2 %multiply_convert_fusion.1 = (bf16[1024,3072]{1,0:T(8,128)(2,1)}, f32[1024,3072]{1,0:T(8,128)}, f32[1024,3072]{1,0:T(8,128)}) fusion(f32[3072]{0:T(1024)S(1)} %convert_element_type.111, bf16[768,3072]{1,0:T(8,128)(2,1)} %all-gather.9.cloned.1.call-done, f32[1024,768]{0,1:T(8,128)S(1)} %get-tuple-element.512, f32[768]{0:T(1024)S(1)} %convert_element_type.109, ...), kind=kOutput, calls=%fused_computation.52 | convolution fusion | flops 5043388416 | bytes 39348224 | tf_op jit(solution)/shard_map/dot_general | solution.py:183
  234.0 26.6 %all-gather.11.cloned.1.call-done = bf16[3072,768]{1,0:T(8,128)(2,1)} async-done(((bf16[96,768]{1,0:T(8,128)(2,1)}), bf16[3072,768]{1,0:T(8,128)(2,1)}) %all-gather.11.cloned.1.call-update) | async-done | bytes 4718608 | tf_op jit(solution)/shard_map/all_gather | solution.py:176
  277.8 18.1 %convert_reduce_fusion = (f32[3072]{0:T(1024)}, bf16[1024,3072]{1,0:T(8,128)(2,1)}) fusion(f32[1024,3072]{1,0:T(8,128)} %get-tuple-element.497, bf16[1024,768]{0,1:T(8,128)(2,1)S(1)} %get-tuple-element.491, bf16[3072,768]{1,0:T(8,128)(2,1)} %all-gather.11.cloned.1.call-done, f32[1024,3072]{1,0:T(8,128)} %get-tuple-element.513, ...), kind=kOutput, calls=%fused_computation.50 | convolution fusion | flops 4885312512 | bytes 37773312 | tf_op jit(solution)/shard_map/td,fd->tf/dot_general | solution.py:204
  295.9 11.7 %multiply_reduce_fusion.2 = (f32[768]{0:T(1024)}, f32[1024]{0:T(1024)S(1)}, f32[768]{0:T(1024)}, f32[1024,768]{0,1:T(8,128)S(1)}) fusion(f32[1024,768]{0,1:T(8,128)} %copy-done.1, f32[1024]{0:T(1024)S(1)} %fusion.34, f32[1024]{0:T(1024)S(1)} %broadcast_multiply_fusion.1, f32[768]{0:T(1024)S(1)} %convert_element_type.108, ...), kind=kOutput, calls=%fused_computation.77 | convolution fusion | flops 4845990912 | bytes 22062080 | tf_op jit(solution)/shard_map/tf,df->td/dot_general | solution.py:211
  323.5 307.8 %while.56 = (s32[]{:T(128)}, bf16[12,1024,64]{1,2,0:T(8,128)(2,1)}, bf16[12,1024,64]{1,2,0:T(8,128)(2,1)}, bf16[12,1024,64]{1,2,0:T(8,128)(2,1)}, bf16[12,1024,6...) while((s32[]{:T(128)}, bf16[12,1024,64]{1,2,0:T(8,128)(2,1)}, ...), condition=%wide.region_20.21_spmd, body=%wide.region_16.20_spmd.sunk | while | flops 341147136 | bytes 21011892 | solution.py:123
  330.5 16.1 %while.58 = (s32[]{:T(128)}, f32[1024,64]{0,1:T(8,128)}, f32[1024,64]{0,1:T(8,128)}, bf16[2,512,64]{1,2,0:T(8,128)(2,1)S(1)}, s32[2,512]{1,0:T(2,128)S(1)}, /*in...) while((s32[]{:T(128)}, f32[1024,64]{0,1:T(8,128)}, ...), condition=%wide.region_19.19_spmd.clone, body=%wide.region_17.18_spmd.clone.sunk | while | flops 341147136 | bytes 18110612 | solution.py:120
  356.2 16.1 %while.58 = (s32[]{:T(128)}, f32[1024,64]{0,1:T(8,128)}, f32[1024,64]{0,1:T(8,128)}, bf16[2,512,64]{1,2,0:T(8,128)(2,1)S(1)}, s32[2,512]{1,0:T(2,128)S(1)}, /*in...) while((s32[]{:T(128)}, f32[1024,64]{0,1:T(8,128)}, ...), condition=%wide.region_19.19_spmd.clone, body=%wide.region_17.18_spmd.clone.sunk | while | flops 341147136 | bytes 18110612 | solution.py:120
  381.9 16.1 %while.58 = (s32[]{:T(128)}, f32[1024,64]{0,1:T(8,128)}, f32[1024,64]{0,1:T(8,128)}, bf16[2,512,64]{1,2,0:T(8,128)(2,1)S(1)}, s32[2,512]{1,0:T(2,128)S(1)}, /*in...) while((s32[]{:T(128)}, f32[1024,64]{0,1:T(8,128)}, ...), condition=%wide.region_19.19_spmd.clone, body=%wide.region_17.18_spmd.clone.sunk | while | flops 341147136 | bytes 18110612 | solution.py:120
  407.5 16.1 %while.58 = (s32[]{:T(128)}, f32[1024,64]{0,1:T(8,128)}, f32[1024,64]{0,1:T(8,128)}, bf16[2,512,64]{1,2,0:T(8,128)(2,1)S(1)}, s32[2,512]{1,0:T(2,128)S(1)}, /*in...) while((s32[]{:T(128)}, f32[1024,64]{0,1:T(8,128)}, ...), condition=%wide.region_19.19_spmd.clone, body=%wide.region_17.18_spmd.clone.sunk | while | flops 341147136 | bytes 18110612 | solution.py:120
  433.2 16.1 %while.58 = (s32[]{:T(128)}, f32[1024,64]{0,1:T(8,128)}, f32[1024,64]{0,1:T(8,128)}, bf16[2,512,64]{1,2,0:T(8,128)(2,1)S(1)}, s32[2,512]{1,0:T(2,128)S(1)}, /*in...) while((s32[]{:T(128)}, f32[1024,64]{0,1:T(8,128)}, ...), condition=%wide.region_19.19_spmd.clone, body=%wide.region_17.18_spmd.clone.sunk | while | flops 341147136 | bytes 18110612 | solution.py:120
  458.8 16.1 %while.58 = (s32[]{:T(128)}, f32[1024,64]{0,1:T(8,128)}, f32[1024,64]{0,1:T(8,128)}, bf16[2,512,64]{1,2,0:T(8,128)(2,1)S(1)}, s32[2,512]{1,0:T(2,128)S(1)}, /*in...) while((s32[]{:T(128)}, f32[1024,64]{0,1:T(8,128)}, ...), condition=%wide.region_19.19_spmd.clone, body=%wide.region_17.18_spmd.clone.sunk | while | flops 341147136 | bytes 18110612 | solution.py:120
  484.4 16.1 %while.58 = (s32[]{:T(128)}, f32[1024,64]{0,1:T(8,128)}, f32[1024,64]{0,1:T(8,128)}, bf16[2,512,64]{1,2,0:T(8,128)(2,1)S(1)}, s32[2,512]{1,0:T(2,128)S(1)}, /*in...) while((s32[]{:T(128)}, f32[1024,64]{0,1:T(8,128)}, ...), condition=%wide.region_19.19_spmd.clone, body=%wide.region_17.18_spmd.clone.sunk | while | flops 341147136 | bytes 18110612 | solution.py:120
  510.0 16.1 %while.58 = (s32[]{:T(128)}, f32[1024,64]{0,1:T(8,128)}, f32[1024,64]{0,1:T(8,128)}, bf16[2,512,64]{1,2,0:T(8,128)(2,1)S(1)}, s32[2,512]{1,0:T(2,128)S(1)}, /*in...) while((s32[]{:T(128)}, f32[1024,64]{0,1:T(8,128)}, ...), condition=%wide.region_19.19_spmd.clone, body=%wide.region_17.18_spmd.clone.sunk | while | flops 341147136 | bytes 18110612 | solution.py:120
  535.6 16.1 %while.58 = (s32[]{:T(128)}, f32[1024,64]{0,1:T(8,128)}, f32[1024,64]{0,1:T(8,128)}, bf16[2,512,64]{1,2,0:T(8,128)(2,1)S(1)}, s32[2,512]{1,0:T(2,128)S(1)}, /*in...) while((s32[]{:T(128)}, f32[1024,64]{0,1:T(8,128)}, ...), condition=%wide.region_19.19_spmd.clone, body=%wide.region_17.18_spmd.clone.sunk | while | flops 341147136 | bytes 18110612 | solution.py:120
  561.3 16.1 %while.58 = (s32[]{:T(128)}, f32[1024,64]{0,1:T(8,128)}, f32[1024,64]{0,1:T(8,128)}, bf16[2,512,64]{1,2,0:T(8,128)(2,1)S(1)}, s32[2,512]{1,0:T(2,128)S(1)}, /*in...) while((s32[]{:T(128)}, f32[1024,64]{0,1:T(8,128)}, ...), condition=%wide.region_19.19_spmd.clone, body=%wide.region_17.18_spmd.clone.sunk | while | flops 341147136 | bytes 18110612 | solution.py:120
  586.9 16.1 %while.58 = (s32[]{:T(128)}, f32[1024,64]{0,1:T(8,128)}, f32[1024,64]{0,1:T(8,128)}, bf16[2,512,64]{1,2,0:T(8,128)(2,1)S(1)}, s32[2,512]{1,0:T(2,128)S(1)}, /*in...) while((s32[]{:T(128)}, f32[1024,64]{0,1:T(8,128)}, ...), condition=%wide.region_19.19_spmd.clone, body=%wide.region_17.18_spmd.clone.sunk | while | flops 341147136 | bytes 18110612 | solution.py:120
  612.5 16.1 %while.58 = (s32[]{:T(128)}, f32[1024,64]{0,1:T(8,128)}, f32[1024,64]{0,1:T(8,128)}, bf16[2,512,64]{1,2,0:T(8,128)(2,1)S(1)}, s32[2,512]{1,0:T(2,128)S(1)}, /*in...) while((s32[]{:T(128)}, f32[1024,64]{0,1:T(8,128)}, ...), condition=%wide.region_19.19_spmd.clone, body=%wide.region_17.18_spmd.clone.sunk | while | flops 341147136 | bytes 18110612 | solution.py:120
  662.5 10.7 %fusion.38 = f32[768,3072]{1,0:T(8,128)} fusion(bf16[1024,3072]{1,0:T(8,128)(2,1)} %get-tuple-element.518, f32[1024,768]{0,1:T(8,128)S(1)} %copy-done.3, f32[768]{0:T(1024)S(1)} %copy-done.33, f32[768]{0:T(1024)S(1)} %copy-done.20, f32[1024]{0:T(1024)S(1)} %copy-done.24, f32[1024]{0:T(1024)S(1)} %copy-done.18), kind=kOutput, calls=%fused_computation.116 | convolution fusion | flops 4835770368 | bytes 18888704 | tf_op jit(solution)/shard_map/td,tf->df/dot_general | solution.py:210
  676.0 41.3 %all-reduce.18 = (f32[768]{0:T(1024)S(1)}, f32[768]{0:T(1024)S(1)}, f32[768]{0:T(1024)S(1)}, f32[768]{0:T(1024)S(1)}, f32[768]{0:T(1024)S(1)}, /*index=5*/f32[30...) all-reduce(f32[768]{0:T(1024)S(1)} %get-tuple-element.520, ...), channel_id=6, replica_groups=mesh['dp'=32] {'dp'}, use_global_device_ids=true, to_apply=%region_26.27.clone | all-reduce | flops 9216 | bytes 73728
  737.0 30.9 %reduce-scatter.13.cloned.1.call-done = f32[24,2304]{1,0:T(8,128)} async-done(((f32[768,2304]{1,0:T(8,128)}), f32[24,2304]{1,0:T(8,128)}) %reduce-scatter.13.cloned.1.call-update) | async-done | bytes 221200
  767.9 141.5 %reduce-scatter.11.cloned.1.call-done = f32[96,768]{1,0:T(8,128)} async-done(((f32[3072,768]{1,0:T(8,128)}), f32[96,768]{1,0:T(8,128)}) %reduce-scatter.11.cloned.1.call-update) | async-done | bytes 294928 | tf_op jit(solution)/shard_map/reduce_scatter | solution.py:216
  909.3 142.0 %reduce-scatter.9.cloned.1.call-done = f32[24,3072]{1,0:T(8,128)} async-done(((f32[768,3072]{1,0:T(8,128)}), f32[24,3072]{1,0:T(8,128)}) %reduce-scatter.9.cloned.1.call-update) | async-done | bytes 294928 | tf_op jit(solution)/shard_map/reduce_scatter | solution.py:215
  (790 shorter events, 578.3 us)
Async XLA Ops:
  7.2 60.9 %copy-start.11 = (bf16[1024,768]{1,0:T(8,128)(2,1)S(1)}, bf16[1024,768]{1,0:T(8,128)(2,1)}, u32[]{:S(2)}) copy-start(bf16[1024,768]{1,0:T(8,128)(2,1)} %param.25) | copy-start | bytes 4718596
  7.2 67.3 %all-gather.5.cloned.1.call-start = ((), (), s32[]{:S(2)}) async-start(), calls=%async_computation.4 | async-start | bytes 3649536 | tf_op jit(solution)/shard_map/all_gather | solution.py:148
  7.9 183.5 %all-gather.7.cloned.1.call-start = ((), (), s32[]{:S(2)}) async-start(), calls=%async_computation.5 | async-start | bytes 1216512 | tf_op jit(solution)/shard_map/all_gather | solution.py:149
  8.7 187.2 %all-gather.9.cloned.1.call-start = ((), (), s32[]{:S(2)}) async-start(), calls=%async_computation.6 | async-start | bytes 4866048 | tf_op jit(solution)/shard_map/all_gather | solution.py:175
  9.4 251.2 %all-gather.11.cloned.1.call-start = ((), (), s32[]{:S(2)}) async-start(), calls=%async_computation.7 | async-start | bytes 4866048 | tf_op jit(solution)/shard_map/all_gather | solution.py:176
  10.0 727.0 %reduce-scatter.7.cloned.1.call-start = ((), (), s32[]{:S(2)}) async-start(), calls=%async_computation.8 | async-start | bytes 2433024 | tf_op jit(solution)/shard_map/reduce_scatter | solution.py:247
  64.1 10.3 copy-start.12
  66.9 240.7 %copy-start.19 = (f32[768]{0:T(1024)}, f32[768]{0:T(1024)S(1)}, u32[]{:S(2)}) copy-start(f32[768]{0:T(1024)S(1)} %convert_element_type.108) | copy-start | bytes 9220
  66.9 193.8 %copy-start.32 = (f32[768]{0:T(1024)}, f32[768]{0:T(1024)S(1)}, u32[]{:S(2)}) copy-start(f32[768]{0:T(1024)S(1)} %convert_element_type.109) | copy-start | bytes 9220
  195.4 38.6 %copy-start.1 = (f32[1024,768]{0,1:T(8,128)}, f32[1024,768]{0,1:T(8,128)S(1)}, u32[]{:S(2)}) copy-start(f32[1024,768]{0,1:T(8,128)S(1)} %get-tuple-element.512) | copy-start | bytes 9437188
  195.4 112.2 %copy-start.17 = (f32[1024]{0:T(1024)}, f32[1024]{0:T(1024)S(1)}, u32[]{:S(2)}) copy-start(f32[1024]{0:T(1024)S(1)} %broadcast_multiply_fusion.1) | copy-start | bytes 12292
  195.8 111.8 %copy-start.23 = (f32[1024]{0:T(1024)}, f32[1024]{0:T(1024)S(1)}, u32[]{:S(2)}) copy-start(f32[1024]{0:T(1024)S(1)} %fusion.34) | copy-start | bytes 12292
  195.8 64.8 %copy-start.34 = (f32[768]{0:T(1024)S(1)}, f32[768]{0:T(1024)}, u32[]{:S(2)}) copy-start(f32[768]{0:T(1024)} %convert_element_type.113) | copy-start | bytes 9220
  260.6 9.9 copy-start
  260.6 9.9 copy-start.16
  260.6 9.9 copy-start.31
  277.8 18.1 %copy-start.14 = (bf16[1024,768]{0,1:T(8,128)(2,1)}, bf16[1024,768]{0,1:T(8,128)(2,1)S(1)}, u32[]{:S(2)}) copy-start(bf16[1024,768]{0,1:T(8,128)(2,1)S(1)} %get-tuple-element.491) | copy-start | bytes 4718596
  295.9 11.7 %copy-start.2 = (f32[1024,768]{0,1:T(8,128)S(1)}, f32[1024,768]{0,1:T(8,128)}, u32[]{:S(2)}) copy-start(f32[1024,768]{0,1:T(8,128)} %copy-done.1) | copy-start | bytes 9437188
  319.4 4.2 copy-start.10
  319.4 448.5 %reduce-scatter.13.cloned.1.call-start = ((), (), s32[]{:S(2)}) async-start(), calls=%async_computation.11 | async-start | bytes 7299072
  649.0 260.4 %reduce-scatter.11.cloned.1.call-start = ((), (), s32[]{:S(2)}) async-start(), calls=%async_computation.10 | async-start | bytes 9732096 | tf_op jit(solution)/shard_map/reduce_scatter | solution.py:216
  660.5 390.9 %reduce-scatter.9.cloned.1.call-start = ((), (), s32[]{:S(2)}) async-start(), calls=%async_computation.9 | async-start | bytes 9732096 | tf_op jit(solution)/shard_map/reduce_scatter | solution.py:215
  673.3 48.7 %copy-start.5 = (f32[1024,768]{0,1:T(8,128)S(1)}, f32[1024,768]{0,1:T(8,128)}, u32[]{:S(2)}) copy-start(f32[1024,768]{0,1:T(8,128)} %copy-done.4) | copy-start | bytes 9437188
  673.3 48.7 %copy-start.22 = (f32[1024]{0:T(1024)S(1)}, f32[1024]{0:T(1024)}, u32[]{:S(2)}) copy-start(f32[1024]{0:T(1024)} %copy-done.21) | copy-start | bytes 12292
  (21 other events, 55.3 us)
Sparse Core Ops, SparseCore 0:
  10.9 63.4 all-gather.4
  77.4 52.6 all-gather.6
  133.0 62.3 all-gather.8
  198.1 62.4 all-gather.10
  319.5 97.8 reduce-scatter.6
  649.1 118.7 reduce-scatter.12
  774.4 134.9 reduce-scatter.10
  916.8 134.5 reduce-scatter.8
where the time goes:
time: 1070 us; the launch traced here: 1060 us
  waiting for transfers between devices  348 us (33%)
  matrix products  345 us (32%)
  local copies, waits for them, and re-layouts  226 us (21%)
  blocking collectives  83.8 us (8%)
  other arithmetic  37.6 us (4%)
  between operations  15.1 us (1%)
    reduce_scatter x1, waiting for transfers between devices, body(): lax.psum_scatter(grad_w_up, 'dp', scatter_dimension=0, tiled=True)  142 us
    reduce_scatter x1, waiting for transfers between devices, body(): lax.psum_scatter(grad_w_down, 'dp', scatter_dimension=0, tiled=True)  141 us
    unnamed x2, blocking collectives  83.8 us
    dynamic_update_slice x72, local copies, waits for them, and re-layouts, attend_forward(): return lax.map(one_head, (query_h, keys_h, values_h))  56.9 us
    dot_general x48, matrix products, one_block(): jnp.einsum('qd,kd->qk', query_part, keys_one, preferred_element_type=jnp....  56.1 us
    dynamic_slice x36, local copies, waits for them, and re-layouts, attend_forward(): return lax.map(one_head, (query_h, keys_h, values_h))  51.9 us
    dot_general x24, matrix products, one_block(): jnp.einsum('qk,qd->kd', grad_scores, query_part, preferred_element_type=j...  48.4 us
    dot_general x24, matrix products, one_block(): jnp.einsum('qk,qd->kd', probs.astype(jnp.bfloat16), grad_part, preferred_...  48.3 us
  transfers between devices with their start and end apart: 8, of which 5 were waited for; matrix products, arithmetic and copies ran while one was open for 52% of the time, Pallas kernels for 0%

commit v1 on v0

v1 whole, which is shorter than its diff:
```python
import functools
import math

import jax
import jax.numpy as jnp
import numpy as np
from jax import lax
from jax.experimental import pallas as pl
from jax.experimental.pallas import tpu as pltpu
from jax.sharding import PartitionSpec as P

HD = 64
QB = 256
KB = 128
TB = 256
FB = 768
BLOCKS = 32
NORM_EPS = 1e-06
MASKED = -1000000000.0
SCALE = 1.0 / math.sqrt(HD)
NT = (((1,), (1,)), ((), ()))
TN = (((0,), (0,)), ((), ()))
f32 = jnp.float32
bf16 = jnp.bfloat16


def dot(a, b, dims=(((1,), (0,)), ((), ()))):
    return lax.dot_general(a, b, dims, preferred_element_type=f32)


def ends_of(len_ref):
    ends, total = [], jnp.int32(0)
    for j in range(len_ref.shape[1]):
        total = total + len_ref[0, j]
        ends.append(total)
    return ends


def segment_of(position, ends):
    member = jnp.zeros_like(position)
    for end in ends:
        member = member + (position >= end).astype(jnp.int32)
    return jnp.where(position < ends[-1], member, position + len(ends))


def key_range(ends, first, last, rows):
    low, high = jnp.int32(0), jnp.int32(0)
    start = jnp.int32(0)
    for end in ends:
        low = jnp.where((first >= start) & (first < end), start, low)
        high = jnp.where((last >= start) & (last < end), end, high)
        start = end
    total = ends[-1]
    low = jnp.where(first >= total, first, low)
    high = jnp.where(last >= total, last + 1, high)
    return low // KB, (high + KB - 1) // KB


def attend_forward_kernel(
    len_ref, x_ref, wq_ref, wk_ref, wv_ref, bq_ref, bv_ref,
    q_ref, k_ref, v_ref, mixed_ref, lse_ref,
    qs_ref, va_ref, acc_ref, top_ref,
):
    group = pl.program_id(0)
    rows, cols = q_ref.shape
    heads = cols // HD
    x = x_ref[...]
    query = (dot(x, wq_ref[...]) + bq_ref[...].astype(f32)).astype(bf16)
    q_ref[...] = query
    k_ref[...] = dot(x, wk_ref[...]).astype(bf16)
    value = (dot(x, wv_ref[...]) + bv_ref[...].astype(f32)).astype(bf16)
    v_ref[...] = value
    lane = lax.broadcasted_iota(jnp.int32, (rows, 128), 1)
    for h in range(heads):
        pair = slice(128 * (h // 2), 128 * (h // 2) + 128)
        own = (lane >= HD) if h % 2 else (lane < HD)
        qs_ref[h] = jnp.where(own, query[:, pair] * bf16(SCALE), bf16(0))
        va_ref[h] = jnp.where(own, value[:, pair], bf16(1))
    ends = ends_of(len_ref)

    @pl.when(group == 0)
    def _():
        lse_ref[...] = jnp.zeros_like(lse_ref)

    def q_step(qi, _):
        q_rows = pl.ds(pl.multiple_of(qi * QB, QB), QB)
        seg_q = segment_of(qi * QB + lax.broadcasted_iota(jnp.int32, (QB, 128), 0), ends)
        low, high = key_range(ends, qi * QB, qi * QB + QB - 1, rows)
        acc_ref[...] = jnp.zeros_like(acc_ref)
        top_ref[...] = jnp.full_like(top_ref, -3e38)

        def k_step(ki, _):
            k_rows = pl.ds(pl.multiple_of(ki * KB, KB), KB)
            seg_k = segment_of(ki * KB + lax.broadcasted_iota(jnp.int32, (1, KB), 1), ends)
            allowed = seg_q == seg_k
            for h in range(heads):
                pair = slice(128 * (h // 2), 128 * (h // 2) + 128)
                scores = dot(qs_ref[h, q_rows, :], k_ref[k_rows, pair], NT)
                scores = jnp.where(allowed, scores, MASKED)
                before = top_ref[h]
                top = jnp.maximum(before, jnp.max(scores, axis=1, keepdims=True))
                weights = jnp.exp(scores - top)
                acc_ref[h] = acc_ref[h] * jnp.exp(before - top) + dot(
                    weights.astype(bf16), va_ref[h, k_rows, :]
                )
                top_ref[h] = top
            return 0

        lax.fori_loop(low, high, k_step, 0)
        q_lane = lax.broadcasted_iota(jnp.int32, (QB, 128), 1)
        lse = lse_ref[q_rows, :]
        for p in range(heads // 2):
            out_a, out_b = acc_ref[2 * p], acc_ref[2 * p + 1]
            sum_a = pltpu.roll(out_a, HD, 1)
            sum_b = pltpu.roll(out_b, HD, 1)
            first = q_lane < HD
            mixed = jnp.where(first, out_a, out_b) / jnp.where(first, sum_a, sum_b)
            mixed_ref[q_rows, 128 * p : 128 * p + 128] = mixed.astype(bf16)
            head = group * heads + 2 * p
            lse = jnp.where(q_lane == head, top_ref[2 * p] + jnp.log(sum_a), lse)
            lse = jnp.where(q_lane == head + 1, top_ref[2 * p + 1] + jnp.log(out_b), lse)
        lse_ref[q_rows, :] = lse
        return 0

    lax.fori_loop(0, rows // QB, q_step, 0)


def attend_forward(lengths, tokens, full_qkv, bias_q, bias_v):
    rows, width = tokens.shape
    cols = 256
    groups = width // cols
    heads = cols // HD
    low = jax.ShapeDtypeStruct((rows, width), bf16)
    by_group = pl.BlockSpec((rows, cols), lambda g: (0, g))
    bias_spec = pl.BlockSpec((1, cols), lambda g: (0, g))
    return pl.pallas_call(
        attend_forward_kernel,
        grid=(groups,),
        in_specs=[
            pl.BlockSpec(memory_space=pltpu.SMEM),
            pl.BlockSpec((rows, width), lambda g: (0, 0)),
            pl.BlockSpec((width, cols), lambda g: (0, g)),
            pl.BlockSpec((width, cols), lambda g: (0, g + groups)),
            pl.BlockSpec((width, cols), lambda g: (0, g + 2 * groups)),
            bias_spec,
            bias_spec,
        ],
        out_specs=[by_group] * 4 + [pl.BlockSpec((rows, 128), lambda g: (0, 0))],
        out_shape=[low] * 4 + [jax.ShapeDtypeStruct((rows, 128), f32)],
        scratch_shapes=[
            pltpu.VMEM((heads, rows, 128), bf16),
            pltpu.VMEM((heads, rows, 128), bf16),
            pltpu.VMEM((heads, QB, 128), f32),
            pltpu.VMEM((heads, QB, 128), f32),
        ],
        compiler_params=pltpu.CompilerParams(vmem_limit_bytes=48 << 20),
        cost_estimate=pl.CostEstimate(flops=6 * rows * width * width, bytes_accessed=12 << 20, transcendentals=0),
        name="attend_forward",
    )(lengths, tokens, full_qkv, full_qkv, full_qkv, bias_q, bias_v)


def feed_forward_kernel(
    len_ref, x_ref, mixed_ref, cot_ref, wo_ref, wu_ref, wd_ref, vec_ref, bu_ref,
    out_ref, gp_ref, ga_ref, gm_ref, hl_ref, gb_ref, act_ref, gu_ref, gvec_ref, gbu_ref,
    slope_ref,
):
    step = pl.program_id(0)
    rows, width = x_ref.shape
    hidden_units = bu_ref.shape[1]

    @pl.when(step == 0)
    def _():
        gvec_ref[...] = jnp.zeros_like(gvec_ref)
        gbu_ref[...] = jnp.zeros_like(gbu_ref)

    total = ends_of(len_ref)[-1]
    position = step * rows + lax.broadcasted_iota(jnp.int32, (rows, 1), 0)
    valid = (position < total).astype(f32)

    def vec(i):
        return vec_ref[i : i + 1, :].astype(f32)

    def norm(values):
        centered = values - jnp.mean(values, axis=1, keepdims=True)
        scale = lax.rsqrt(jnp.mean(centered * centered, axis=1, keepdims=True) + NORM_EPS)
        return centered * scale, scale

    def norm_back(grad, gain, unit, scale):
        grad = grad * gain
        mean_grad = jnp.mean(grad, axis=1, keepdims=True)
        mean_unit = jnp.mean(grad * unit, axis=1, keepdims=True)
        return scale * (grad - mean_grad - unit * mean_unit)

    def add_vec(i, value):
        gvec_ref[i : i + 1, :] += jnp.sum(value, axis=0, keepdims=True)

    pre_one = x_ref[...].astype(f32) + dot(mixed_ref[...], wo_ref[...]) + vec(0)
    unit_one, scale_one = norm(pre_one)
    hidden = unit_one * vec(1) + vec(2)
    hidden_low = hidden.astype(bf16)
    hl_ref[...] = hidden_low
    branch = jnp.zeros((rows, width), f32)
    for f in range(hidden_units // FB):
        part = slice(f * FB, f * FB + FB)
        up = dot(hidden_low, wu_ref[:, part]) + bu_ref[:, part].astype(f32)
        bell = jnp.exp(up * up * -0.5)
        t = 1.0 / (1.0 + (0.3275911 * math.sqrt(0.5)) * jnp.abs(up))
        poly = 0.5 * 1.061405429 * t - 0.5 * 1.453152027
        poly = poly * t + 0.5 * 1.421413741
        poly = poly * t - 0.5 * 0.284496736
        poly = poly * t + 0.5 * 0.254829592
        tail = poly * t * bell
        share = jnp.where(up >= 0, 1.0 - tail, tail)
        active = (up * share).astype(bf16)
        act_ref[:, part] = active
        slope_ref[:, part] = share + up * bell * (1.0 / math.sqrt(2.0 * math.pi))
        branch = branch + dot(active, wd_ref[part, :])
    unit_two, scale_two = norm(hidden + branch + vec(3))
    out_ref[...] = (valid * (unit_two * vec(4) + vec(5))).astype(bf16)
    grad_out = valid * cot_ref[...].astype(f32)
    add_vec(0, grad_out * unit_two)
    add_vec(1, grad_out)
    grad_two = norm_back(grad_out, vec(4), unit_two, scale_two)
    grad_branch = grad_two.astype(bf16)
    gb_ref[...] = grad_branch
    add_vec(2, grad_branch.astype(f32))
    grad_hidden = grad_two
    for f in range(hidden_units // FB):
        part = slice(f * FB, f * FB + FB)
        grad_up = (dot(grad_branch, wd_ref[part, :], NT) * slope_ref[:, part]).astype(bf16)
        gu_ref[:, part] = grad_up
        gbu_ref[:, part] += jnp.sum(grad_up.astype(f32), axis=0, keepdims=True)
        grad_hidden = grad_hidden + dot(grad_up, wu_ref[:, part], NT)
    add_vec(3, grad_hidden * unit_one)
    add_vec(4, grad_hidden)
    grad_one = norm_back(grad_hidden, vec(1), unit_one, scale_one)
    gp_ref[...] = grad_one
    grad_attn = grad_one.astype(bf16)
    ga_ref[...] = grad_attn
    add_vec(5, grad_attn.astype(f32))
    gm_ref[...] = dot(grad_attn, wo_ref[...], NT).astype(bf16)


def feed_forward(lengths, tokens, mixed, cotangent, full_out, full_up, full_down, vecs, bias_up):
    rows, width = tokens.shape
    units = full_up.shape[1]
    by_rows = pl.BlockSpec((TB, width), lambda i: (i, 0))
    by_units = pl.BlockSpec((TB, units), lambda i: (i, 0))

    def whole(shape):
        return pl.BlockSpec(shape, lambda i: (0,) * len(shape), pipeline_mode=pl.Buffered(1))

    def kept(shape):
        return pl.BlockSpec(shape, lambda i: (0,) * len(shape))

    low = jax.ShapeDtypeStruct((rows, width), bf16)
    wide = jax.ShapeDtypeStruct((rows, units), bf16)
    return pl.pallas_call(
        feed_forward_kernel,
        grid=(rows // TB,),
        in_specs=[
            pl.BlockSpec(memory_space=pltpu.SMEM),
            by_rows, by_rows, by_rows,
            whole(full_out.shape), whole(full_up.shape), whole(full_down.shape),
            whole(vecs.shape), whole(bias_up.shape),
        ],
        out_specs=[by_rows] * 6 + [by_units] * 2 + [kept((8, width)), kept((1, units))],
        out_shape=[low, jax.ShapeDtypeStruct((rows, width), f32), low, low, low, low, wide, wide,
                   jax.ShapeDtypeStruct((8, width), f32), jax.ShapeDtypeStruct((1, units), f32)],
        scratch_shapes=[pltpu.VMEM((TB, units), f32)],
        compiler_params=pltpu.CompilerParams(vmem_limit_bytes=56 << 20),
        cost_estimate=pl.CostEstimate(flops=8 * rows * width * units + 4 * rows * width * width, bytes_accessed=40 << 20, transcendentals=0),
        name="feed_forward",
    )(lengths, tokens, mixed, cotangent, full_out, full_up, full_down, vecs, bias_up)


def weight_grad_kernel(place_ref, left_ref, right_ref, out_ref, left_t_ref, total_ref):
    @pl.when(pl.program_id(0) == 0)
    def _():
        left_t_ref[...] = left_ref[...].T

    total_ref[...] = dot(left_t_ref[...], right_ref[...])
    size = out_ref.shape[2]
    for b in range(out_ref.shape[0]):
        out_ref[place_ref[b], 0] = total_ref[b * size : b * size + size, :].astype(bf16)


def weight_grad_wide(place, left, right):
    rows, width = left.shape
    groups = right.shape[1] // width
    size = width // BLOCKS
    return pl.pallas_call(
        weight_grad_kernel,
        grid=(groups,),
        in_specs=[
            pl.BlockSpec(memory_space=pltpu.SMEM),
            pl.BlockSpec((rows, width), lambda g: (0, 0)),
            pl.BlockSpec((rows, width), lambda g: (0, g)),
        ],
        out_specs=pl.BlockSpec((BLOCKS, 1, size, width), lambda g: (0, g, 0, 0)),
        out_shape=jax.ShapeDtypeStruct((BLOCKS, groups, size, width), bf16),
        scratch_shapes=[pltpu.VMEM((width, rows), bf16), pltpu.VMEM((width, width), f32)],
        compiler_params=pltpu.CompilerParams(vmem_limit_bytes=40 << 20),
        cost_estimate=pl.CostEstimate(flops=2 * rows * width * right.shape[1], bytes_accessed=12 << 20, transcendentals=0),
        name="weight_grad_wide",
    )(place, left, right)


def weight_grad_tall_kernel(place_ref, left_ref, right_ref, out_ref, total_ref):
    total_ref[...] = dot(left_ref[...], right_ref[...], TN)
    size = out_ref.shape[1]
    base = pl.program_id(0) * (total_ref.shape[0] // size)
    for b in range(total_ref.shape[0] // size):
        out_ref[place_ref[base + b]] = total_ref[b * size : b * size + size, :].astype(bf16)


def weight_grad_tall(place, left, right):
    rows, units = left.shape
    width = right.shape[1]
    size = units // BLOCKS
    return pl.pallas_call(
        weight_grad_tall_kernel,
        grid=(units // width,),
        in_specs=[
            pl.BlockSpec(memory_space=pltpu.SMEM),
            pl.BlockSpec((rows, width), lambda g: (0, g)),
            pl.BlockSpec((rows, width), lambda g: (0, 0)),
        ],
        out_specs=pl.BlockSpec((BLOCKS, size, width), lambda g: (0, 0, 0)),
        out_shape=jax.ShapeDtypeStruct((BLOCKS, size, width), bf16),
        scratch_shapes=[pltpu.VMEM((width, width), f32)],
        compiler_params=pltpu.CompilerParams(vmem_limit_bytes=40 << 20),
        cost_estimate=pl.CostEstimate(flops=2 * rows * width * units, bytes_accessed=12 << 20, transcendentals=0),
        name="weight_grad_tall",
    )(place, left, right)


def attend_backward_kernel(
    len_ref, place_ref, x_ref, q_ref, k_ref, v_ref, do_ref, o_ref, lse_ref,
    dq_ref, dk_ref, dv_ref, gw_ref, gbias_ref,
    xt_ref, qs_ref, dos_ref, kt_ref, lse_t_ref, delta_ref, dqt_ref, dk_acc, dv_acc, total_ref,
):
    group = pl.program_id(0)
    rows, cols = q_ref.shape
    heads = cols // HD

    @pl.when(group == 0)
    def _():
        xt_ref[...] = x_ref[...].T
        lse_t_ref[...] = lse_ref[...].T

    query, keys, values, grad = q_ref[...], k_ref[...], v_ref[...], do_ref[...]
    lane = lax.broadcasted_iota(jnp.int32, (rows, 128), 1)
    for h in range(heads):
        pair = slice(128 * (h // 2), 128 * (h // 2) + 128)
        own = (lane >= HD) if h % 2 else (lane < HD)
        qs_ref[h] = jnp.where(own, query[:, pair] * bf16(SCALE), bf16(0))
        dos_ref[h] = jnp.where(own, grad[:, pair], bf16(0))
    kt_ref[...] = keys.T
    product = grad.astype(f32) * o_ref[...].astype(f32)
    high_part = product.astype(bf16)
    low_part = (product - high_part.astype(f32)).astype(bf16)
    pick = (
        lax.broadcasted_iota(jnp.int32, (8, cols), 1) // HD
        == lax.broadcasted_iota(jnp.int32, (8, cols), 0)
    ).astype(bf16)
    delta_ref[...] = dot(pick, high_part, NT) + dot(pick, low_part, NT)
    dk_acc[...] = jnp.zeros_like(dk_acc)
    dv_acc[...] = jnp.zeros_like(dv_acc)
    ends = ends_of(len_ref)

    def q_step(qi, _):
        q_start = pl.multiple_of(qi * QB, QB)
        q_rows = pl.ds(q_start, QB)
        seg_q = segment_of(qi * QB + lax.broadcasted_iota(jnp.int32, (1, QB), 1), ends)
        low, high = key_range(ends, qi * QB, qi * QB + QB - 1, rows)
        dqt_ref[...] = jnp.zeros_like(dqt_ref)

        def k_step(ki, _):
            k_rows = pl.ds(pl.multiple_of(ki * KB, KB), KB)
            seg_k = segment_of(ki * KB + lax.broadcasted_iota(jnp.int32, (KB, 128), 0), ends)
            allowed = jnp.concatenate([seg_k] * (QB // 128), axis=1) == seg_q
            for p in range(heads // 2):
                pair = slice(128 * p, 128 * p + 128)
                probs_pair, grads_pair = [], []
                for h in (2 * p, 2 * p + 1):
                    scores = dot(k_ref[k_rows, pair], qs_ref[h, q_rows, :], NT)
                    log_total = lse_t_ref[pl.ds(group * heads + h, 1), q_rows]
                    probs = jnp.exp(jnp.where(allowed, scores, MASKED) - log_total)
                    grad_probs = dot(v_ref[k_rows, pair], dos_ref[h, q_rows, :], NT)
                    grad_scores = (probs * (grad_probs - delta_ref[h : h + 1, q_rows])).astype(bf16)
                    probs_pair.append(probs.astype(bf16))
                    grads_pair.append(grad_scores)
                    dqt_ref[h * HD : h * HD + HD, :] += dot(
                        kt_ref[h * HD : h * HD + HD, k_rows], grad_scores
                    )
                dv_acc[k_rows, pair] += dot(probs_pair[0], dos_ref[2 * p, q_rows, :]) + dot(
                    probs_pair[1], dos_ref[2 * p + 1, q_rows, :]
                )
                dk_acc[k_rows, pair] += dot(grads_pair[0], qs_ref[2 * p, q_rows, :]) + dot(
                    grads_pair[1], qs_ref[2 * p + 1, q_rows, :]
                )
            return 0

        lax.fori_loop(low, high, k_step, 0)
        dq_ref[q_rows, :] = (dqt_ref[...] * SCALE).T.astype(bf16)
        return 0

    lax.fori_loop(0, rows // QB, q_step, 0)
    dk_ref[...] = dk_acc[...].astype(bf16)
    dv_ref[...] = dv_acc[...].astype(bf16)
    size = gw_ref.shape[2]
    for s, part in enumerate((dq_ref, dk_ref, dv_ref)):
        total_ref[...] = dot(xt_ref[...], part[...])
        for b in range(BLOCKS):
            gw_ref[place_ref[b], s] = total_ref[b * size : b * size + size, :].astype(bf16)
    gbias_ref[0:1, :] = jnp.sum(dq_ref[...].astype(f32), axis=0, keepdims=True)
    gbias_ref[1:2, :] = jnp.sum(dv_ref[...].astype(f32), axis=0, keepdims=True)


def attend_backward(lengths, place, tokens, query, keys, values, grad_mixed, mixed, lse):
    rows, width = tokens.shape
    cols = 256
    groups = width // cols
    heads = cols // HD
    size = width // BLOCKS
    by_group = pl.BlockSpec((rows, cols), lambda g: (0, g))
    low = jax.ShapeDtypeStruct((rows, width), bf16)
    return pl.pallas_call(
        attend_backward_kernel,
        grid=(groups,),
        in_specs=[
            pl.BlockSpec(memory_space=pltpu.SMEM),
            pl.BlockSpec(memory_space=pltpu.SMEM),
            pl.BlockSpec((rows, width), lambda g: (0, 0)),
        ]
        + [by_group] * 5
        + [pl.BlockSpec((rows, 128), lambda g: (0, 0))],
        out_specs=[by_group] * 3
        + [
            pl.BlockSpec((BLOCKS, 3, size, cols), lambda g: (0, 0, 0, g)),
            pl.BlockSpec((8, cols), lambda g: (0, g)),
        ],
        out_shape=[low] * 3
        + [
            jax.ShapeDtypeStruct((BLOCKS, 3, size, width), bf16),
            jax.ShapeDtypeStruct((8, width), f32),
        ],
        scratch_shapes=[
            pltpu.VMEM((width, rows), bf16),
            pltpu.VMEM((heads, rows, 128), bf16),
            pltpu.VMEM((heads, rows, 128), bf16),
            pltpu.VMEM((cols, rows), bf16),
            pltpu.VMEM((128, rows), f32),
            pltpu.VMEM((8, rows), f32),
            pltpu.VMEM((cols, QB), f32),
            pltpu.VMEM((rows, cols), f32),
            pltpu.VMEM((rows, cols), f32),
            pltpu.VMEM((width, cols), f32),
        ],
        compiler_params=pltpu.CompilerParams(vmem_limit_bytes=48 << 20),
        cost_estimate=pl.CostEstimate(flops=20 * rows * width * width, bytes_accessed=16 << 20, transcendentals=0),
        name="attend_backward",
    )(lengths, place, tokens, query, keys, values, grad_mixed, mixed, lse)


def token_grad_kernel(gp_ref, dq_ref, dk_ref, dv_ref, w_ref, out_ref):
    width = gp_ref.shape[1]
    out_ref[...] = (
        gp_ref[...]
        + dot(dq_ref[...], w_ref[:, :width], NT)
        + dot(dk_ref[...], w_ref[:, width : 2 * width], NT)
        + dot(dv_ref[...], w_ref[:, 2 * width :], NT)
    )


def token_grad(grad_one, dq, dk, dv, full_qkv):
    rows, width = grad_one.shape
    by_rows = pl.BlockSpec((TB, width), lambda i: (i, 0))
    return pl.pallas_call(
        token_grad_kernel,
        grid=(rows // TB,),
        in_specs=[by_rows] * 4
        + [pl.BlockSpec(full_qkv.shape, lambda i: (0, 0), pipeline_mode=pl.Buffered(1))],
        out_specs=by_rows,
        out_shape=jax.ShapeDtypeStruct((rows, width), f32),
        compiler_params=pltpu.CompilerParams(vmem_limit_bytes=40 << 20),
        cost_estimate=pl.CostEstimate(flops=6 * rows * width * width, bytes_accessed=14 << 20, transcendentals=0),
        name="token_grad",
    )(grad_one, dq, dk, dv, full_qkv)


CORE, X, Y, Z_LOW, Z_HIGH = 1, 2, 4, 8, 16


def relative_places():
    places = np.zeros((32, 32), np.int32)
    for i in range(32):
        for b in range(32):
            bits = i ^ b
            x, y = int(bits & X > 0), int(bits & Y > 0)
            first, second = (y, x) if b & CORE else (x, y)
            low, high = int(bits & Z_LOW > 0), int(bits & Z_HIGH > 0)
            places[i, b] = 16 * (bits & CORE) + 8 * first + 4 * second + 2 * low + high
    return places


def exchange(values, even, odd):
    return lax.ppermute(
        values, "dp", [(i, i ^ (odd if i & CORE else even)) for i in range(32)]
    )


def added(a, b):
    return (a.astype(f32) + b.astype(f32)).astype(bf16)


def reduce_blocks(parts):
    halves = [part.reshape(2, 16, *part.shape[1:]) for part in parts]
    received = [exchange(half[1], CORE, CORE) for half in halves]

    def joined(rows):
        return jnp.concatenate(
            [added(half[0, rows], got[rows]) for half, got in zip(halves, received)], axis=1
        )

    send, keep = joined(slice(8, 16)), joined(slice(0, 8))
    for even, odd in ((X, Y), (Y, X), (Z_LOW, Z_LOW)):
        got = exchange(send, even, odd)
        half = keep.shape[0] // 2
        send, keep = added(keep[half:], got[half:]), added(keep[:half], got[:half])
    got = exchange(send, Z_HIGH, Z_HIGH)
    return keep[0].astype(f32) + got[0].astype(f32)


def body(
    tokens, cotangent, lengths, w_qkv, w_out, w_up, w_down, bias_q, bias_v, bias_out,
    gain_one, shift_one, bias_up, bias_down, gain_two, shift_two,
):
    count = lax.axis_size("dp")
    index = lax.axis_index("dp")
    width = tokens.shape[1]
    units = w_up.shape[1]
    shard = w_qkv.shape[0]
    ratio = units // width
    small = jnp.stack(
        [bias_q, bias_v, bias_out, gain_one, shift_one, bias_down, gain_two, shift_two], axis=1
    )
    small = jnp.concatenate([small, bias_up.reshape(shard, ratio)], axis=1)
    small = jnp.pad(small, ((0, 0), (0, 128 - small.shape[1])))
    attn = lax.all_gather(jnp.concatenate([w_qkv, small], axis=1), "dp", axis=0, tiled=True)
    rest = lax.all_gather(
        jnp.concatenate([w_out, w_up, w_down.reshape(shard, ratio * width)], axis=1),
        "dp", axis=0, tiled=True,
    )
    full_qkv = attn[:, : 3 * width]
    vectors = attn[:, 3 * width :]
    rows8 = vectors[:, :8].T
    full_bias_up = vectors[:, 8 : 8 + ratio].reshape(1, units)
    full_out = rest[:, :width]
    full_up = rest[:, width : width + units]
    full_down = rest[:, width + units :].reshape(units, width)
    vecs = jnp.concatenate([rows8[2:], rows8[:2]], axis=0)

    query, keys, values, mixed, lse = attend_forward(
        lengths, tokens, full_qkv, rows8[0:1], rows8[1:2]
    )
    output, grad_one, grad_attn, grad_mixed, hidden_low, grad_branch, active, grad_up, gvec, gbu = (
        feed_forward(lengths, tokens, mixed, cotangent, full_out, full_up, full_down, vecs, full_bias_up)
    )
    if count == BLOCKS:
        table = relative_places()
        place = jnp.asarray(table)[index]
        blocks_at = jnp.asarray(np.argsort(table, axis=1))[index]
    else:
        place = jnp.arange(BLOCKS, dtype=jnp.int32)
    part_down = weight_grad_tall(place, active, grad_branch)
    part_up = weight_grad_wide(place, hidden_low, grad_up)
    part_out = weight_grad_wide(place, mixed, grad_attn)
    dq, dk, dv, part_qkv, gbias = attend_backward(
        lengths, place, tokens, query, keys, values, grad_mixed, mixed, lse
    )
    grad_tokens = token_grad(grad_one, dq, dk, dv, full_qkv)
    if count != BLOCKS:
        def scattered(part):
            return lax.psum_scatter(part, "dp", scatter_dimension=0, tiled=True).astype(f32)

        def lined(part):
            return part.transpose(0, 2, 1, 3).reshape(width, -1)

        lines = jnp.concatenate([gvec, gbias[:2], gbu.reshape(ratio, width)], axis=0)
        return (
            output, grad_tokens, scattered(lined(part_qkv)), scattered(lined(part_out)),
            scattered(lined(part_up)), scattered(part_down.reshape(units, width)),
            scattered(gbias[0]), scattered(gbias[1]), scattered(gvec[5]), scattered(gvec[3]),
            scattered(gvec[4]), scattered(gbu[0]), scattered(gvec[2]), scattered(gvec[0]),
            scattered(gvec[1]),
        )

    def small_part(lines):
        line = jnp.concatenate([row.reshape(BLOCKS, -1) for row in lines], axis=1)
        line = jnp.pad(line.astype(bf16), ((0, 0), (0, width - line.shape[1])))
        return jnp.pad(line[blocks_at][:, None, :], ((0, 0), (0, 7), (0, 0)))

    def rows_of(part):
        return part.reshape(BLOCKS, -1, width)

    small_mlp = small_part([*gvec[:6], gbu[0]])
    mlp = reduce_blocks([part_down, rows_of(part_up), small_mlp])
    small_attn = small_part([*gbias[:2]])
    rest = reduce_blocks([rows_of(part_qkv), rows_of(part_out), small_attn])

    def wide_of(rows):
        return rows.reshape(-1, shard, width).transpose(1, 0, 2).reshape(shard, -1)

    tall = ratio * shard
    line = mlp[2 * tall]
    line_attn = rest[4 * shard]

    def piece(line, i):
        return line[i * shard : i * shard + shard]

    return (
        output, grad_tokens, wide_of(rest[: 3 * shard]), rest[3 * shard : 4 * shard],
        wide_of(mlp[tall : 2 * tall]), mlp[:tall],
        piece(line_attn, 0), piece(line_attn, 1), piece(line, 5), piece(line, 3), piece(line, 4),
        line[6 * shard : 6 * shard + tall], piece(line, 2), piece(line, 0), piece(line, 1),
    )


def solution(mesh):
    rows, vector = P("dp", None), P("dp")
    return jax.shard_map(
        body, mesh=mesh, in_specs=(rows,) * 7 + (vector,) * 9, out_specs=(rows,) * 6 + (vector,) * 9,
        check_vma=False,
    )
```

time: 1070 us -> 476 us (0.44)
  matrix products: 345 us -> 0 us
  Pallas kernels: 0 us -> 180 us
  waiting for transfers between devices: 348 us -> 170 us
  local copies, waits for them, and re-layouts: 226 us -> 63.6 us
  blocking collectives: 83.8 us -> 0 us
  starting transfers between devices: 0.31 us -> 22.7 us
  other arithmetic: 37.6 us -> 21.2 us
    dot_general x180 -> x0, matrix products: 345 us -> none  [the longest x48 56.1 us: one_block(): jnp.einsum('qd,kd->qk', query_part, keys_one, preferred_element_type=jnp....]
    reduce_scatter x3 -> x0, waiting for transfers between devices: 284 us -> none  [the longest x1 142 us: body(): lax.psum_scatter(grad_w_up, 'dp', scatter_dimension=0, tiled=True)]
    pallas_call x0 -> x7, Pallas kernels: none -> 180 us  [the longest x1 66.6 us: attend_backward(): pl.pallas_call(attend_backward_kernel, grid=(groups,), in_specs=[pl.Block...]
    unnamed x2 -> x0, blocking collectives: 83.8 us -> none
    ppermute x0 -> x14, waiting for transfers between devices: none -> 80.9 us  [exchange(): lax.ppermute(values, 'dp', [(i, i ^ (odd if i & CORE else even)) for i in...]
    dynamic_slice x120 -> x0, local copies, waits for them, and re-layouts: 61.9 us -> none  [the longest x36 51.9 us: attend_forward(): return lax.map(one_head, (query_h, keys_h, values_h))]
    all_gather x4 -> x2, waiting for transfers between devices: 30.8 us -> 88.7 us  [the longest x1 59.3 us: body(): lax.all_gather(jnp.concatenate([w_qkv, small], axis=1), 'dp', axis=0, til...]
    dynamic_update_slice x96 -> x0, local copies, waits for them, and re-layouts: 57.9 us -> none  [the longest x72 56.9 us: attend_forward(): return lax.map(one_head, (query_h, keys_h, values_h))]
  transfers between devices with their start and end apart: 8 -> 16, of which waited for: 5 -> 10; matrix products, arithmetic and copies ran while one was open for 52% -> 8% of each run, Pallas kernels for 0% -> 28%
where the time goes in v1:
time: 476 us; the launch traced here: 472 us
  Pallas kernels  180 us (38%)
  waiting for transfers between devices  170 us (36%)
  local copies, waits for them, and re-layouts  63.6 us (13%)
  starting transfers between devices  22.7 us (5%)
  other arithmetic  21.2 us (4%)
  between operations  14.6 us (3%)
    ppermute x14, waiting for transfers between devices, exchange(): lax.ppermute(values, 'dp', [(i, i ^ (odd if i & CORE else even)) for i in...  80.9 us
    pallas_call x1, Pallas kernels, attend_backward(): pl.pallas_call(attend_backward_kernel, grid=(groups,), in_specs=[pl.Block...  66.6 us
    all_gather x1, waiting for transfers between devices, body(): lax.all_gather(jnp.concatenate([w_qkv, small], axis=1), 'dp', axis=0, til...  59.3 us
    pallas_call x1, Pallas kernels, attend_forward(): pl.pallas_call(attend_forward_kernel, grid=(groups,), in_specs=[pl.BlockS...  48.3 us
    pallas_call x1, Pallas kernels, feed_forward(): pl.pallas_call(feed_forward_kernel, grid=(rows // TB,), in_specs=[pl.Bloc...  43.4 us
    all_gather x1, waiting for transfers between devices, body(): lax.all_gather(jnp.concatenate([w_out, w_up, w_down.reshape(shard, ratio...  29.4 us
    ppermute x14, starting transfers between devices, exchange(): lax.ppermute(values, 'dp', [(i, i ^ (odd if i & CORE else even)) for i in...  22.6 us
    unnamed x51, local copies, waits for them, and re-layouts  13.7 us
  transfers between devices with their start and end apart: 16, of which 10 were waited for; matrix products, arithmetic and copies ran while one was open for 8% of the time, Pallas kernels for 28%

profile of v1, /device:TPU:0, one launch (start us, length us, event | category | flops | bytes accessed | tf_op | source)
XLA Modules:
  0.0 471.6 jit_solution(2981612254157374268)
XLA Ops:
  19.8 59.3 %all-gather.3.cloned.1.call-done = bf16[768,2432]{1,0:T(8,128)(2,1)} async-done(((bf16[24,2432]{1,0:T(8,128)(2,1)}), bf16[768,2432]{1,0:T(8,128)(2,1)}) %all-gather.3.cloned.1.call-update) | async-done | bytes 3735568 | tf_op jit(solution)/shard_map/all_gather | solution.py:551
  82.8 4.1 slice.388.wq_ref.wk_ref.wv_ref.w_ref
  87.5 48.3 %attend_forward.1 = (bf16[1024,768]{1,0:T(8,128)(2,1)S(1)}, bf16[1024,768]{1,0:T(8,128)(2,1)S(1)}, bf16[1024,768]{1,0:T(8,128)(2,1)S(1)}, bf16[1024,768]{1,0:T(8,128)(2,1)}, f32[1024,128]{1,0:T(8,128)S(1)}) custom-call(s32[1,8]{1,0:T(1,128)S(1)} %copy-done.8, bf16[1024,768]{1,0:T(8,128)(2,1)} %x_ref.5, bf16[768,2304]{1,0:T(8,128)(2,1)} %slice.388.wq_ref.wk_ref.wv_ref.w_ref, ...), custom_call_target="tpu_custom_call" | custom-call | flops 3623878656 | bytes 12582912 | tf_op jit(solution)/shard_map/attend_forward/pallas_call | solution.py:136
  139.3 29.4 %all-gather.5.cloned.1.call-done = bf16[768,6912]{1,0:T(8,128)(2,1)} async-done(((bf16[24,6912]{1,0:T(8,128)(2,1)}), bf16[768,6912]{1,0:T(8,128)(2,1)}) %all-gather.5.cloned.1.call-update) | async-done | bytes 10616848 | tf_op jit(solution)/shard_map/all_gather | solution.py:552
  168.7 8.1 %fusion.15 = (bf16[768,3072]{1,0:T(8,128)(2,1)}, bf16[768,3072]{1,0:T(8,128)(2,1)}) fusion(bf16[768,6912]{1,0:T(8,128)(2,1)} %all-gather.5.cloned.1.call-done), kind=kLoop, calls=%fused_computation.92 | loop fusion | bytes 18874368 | tf_op jit(solution)/shard_map/slice | solution.py:562
  176.9 8.5 %reshape.150.wd_ref = bf16[3072,768]{1,0:T(8,128)(2,1)} reshape(bf16[768,3072]{1,0:T(8,128)(2,1)} %get-tuple-element.63) | data formatting | bytes 9437184 | tf_op jit(solution)/shard_map/reshape | solution.py:562
  187.7 43.4 %feed_forward.1 = (bf16[1024,768]{1,0:T(8,128)(2,1)}, f32[1024,768]{1,0:T(8,128)}, bf16[1024,768]{1,0:T(8,128)(2,1)}, bf16[1024,768]{1,0:T(8,128)(2,1)}, bf16[10...) custom-call(s32[1,8]{1,0:T(1,128)} %len_ref.5, ...), custom_call_target="tpu_custom_call" | custom-call | flops 21743271936 | bytes 41943040 | tf_op jit(solution)/shard_map/feed_forward/pallas_call | solution.py:258
  231.8 2.8 copy-done.16
  236.0 6.7 %weight_grad_tall.1 = bf16[32,96,768]{2,1,0:T(8,128)(2,1)S(1)} custom-call(s32[32]{0:T(128)S(1)} %dynamic-slice_bitcast_fusion.place_ref, bf16[1024,3072]{1,0:T(8,128)(2,1)S(1)} %copy-done.16, bf16[1024,768]{1,0:T(8,128)(2,1)S(1)} %copy-done.18), custom_call_target="tpu_custom_call" | custom-call | flops 4831838208 | bytes 12582912 | tf_op jit(solution)/shard_map/weight_grad_tall/pallas_call | solution.py:321
  245.9 7.5 %weight_grad_wide.3 = bf16[32,4,24,768]{3,2,1,0:T(8,128)(2,1)S(1)} custom-call(s32[32]{0:T(128)S(1)} %dynamic-slice_bitcast_fusion.place_ref, bf16[1024,768]{1,0:T(8,128)(2,1)S(1)} %copy-done.17, bf16[1024,3072]{1,0:T(8,128)(2,1)S(1)} %copy-done.15), custom_call_target="tpu_custom_call" | custom-call | flops 4831838208 | bytes 12582912 | tf_op jit(solution)/shard_map/weight_grad_wide/pallas_call | solution.py:292
  259.4 66.6 %attend_backward.1 = (bf16[1024,768]{1,0:T(8,128)(2,1)S(1)}, bf16[1024,768]{1,0:T(8,128)(2,1)S(1)}, bf16[1024,768]{1,0:T(8,128)(2,1)S(1)}, bf16[32,3,24,768]{3,2,1,0:T(8,128)(2,1)}, f32[8,768]{1,0:T(8,128)S(1)}) custom-call(s32[1,8]{1,0:T(1,128)S(1)} %copy-done.9, s32[32]{0:T(128)S(1)} %dynamic-slice_bitcast_fusion.place_ref, bf16[1024,768]{1,0:T(8,128)(2,1)} %x_ref.5, ...), custom_call_target="tpu_custom_call" | custom-call | flops 12079595520 | bytes 16777216 | tf_op jit(solution)/shard_map/attend_backward/pallas_call | solution.py:429
  326.0 3.9 slice.307
  329.9 6.5 %collective-permute-start = (bf16[16,72,768]{2,1,0:T(8,128)(2,1)}, bf16[16,72,768]{2,1,0:T(8,128)(2,1)}, u32[]{:S(2)}, u32[]{:S(2)}) collective-permute-start(bf16[16,72,768]{2,1,0:T(8,128)(2,1)} %bitcast.12), channel_id=1, source_target_pairs={{0,1},{1,0},{2,3},{3,2},{4,5},{5,4},{6,7},{7,6},{8,9},{9,8},{10,11... | collective-permute-start | bytes 5308424 | tf_op jit(solution)/shard_map/ppermute | solution.py:509
  342.6 4.1 fusion.3
  346.7 3.3 fusion.2
  359.3 22.6 %collective-permute-done.10 = bf16[8,200,768]{2,1,0:T(8,128)(2,1)} collective-permute-done((bf16[8,200,768]{2,1,0:T(8,128)(2,1)}, bf16[8,200,768]{2,1,0:T(8,128)(2,1)}, u32[]{:S(2)}, u32[]{:S(2)}) %collective-permute-start.10) | collective-permute-done | bytes 2457632 | tf_op jit(solution)/shard_map/ppermute | solution.py:509
  384.3 20.6 %collective-permute-done.3 = bf16[8,104,768]{2,1,0:T(8,128)(2,1)S(1)} collective-permute-done((bf16[8,104,768]{2,1,0:T(8,128)(2,1)S(1)}, bf16[8,104,768]{2,1,0:T(8,128)(2,1)S(1)}, u32[]{:S(2)}, u32[]{:S(2)}) %collective-permute-start.3) | collective-permute-done | bytes 1277984 | tf_op jit(solution)/shard_map/ppermute | solution.py:509
  405.3 10.4 %collective-permute-done.4 = bf16[4,104,768]{2,1,0:T(8,128)(2,1)S(1)} collective-permute-done((bf16[4,104,768]{2,1,0:T(8,128)(2,1)S(1)}, bf16[4,104,768]{2,1,0:T(8,128)(2,1)S(1)}, u32[]{:S(2)}, u32[]{:S(2)}) %collective-permute-start.4) | collective-permute-done | bytes 639008 | tf_op jit(solution)/shard_map/ppermute | solution.py:509
  415.8 9.5 %collective-permute-start.5 = (bf16[2,104,768]{2,1,0:T(8,128)(2,1)S(1)}, bf16[2,104,768]{2,1,0:T(8,128)(2,1)S(1)}, u32[]{:S(2)}, u32[]{:S(2)}) collective-permute-start(bf16[2,104,768]{2,1,0:T(8,128)(2,1)S(1)} %get-tuple-element.80), channel_id=1, source_target_pairs={{0,8},{1,9},{2,10},{3,11},{4,12},{5,13},{6,14},{7,15},{8,0},{9,1},... | collective-permute-start | bytes 958472 | tf_op jit(solution)/shard_map/ppermute | solution.py:509
  425.7 9.8 %collective-permute-done.5 = bf16[2,104,768]{2,1,0:T(8,128)(2,1)S(1)} collective-permute-done((bf16[2,104,768]{2,1,0:T(8,128)(2,1)S(1)}, bf16[2,104,768]{2,1,0:T(8,128)(2,1)S(1)}, u32[]{:S(2)}, u32[]{:S(2)}) %collective-permute-start.5) | collective-permute-done | bytes 319520 | tf_op jit(solution)/shard_map/ppermute | solution.py:509
  435.6 5.4 %token_grad.1 = f32[1024,768]{1,0:T(8,128)} custom-call(f32[1024,768]{1,0:T(8,128)S(1)} %copy-done.3, bf16[1024,768]{1,0:T(8,128)(2,1)S(1)} %get-tuple-element.43.dq_ref, bf16[1024,768]{1,0:T(8,128)(2,1)S(1)} %copy-done.5, bf16[1024,768]{1,0:T(8,128)(2,1)S(1)} %copy-done.7, bf16[768,2304]{1,0:T(8,128)(2,1)S(1)} %copy-done), custom_call_target="tpu_custom_call" | custom-call | flops 3623878656 | bytes 14680064 | tf_op jit(solution)/shard_map/token_grad/pallas_call | solution.py:480
  441.0 5.3 %collective-permute-done.6 = bf16[1,104,768]{2,1,0:T(8,128)(2,1)S(1)} collective-permute-done((bf16[1,104,768]{2,1,0:T(8,128)(2,1)S(1)}, bf16[1,104,768]{2,1,0:T(8,128)(2,1)S(1)}, u32[]{:S(2)}, u32[]{:S(2)}) %collective-permute-start.6) | collective-permute-done | bytes 159776 | tf_op jit(solution)/shard_map/ppermute | solution.py:509
  447.2 2.8 collective-permute-start.13
  452.0 9.9 %collective-permute-done.13 = bf16[1,200,768]{2,1,0:T(8,128)(2,1)S(1)} collective-permute-done((bf16[1,200,768]{2,1,0:T(8,128)(2,1)S(1)}, bf16[1,200,768]{2,1,0:T(8,128)(2,1)S(1)}, u32[]{:S(2)}, u32[]{:S(2)}) %collective-permute-start.13) | collective-permute-done | bytes 307232 | tf_op jit(solution)/shard_map/ppermute | solution.py:509
  (156 shorter events, 58.2 us)
Async XLA Ops:
  7.2 71.9 %all-gather.3.cloned.1.call-start = ((), (), s32[]{:S(2)}) async-start(), calls=%async_computation | async-start | bytes 3852288 | tf_op jit(solution)/shard_map/all_gather | solution.py:551
  15.7 153.1 %all-gather.5.cloned.1.call-start = ((), (), s32[]{:S(2)}) async-start(), calls=%async_computation.1 | async-start | bytes 10948608 | tf_op jit(solution)/shard_map/all_gather | solution.py:552
  236.0 9.9 %copy-start.15 = (bf16[1024,3072]{1,0:T(8,128)(2,1)S(1)}, bf16[1024,3072]{1,0:T(8,128)(2,1)}, u32[]{:S(2)}) copy-start(bf16[1024,3072]{1,0:T(8,128)(2,1)} %get-tuple-element.52.right_ref) | copy-start | bytes 18874372
  245.7 96.9 %collective-permute-start.7 = (bf16[16,96,768]{2,1,0:T(8,128)(2,1)}, bf16[16,96,768]{2,1,0:T(8,128)(2,1)}, u32[]{:S(2)}, u32[]{:S(2)}) collective-permute-start(bf16[16,96,768]{2,1,0:T(8,128)(2,1)} %slice.426), channel_id=1, source_target_pairs={{0,1},{1,0},{2,3},{3,2},{4,5},{5,4},{6,7},{7,6},{8,9},{9,8},{10,11... | collective-permute-start | bytes 7077896 | tf_op jit(solution)/shard_map/ppermute | solution.py:509
  253.5 5.9 %copy-start.9 = (s32[1,8]{1,0:T(1,128)S(1)}, s32[1,8]{1,0:T(1,128)}, u32[]{:S(2)}) copy-start(s32[1,8]{1,0:T(1,128)} %len_ref.5) | copy-start | bytes 100
  256.3 90.4 %collective-permute-start.8 = (bf16[16,96,768]{2,1,0:T(8,128)(2,1)}, bf16[16,96,768]{2,1,0:T(8,128)(2,1)}, u32[]{:S(2)}, u32[]{:S(2)}) collective-permute-start(bf16[16,96,768]{2,1,0:T(8,128)(2,1)} %bitcast.31), channel_id=1, source_target_pairs={{0,1},{1,0},{2,3},{3,2},{4,5},{5,4},{6,7},{7,6},{8,9},{9,8},{10,11... | collective-permute-start | bytes 7077896 | tf_op jit(solution)/shard_map/ppermute | solution.py:509
  258.2 83.3 %collective-permute-start.9 = (bf16[16,8,768]{2,1,0:T(8,128)(2,1)S(1)}, bf16[16,8,768]{2,1,0:T(8,128)(2,1)}, u32[]{:S(2)}, u32[]{:S(2)}) collective-permute-start(bf16[16,8,768]{2,1,0:T(8,128)(2,1)S(1)} %pad_slice_fusion.1), channel_id=1, source_target_pairs={{0,1},{1,0},{2,3},{3,2},{4,5},{5,4},{6,7},{7,6},{8,9},{9,8},{10,11... | collective-permute-start | bytes 589832 | tf_op jit(solution)/shard_map/ppermute | solution.py:509
  326.0 20.7 %slice-start = ((s8[4718592]{0:T(1024)(128)(4,1)}), s8[524288]{0:T(1024)(128)(4,1)S(1)}, s32[]{:S(2)}) async-start(s8[4718592]{0:T(1024)(128)(4,1)} %bitcast.128), calls=%async_computation.2 | async-start | bytes 1048576
  329.9 25.0 %collective-permute-start = (bf16[16,72,768]{2,1,0:T(8,128)(2,1)}, bf16[16,72,768]{2,1,0:T(8,128)(2,1)}, u32[]{:S(2)}, u32[]{:S(2)}) collective-permute-start(bf16[16,72,768]{2,1,0:T(8,128)(2,1)} %bitcast.12), channel_id=1, source_target_pairs={{0,1},{1,0},{2,3},{3,2},{4,5},{5,4},{6,7},{7,6},{8,9},{9,8},{10,11... | collective-permute-start | bytes 5308424 | tf_op jit(solution)/shard_map/ppermute | solution.py:509
  339.5 7.2 %slice-start.1 = ((s8[4718592]{0:T(1024)(128)(4,1)}), s8[4194304]{0:T(1024)(128)(4,1)S(1)}, s32[]{:S(2)}) async-start(s8[4718592]{0:T(1024)(128)(4,1)} %bitcast.128), calls=%async_computation.3 | async-start | bytes 8388608
  351.6 30.2 %collective-permute-start.10 = (bf16[8,200,768]{2,1,0:T(8,128)(2,1)}, bf16[8,200,768]{2,1,0:T(8,128)(2,1)}, u32[]{:S(2)}, u32[]{:S(2)}) collective-permute-start(bf16[8,200,768]{2,1,0:T(8,128)(2,1)} %pad_maximum_fusion.1), channel_id=1, source_target_pairs={{0,2},{1,5},{2,0},{3,7},{4,6},{5,1},{6,4},{7,3},{8,10},{9,13},{10,... | collective-permute-start | bytes 7372808 | tf_op jit(solution)/shard_map/ppermute | solution.py:509
  352.4 2.4 collective-permute-start.1
  352.5 2.2 collective-permute-start.2
  357.0 47.9 %collective-permute-start.3 = (bf16[8,104,768]{2,1,0:T(8,128)(2,1)S(1)}, bf16[8,104,768]{2,1,0:T(8,128)(2,1)S(1)}, u32[]{:S(2)}, u32[]{:S(2)}) collective-permute-start(bf16[8,104,768]{2,1,0:T(8,128)(2,1)S(1)} %pad_maximum_fusion.3), channel_id=1, source_target_pairs={{0,2},{1,5},{2,0},{3,7},{4,6},{5,1},{6,4},{7,3},{8,10},{9,13},{10,... | collective-permute-start | bytes 3833864 | tf_op jit(solution)/shard_map/ppermute | solution.py:509
  384.1 41.2 %collective-permute-start.11 = (bf16[4,200,768]{2,1,0:T(8,128)(2,1)S(1)}, bf16[4,200,768]{2,1,0:T(8,128)(2,1)S(1)}, u32[]{:S(2)}, u32[]{:S(2)}) collective-permute-start(bf16[4,200,768]{2,1,0:T(8,128)(2,1)S(1)} %get-tuple-element.72), channel_id=1, source_target_pairs={{0,4},{1,3},{2,6},{3,1},{4,0},{5,7},{6,2},{7,5},{8,12},{9,11},{10,... | collective-permute-start | bytes 3686408 | tf_op jit(solution)/shard_map/ppermute | solution.py:509
  404.9 30.7 %copy-start.3 = (f32[1024,768]{1,0:T(8,128)S(1)}, f32[1024,768]{1,0:T(8,128)}, u32[]{:S(2)}) copy-start(f32[1024,768]{1,0:T(8,128)} %get-tuple-element.37.gp_ref) | copy-start | bytes 9437188
  404.9 30.7 %copy-start.7 = (bf16[1024,768]{1,0:T(8,128)(2,1)S(1)}, bf16[1024,768]{1,0:T(8,128)(2,1)}, u32[]{:S(2)}) copy-start(bf16[1024,768]{1,0:T(8,128)(2,1)} %copy-done.6) | copy-start | bytes 4718596
  405.2 10.5 %collective-permute-start.4 = (bf16[4,104,768]{2,1,0:T(8,128)(2,1)S(1)}, bf16[4,104,768]{2,1,0:T(8,128)(2,1)S(1)}, u32[]{:S(2)}, u32[]{:S(2)}) collective-permute-start(bf16[4,104,768]{2,1,0:T(8,128)(2,1)S(1)} %get-tuple-element.74), channel_id=1, source_target_pairs={{0,4},{1,3},{2,6},{3,1},{4,0},{5,7},{6,2},{7,5},{8,12},{9,11},{10,... | collective-permute-start | bytes 1916936 | tf_op jit(solution)/shard_map/ppermute | solution.py:509
  415.7 19.9 %copy-start.5 = (bf16[1024,768]{1,0:T(8,128)(2,1)S(1)}, bf16[1024,768]{1,0:T(8,128)(2,1)}, u32[]{:S(2)}) copy-start(bf16[1024,768]{1,0:T(8,128)(2,1)} %copy-done.4) | copy-start | bytes 4718596
  415.8 19.7 %collective-permute-start.5 = (bf16[2,104,768]{2,1,0:T(8,128)(2,1)S(1)}, bf16[2,104,768]{2,1,0:T(8,128)(2,1)S(1)}, u32[]{:S(2)}, u32[]{:S(2)}) collective-permute-start(bf16[2,104,768]{2,1,0:T(8,128)(2,1)S(1)} %get-tuple-element.80), channel_id=1, source_target_pairs={{0,8},{1,9},{2,10},{3,11},{4,12},{5,13},{6,14},{7,15},{8,0},{9,1},... | collective-permute-start | bytes 958472 | tf_op jit(solution)/shard_map/ppermute | solution.py:509
  425.3 10.3 %copy-start = (bf16[768,2304]{1,0:T(8,128)(2,1)S(1)}, bf16[768,2304]{1,0:T(8,128)(2,1)}, u32[]{:S(2)}) copy-start(bf16[768,2304]{1,0:T(8,128)(2,1)} %slice.388.wq_ref.wk_ref.wv_ref.w_ref) | copy-start | bytes 10616836
  425.6 21.5 %collective-permute-start.12 = (bf16[2,200,768]{2,1,0:T(8,128)(2,1)S(1)}, bf16[2,200,768]{2,1,0:T(8,128)(2,1)S(1)}, u32[]{:S(2)}, u32[]{:S(2)}) collective-permute-start(bf16[2,200,768]{2,1,0:T(8,128)(2,1)S(1)} %get-tuple-element.76), channel_id=1, source_target_pairs={{0,8},{1,9},{2,10},{3,11},{4,12},{5,13},{6,14},{7,15},{8,0},{9,1},... | collective-permute-start | bytes 1843208 | tf_op jit(solution)/shard_map/ppermute | solution.py:509
  435.5 10.8 %collective-permute-start.6 = (bf16[1,104,768]{2,1,0:T(8,128)(2,1)S(1)}, bf16[1,104,768]{2,1,0:T(8,128)(2,1)S(1)}, u32[]{:S(2)}, u32[]{:S(2)}) collective-permute-start(bf16[1,104,768]{2,1,0:T(8,128)(2,1)S(1)} %add_convert_fusion.10), channel_id=1, source_target_pairs={{0,16},{1,17},{2,18},{3,19},{4,20},{5,21},{6,22},{7,23},{8,24},{9,... | collective-permute-start | bytes 479240 | tf_op jit(solution)/shard_map/ppermute | solution.py:509
  447.2 14.8 %collective-permute-start.13 = (bf16[1,200,768]{2,1,0:T(8,128)(2,1)S(1)}, bf16[1,200,768]{2,1,0:T(8,128)(2,1)S(1)}, u32[]{:S(2)}, u32[]{:S(2)}) collective-permute-start(bf16[1,200,768]{2,1,0:T(8,128)(2,1)S(1)} %add_convert_fusion.8), channel_id=1, source_target_pairs={{0,16},{1,17},{2,18},{3,19},{4,20},{5,21},{6,22},{7,23},{8,24},{9,... | collective-permute-start | bytes 921608 | tf_op jit(solution)/shard_map/ppermute | solution.py:509
  (17 other events, 43.0 us)
Sparse Core Ops, SparseCore 0:
  15.8 63.2 all-gather.2
  82.6 86.0 all-gather.4

commit v2 on v1

v2 whole, which is shorter than its diff:
```python
import functools
import math

import jax
import jax.numpy as jnp
import numpy as np
from jax import lax
from jax.experimental import pallas as pl
from jax.experimental.pallas import tpu as pltpu
from jax.sharding import PartitionSpec as P

HD = 64
FORWARD_TILE = 512
BACKWARD_TILE = 256
FAR = 2.0**30
BITS = 11
COLS = 256
TB = 256
FB = 768
BLOCKS = 32
NORM_EPS = 1e-06
SCALE = 1.0 / math.sqrt(HD)
NT = (((1,), (1,)), ((), ()))
TN = (((0,), (0,)), ((), ()))
f32 = jnp.float32
bf16 = jnp.bfloat16


def dot(a, b, dims=(((1,), (0,)), ((), ()))):
    return lax.dot_general(a, b, dims, preferred_element_type=f32)


def ends_of(len_ref):
    ends, total = [], jnp.int32(0)
    for j in range(len_ref.shape[1]):
        total = total + len_ref[0, j]
        ends.append(total)
    return ends


def segment_of(position, ends):
    member = jnp.zeros_like(position)
    for end in ends:
        member = member + (position >= end).astype(jnp.int32)
    return jnp.where(position < ends[-1], member, position + len(ends))


def key_range(ends, first, last, tile):
    low, high = jnp.int32(0), jnp.int32(0)
    start = jnp.int32(0)
    for end in ends:
        low = jnp.where((first >= start) & (first < end), start, low)
        high = jnp.where((last >= start) & (last < end), end, high)
        start = end
    total = ends[-1]
    low = jnp.where(first >= total, first, low)
    high = jnp.where(last >= total, last + 1, high)
    return low // tile, (high + tile - 1) // tile


def other_half(own, other, h):
    return jnp.concatenate([other, own] if h % 2 else [own, other], axis=0)


def segment_codes(rows, ends):
    spot = lax.broadcasted_iota(jnp.int32, (HD, rows), 0)
    seg = segment_of(lax.broadcasted_iota(jnp.int32, (1, rows), 1), ends)
    bit = (seg >> (spot // 2)) & 1
    code_q = jnp.where(spot < 2 * BITS, jnp.where(spot % 2 == 0, bit, 1 - bit), 0)
    spot = lax.broadcasted_iota(jnp.int32, (rows, 128), 1) % HD
    seg = segment_of(lax.broadcasted_iota(jnp.int32, (rows, 128), 0), ends)
    bit = (seg >> (spot // 2)) & 1
    code_k = jnp.where(spot < 2 * BITS, jnp.where(spot % 2 == 0, 1 - bit, bit), 0)
    return code_q.astype(f32).astype(bf16), code_k.astype(f32) * -FAR


def pieces(value):
    high = value.astype(bf16)
    rest = value - high.astype(f32)
    middle = rest.astype(bf16)
    return [high, middle, (rest - middle.astype(f32)).astype(bf16)]


def attend_forward_kernel(
    group, len_ref, x_ref, wq_ref, wk_ref, wv_ref, vec_ref,
    q_ref, k_ref, v_ref, mixed_ref, lse_ref,
    qt_ref, ka_ref, vt_ref, code_q_ref, code_k_ref, acc_ref, top_ref, bias_ref,
):
    ends = ends_of(len_ref)

    code_q_ref[...], code_k = segment_codes(q_ref.shape[0], ends)
    code_k_ref[...] = code_k.astype(bf16)
    bias_ref[...] = vec_ref[...].astype(f32).T[:8]

    rows, cols = q_ref.shape
    heads = cols // HD
    own_cols = slice(group * cols, group * cols + cols)
    x = x_ref[...]
    query = (dot(x, wq_ref[...]) + bias_ref[0:1, own_cols]).astype(bf16)
    q_ref[...] = query
    keys = dot(x, wk_ref[...]).astype(bf16)
    k_ref[...] = keys
    value = (dot(x, wv_ref[...]) + bias_ref[1:2, own_cols]).astype(bf16)
    v_ref[...] = value
    turned, turned_value = (query * bf16(SCALE)).T, value.T
    lane = lax.broadcasted_iota(jnp.int32, (rows, 128), 1)
    for h in range(heads):
        part = slice(h * HD, h * HD + HD)
        own = (lane >= HD) if h % 2 else (lane < HD)
        qt_ref[h] = other_half(turned[part], code_q_ref[...], h)
        ka_ref[h] = jnp.where(own, keys[:, 128 * (h // 2) : 128 * (h // 2) + 128], code_k_ref[...])
        vt_ref[h, :HD] = turned_value[part]
        vt_ref[h, HD:] = jnp.ones((16, rows), bf16)

    def q_step(qi, _):
        q_cols = pl.ds(pl.multiple_of(qi * FORWARD_TILE, FORWARD_TILE), FORWARD_TILE)
        low, high = key_range(ends, qi * FORWARD_TILE, qi * FORWARD_TILE + FORWARD_TILE - 1, FORWARD_TILE)
        acc_ref[...] = jnp.zeros_like(acc_ref)
        top_ref[...] = jnp.full_like(top_ref, -3e38)

        def k_step(ki, _):
            k_rows = pl.ds(pl.multiple_of(ki * FORWARD_TILE, FORWARD_TILE), FORWARD_TILE)
            tops = top_ref[...]
            new_tops = []

            def scores_of(h):
                return dot(ka_ref[h, k_rows, :], qt_ref[h, :, q_cols])

            ahead = [scores_of(h) for h in range(1)]
            pending = []

            def finish(h, low_weights, fade):
                acc_ref[h] = acc_ref[h] * fade + dot(vt_ref[h, :, k_rows], low_weights)

            for h in range(heads):
                if h + 1 < heads:
                    ahead.append(scores_of(h + 1))
                scores = ahead[h]
                ahead[h] = None
                before = tops[h : h + 1]
                top = jnp.maximum(before, jnp.max(scores, axis=0, keepdims=True))
                new_tops.append(top)
                pending.append((h, jnp.exp(scores - top).astype(bf16), jnp.exp(before - top)))
                if len(pending) > 0:
                    finish(*pending.pop(0))
            for item in pending:
                finish(*item)
            spare = [jnp.zeros((8 - heads, FORWARD_TILE), f32)]
            top_ref[...] = jnp.concatenate(new_tops + spare, axis=0)
            return 0

        lax.fori_loop(low, high, k_step, 0)
        totals = jnp.concatenate([acc_ref[h, HD : HD + 1] for h in range(heads)], axis=0)
        for p in range(heads // 2):
            halves = [acc_ref[h, :HD] / totals[h : h + 1] for h in (2 * p, 2 * p + 1)]
            mixed = jnp.concatenate(halves, axis=0)
            mixed_ref[q_cols, 128 * p : 128 * p + 128] = mixed.T.astype(bf16)
        lse = top_ref[0:heads] + jnp.log(totals)
        lse_ref[0, :, q_cols] = jnp.concatenate([lse, jnp.zeros((8 - heads, FORWARD_TILE), f32)], axis=0)
        return 0

    lax.fori_loop(0, rows // FORWARD_TILE, q_step, 0)


def attend_forward(group, lengths, tokens, full_qkv):
    rows, width = tokens.shape
    cols = COLS
    groups = width // cols
    heads = cols // HD
    low = jax.ShapeDtypeStruct((rows, cols), bf16)
    own = pl.BlockSpec((rows, cols), lambda g: (0, 0))
    return pl.pallas_call(
        functools.partial(attend_forward_kernel, group),
        grid=(1,),
        in_specs=[
            pl.BlockSpec(memory_space=pltpu.SMEM),
            pl.BlockSpec((rows, width), lambda g: (0, 0)),
            pl.BlockSpec((width, cols), lambda g: (0, group)),
            pl.BlockSpec((width, cols), lambda g: (0, group + groups)),
            pl.BlockSpec((width, cols), lambda g: (0, group + 2 * groups)),
            pl.BlockSpec((width, 128), lambda g: (0, 3 * width // 128)),
        ],
        out_specs=[own] * 4 + [pl.BlockSpec((1, 8, rows), lambda g: (0, 0, 0))],
        out_shape=[low] * 4 + [jax.ShapeDtypeStruct((1, 8, rows), f32)],
        scratch_shapes=[
            pltpu.VMEM((heads, 128, rows), bf16),
            pltpu.VMEM((heads, rows, 128), bf16),
            pltpu.VMEM((heads, HD + 16, rows), bf16),
            pltpu.VMEM((HD, rows), bf16),
            pltpu.VMEM((rows, 128), bf16),
            pltpu.VMEM((heads, HD + 16, FORWARD_TILE), f32),
            pltpu.VMEM((8, FORWARD_TILE), f32),
            pltpu.VMEM((8, width), f32),
        ],
        compiler_params=pltpu.CompilerParams(vmem_limit_bytes=44 << 20),
        cost_estimate=pl.CostEstimate(flops=12 * rows * width * width, bytes_accessed=12 << 20, transcendentals=0),
        name="attend_forward",
    )(lengths, tokens, full_qkv, full_qkv, full_qkv, full_qkv)


def feed_forward_kernel(
    len_ref, x_ref, mixed_a_ref, mixed_b_ref, mixed_c_ref, cot_ref, wo_ref, wu_ref, wd_ref, vec_ref, bu_ref,
    out_ref, gp_ref, ga_ref, gm_ref, hl_ref, gb_ref, mixed_ref, act_ref, gu_ref, gvec_ref, gbu_ref,
    slope_ref, rows_ref,
):
    step = pl.program_id(0)
    rows, width = x_ref.shape
    hidden_units = bu_ref.shape[1]

    @pl.when(step == 0)
    def _():
        gvec_ref[...] = jnp.zeros_like(gvec_ref)
        gbu_ref[...] = jnp.zeros_like(gbu_ref)
        rows_ref[...] = vec_ref[...].astype(f32).T[:8]

    total = ends_of(len_ref)[-1]
    position = step * rows + lax.broadcasted_iota(jnp.int32, (rows, 1), 0)
    valid = (position < total).astype(f32)

    def vec(i):
        return rows_ref[i + 2 : i + 3, :]

    def norm(values):
        centered = values - jnp.mean(values, axis=1, keepdims=True)
        scale = lax.rsqrt(jnp.mean(centered * centered, axis=1, keepdims=True) + NORM_EPS)
        return centered * scale, scale

    def norm_back(grad, gain, unit, scale):
        grad = grad * gain
        mean_grad = jnp.mean(grad, axis=1, keepdims=True)
        mean_unit = jnp.mean(grad * unit, axis=1, keepdims=True)
        return scale * (grad - mean_grad - unit * mean_unit)

    def add_vec(i, value):
        gvec_ref[i : i + 1, :] += jnp.sum(value, axis=0, keepdims=True)

    mixed_ref[...] = jnp.concatenate(
        [mixed_a_ref[...], mixed_b_ref[...], mixed_c_ref[...]], axis=1
    )
    pre_one = x_ref[...].astype(f32) + dot(mixed_ref[...], wo_ref[...]) + vec(0)
    unit_one, scale_one = norm(pre_one)
    hidden = unit_one * vec(1) + vec(2)
    hidden_low = hidden.astype(bf16)
    hl_ref[...] = hidden_low
    branch = jnp.zeros((rows, width), f32)
    for f in range(hidden_units // FB):
        part = slice(f * FB, f * FB + FB)
        up = dot(hidden_low, wu_ref[:, part]) + bu_ref[:, part].astype(f32)
        bell = jnp.exp(up * up * -0.5)
        t = 1.0 / (1.0 + (0.3275911 * math.sqrt(0.5)) * jnp.abs(up))
        poly = 0.5 * 1.061405429 * t - 0.5 * 1.453152027
        poly = poly * t + 0.5 * 1.421413741
        poly = poly * t - 0.5 * 0.284496736
        poly = poly * t + 0.5 * 0.254829592
        tail = poly * t * bell
        share = jnp.where(up >= 0, 1.0 - tail, tail)
        active = (up * share).astype(bf16)
        act_ref[:, part] = active
        slope_ref[:, part] = share + up * bell * (1.0 / math.sqrt(2.0 * math.pi))
        branch = branch + dot(active, wd_ref[part, :])
    unit_two, scale_two = norm(hidden + branch + vec(3))
    out_ref[...] = (valid * (unit_two * vec(4) + vec(5))).astype(bf16)
    grad_out = valid * cot_ref[...].astype(f32)
    add_vec(0, grad_out * unit_two)
    add_vec(1, grad_out)
    grad_two = norm_back(grad_out, vec(4), unit_two, scale_two)
    grad_branch = grad_two.astype(bf16)
    gb_ref[...] = grad_branch
    add_vec(2, grad_branch.astype(f32))
    grad_hidden = grad_two
    for f in range(hidden_units // FB):
        part = slice(f * FB, f * FB + FB)
        grad_up = (dot(grad_branch, wd_ref[part, :], NT) * slope_ref[:, part]).astype(bf16)
        gu_ref[:, part] = grad_up
        gbu_ref[:, part] += jnp.sum(grad_up.astype(f32), axis=0, keepdims=True)
        grad_hidden = grad_hidden + dot(grad_up, wu_ref[:, part], NT)
    add_vec(3, grad_hidden * unit_one)
    add_vec(4, grad_hidden)
    grad_one = norm_back(grad_hidden, vec(1), unit_one, scale_one)
    gp_ref[...] = grad_one
    grad_attn = grad_one.astype(bf16)
    ga_ref[...] = grad_attn
    add_vec(5, grad_attn.astype(f32))
    gm_ref[...] = dot(grad_attn, wo_ref[...], NT).astype(bf16)


def feed_forward(lengths, tokens, mixed, cotangent, full_up_out, full_down, full_qkv, bias_up):
    rows, width = tokens.shape
    units = bias_up.shape[1]
    by_rows = pl.BlockSpec((TB, width), lambda i: (i, 0))
    by_units = pl.BlockSpec((TB, units), lambda i: (i, 0))

    def whole(shape, column=0):
        return pl.BlockSpec(shape, lambda i: (0, column), pipeline_mode=pl.Buffered(1))

    def kept(shape):
        return pl.BlockSpec(shape, lambda i: (0,) * len(shape))

    low = jax.ShapeDtypeStruct((rows, width), bf16)
    wide = jax.ShapeDtypeStruct((rows, units), bf16)
    return pl.pallas_call(
        feed_forward_kernel,
        grid=(rows // TB,),
        in_specs=[
            pl.BlockSpec(memory_space=pltpu.SMEM),
            by_rows, *[pl.BlockSpec((TB, part.shape[1]), lambda i: (i, 0)) for part in mixed], by_rows,
            whole((width, width), units // width), whole((width, units)), whole(full_down.shape),
            whole((width, 128), 3 * width // 128), whole(bias_up.shape),
        ],
        out_specs=[by_rows] * 7 + [by_units] * 2 + [kept((8, width)), kept((1, units))],
        out_shape=[low, jax.ShapeDtypeStruct((rows, width), f32), low, low, low, low, low, wide, wide,
                   jax.ShapeDtypeStruct((8, width), f32), jax.ShapeDtypeStruct((1, units), f32)],
        scratch_shapes=[pltpu.VMEM((TB, units), f32), pltpu.VMEM((8, width), f32)],
        compiler_params=pltpu.CompilerParams(vmem_limit_bytes=56 << 20),
        cost_estimate=pl.CostEstimate(flops=8 * rows * width * units + 4 * rows * width * width, bytes_accessed=40 << 20, transcendentals=0),
        name="feed_forward",
    )(lengths, tokens, *mixed, cotangent, full_up_out, full_up_out, full_down, full_qkv, bias_up)


def store_blocks(place_ref, total_ref, near_ref, far_ref, at, base=0):
    size = near_ref.shape[-2]
    own = place_ref[BLOCKS]
    for pair in range(total_ref.shape[0] // (2 * size)):
        for ref, core in ((near_ref, own), (far_ref, 1 - own)):
            block = 2 * pair + core
            rows = pl.ds(pl.multiple_of(block * size, size), size)
            ref[(place_ref[base + block] % (BLOCKS // 2), *at)] = total_ref[rows, :].astype(bf16)


def weight_grad_kernel(place_ref, left_ref, right_ref, near_ref, far_ref, left_t_ref, total_ref):
    @pl.when(pl.program_id(0) == 0)
    def _():
        left_t_ref[...] = left_ref[...].T

    total_ref[...] = dot(left_t_ref[...], right_ref[...])
    store_blocks(place_ref, total_ref, near_ref, far_ref, (0,))


def weight_grad_wide(place, left, right, cols):
    rows, width = left.shape
    groups = right.shape[1] // cols
    size = width // BLOCKS
    return pl.pallas_call(
        weight_grad_kernel,
        grid=(groups,),
        in_specs=[
            pl.BlockSpec(memory_space=pltpu.SMEM),
            pl.BlockSpec((rows, width), lambda g: (0, 0)),
            pl.BlockSpec((rows, cols), lambda g: (0, g)),
        ],
        out_specs=[pl.BlockSpec((BLOCKS // 2, 1, size, cols), lambda g: (0, g, 0, 0))] * 2,
        out_shape=[jax.ShapeDtypeStruct((BLOCKS // 2, groups, size, cols), bf16)] * 2,
        scratch_shapes=[pltpu.VMEM((width, rows), bf16), pltpu.VMEM((width, cols), f32)],
        compiler_params=pltpu.CompilerParams(vmem_limit_bytes=20 << 20),
        cost_estimate=pl.CostEstimate(flops=2 * rows * width * right.shape[1], bytes_accessed=12 << 20, transcendentals=0),
        name="weight_grad_wide",
    )(place, left, right)


def weight_grad_tall_kernel(place_ref, left_ref, right_ref, near_ref, far_ref, total_ref):
    total_ref[...] = dot(left_ref[...], right_ref[...], TN)
    base = pl.program_id(0) * (total_ref.shape[0] // near_ref.shape[1])
    store_blocks(place_ref, total_ref, near_ref, far_ref, (), base)


def weight_grad_tall(place, left, right):
    rows, units = left.shape
    width = right.shape[1]
    size = units // BLOCKS
    return pl.pallas_call(
        weight_grad_tall_kernel,
        grid=(units // width,),
        in_specs=[
            pl.BlockSpec(memory_space=pltpu.SMEM),
            pl.BlockSpec((rows, width), lambda g: (0, g)),
            pl.BlockSpec((rows, width), lambda g: (0, 0)),
        ],
        out_specs=[pl.BlockSpec((BLOCKS // 2, size, width), lambda g: (0, 0, 0))] * 2,
        out_shape=[jax.ShapeDtypeStruct((BLOCKS // 2, size, width), bf16)] * 2,
        scratch_shapes=[pltpu.VMEM((width, width), f32)],
        compiler_params=pltpu.CompilerParams(vmem_limit_bytes=20 << 20),
        cost_estimate=pl.CostEstimate(flops=2 * rows * width * units, bytes_accessed=12 << 20, transcendentals=0),
        name="weight_grad_tall",
    )(place, left, right)


def attend_backward_kernel(
    len_ref, place_ref, x_ref, q_ref, k_ref, v_ref, do_ref, o_ref, lse_ref,
    dq_ref, dk_ref, dv_ref, near_ref, far_ref, gbias_ref,
    xt_ref, qs_ref, dos_ref, qt_ref, dot_ref, ka_ref, va_ref, kt_ref, code_q_ref, code_k_ref,
    dqt_ref, dk_acc, dv_acc, total_ref,
):
    rows, cols = q_ref.shape
    heads = cols // HD
    ends = ends_of(len_ref)

    xt_ref[...] = x_ref[...].T
    code_q, code_k = segment_codes(rows, ends)
    code_q_ref[...] = code_q
    spot = lax.broadcasted_iota(jnp.int32, (rows, 128), 1) % HD
    code_k_ref[...] = jnp.where((spot >= 2 * BITS) & (spot < 2 * BITS + 3), 1.0, code_k).astype(bf16)

    query, keys, values, grad = q_ref[...], k_ref[...], v_ref[...], do_ref[...]
    lane = lax.broadcasted_iota(jnp.int32, (rows, 128), 1)
    for h in range(heads):
        pair = slice(128 * (h // 2), 128 * (h // 2) + 128)
        own = (lane >= HD) if h % 2 else (lane < HD)
        qs_ref[h] = jnp.where(own, query[:, pair] * bf16(SCALE), bf16(0))
        dos_ref[h] = jnp.where(own, grad[:, pair], bf16(0))
    kt_ref[...] = keys.T
    product = grad.astype(f32) * o_ref[...].astype(f32)
    high_part = product.astype(bf16)
    low_part = (product - high_part.astype(f32)).astype(bf16)
    pick = (
        lax.broadcasted_iota(jnp.int32, (8, cols), 1) // HD
        == lax.broadcasted_iota(jnp.int32, (8, cols), 0)
    ).astype(bf16)
    delta = dot(pick, high_part, NT) + dot(pick, low_part, NT)
    turned, turned_grad = (query * bf16(SCALE)).T, grad.T
    lane = lax.broadcasted_iota(jnp.int32, (rows, 128), 1)
    ones = jnp.where(lane % HD < 3, 1.0, 0.0).astype(bf16)
    for h in range(heads):
        part = slice(h * HD, h * HD + HD)
        pair = slice(128 * (h // 2), 128 * (h // 2) + 128)
        own = (lane >= HD) if h % 2 else (lane < HD)
        code = jnp.concatenate(
            [code_q_ref[: 2 * BITS].astype(f32)]
            + [piece.astype(f32) for piece in pieces(-lse_ref[0, h : h + 1, :])]
            + [jnp.zeros((HD - 2 * BITS - 3, rows), f32)],
            axis=0,
        ).astype(bf16)
        qt_ref[h] = other_half(turned[part], code, h)
        ka_ref[h] = jnp.where(own, keys[:, pair], code_k_ref[...])
        shift = jnp.concatenate(
            [piece.astype(f32) for piece in pieces(-delta[h : h + 1, :])]
            + [jnp.zeros((HD - 3, rows), f32)],
            axis=0,
        ).astype(bf16)
        dot_ref[h] = other_half(turned_grad[part], shift, h)
        va_ref[h] = jnp.where(own, values[:, pair], ones)
    dk_acc[...] = jnp.zeros_like(dk_acc)
    dv_acc[...] = jnp.zeros_like(dv_acc)

    def q_step(qi, _):
        q_rows = pl.ds(pl.multiple_of(qi * BACKWARD_TILE, BACKWARD_TILE), BACKWARD_TILE)
        low, high = key_range(ends, qi * BACKWARD_TILE, qi * BACKWARD_TILE + BACKWARD_TILE - 1, BACKWARD_TILE)
        dqt_ref[...] = jnp.zeros_like(dqt_ref)

        def k_step(ki, _):
            k_rows = pl.ds(pl.multiple_of(ki * BACKWARD_TILE, BACKWARD_TILE), BACKWARD_TILE)

            def products_of(h):
                return (
                    dot(ka_ref[h, k_rows, :], qt_ref[h, :, q_rows]),
                    dot(va_ref[h, k_rows, :], dot_ref[h, :, q_rows]),
                )

            ahead = [products_of(h) for h in range(2)]
            pending = []

            def finish(p, probs_a, grads_a, probs_b, grads_b):
                pair = slice(128 * p, 128 * p + 128)
                dv_acc[k_rows, pair] += dot(probs_a, dos_ref[2 * p, q_rows, :]) + dot(
                    probs_b, dos_ref[2 * p + 1, q_rows, :]
                )
                dk_acc[k_rows, pair] += dot(grads_a, qs_ref[2 * p, q_rows, :]) + dot(
                    grads_b, qs_ref[2 * p + 1, q_rows, :]
                )
                for h, grads in ((2 * p, grads_a), (2 * p + 1, grads_b)):
                    part = slice(h * HD, h * HD + HD)
                    dqt_ref[part, :] += dot(kt_ref[part, k_rows], grads)

            held = []
            for h in range(heads):
                if h + 2 < heads:
                    ahead.append(products_of(h + 2))
                scores, grad_probs = ahead[h]
                ahead[h] = None
                probs = jnp.exp(scores)
                grad_scores = (probs * grad_probs).astype(bf16)
                held += [probs.astype(bf16), grad_scores]
                if h % 2:
                    pending.append((h // 2, *held))
                    held = []
                if h % 2 and len(pending) > 1:
                    finish(*pending.pop(0))
            for item in pending:
                finish(*item)
            return 0

        lax.fori_loop(low, high, k_step, 0)
        dq_ref[q_rows, :] = (dqt_ref[...] * SCALE).T.astype(bf16)
        return 0

    lax.fori_loop(0, rows // BACKWARD_TILE, q_step, 0)
    dk_ref[...] = dk_acc[...].astype(bf16)
    dv_ref[...] = dv_acc[...].astype(bf16)
    for s, part in enumerate((dq_ref, dk_ref, dv_ref)):
        total_ref[...] = dot(xt_ref[...], part[...])
        store_blocks(place_ref, total_ref, near_ref, far_ref, (s,))
    gbias_ref[0:1, :] = jnp.sum(dq_ref[...].astype(f32), axis=0, keepdims=True)
    gbias_ref[1:2, :] = jnp.sum(dv_ref[...].astype(f32), axis=0, keepdims=True)


def attend_backward(group, lengths, place, tokens, query, keys, values, grad_mixed, mixed, lse):
    rows, width = tokens.shape
    cols = COLS
    heads = cols // HD
    size = width // BLOCKS
    by_group = pl.BlockSpec((rows, cols), lambda g: (0, group))
    own = pl.BlockSpec((rows, cols), lambda g: (0, 0))
    low = jax.ShapeDtypeStruct((rows, cols), bf16)
    return pl.pallas_call(
        attend_backward_kernel,
        grid=(1,),
        in_specs=[
            pl.BlockSpec(memory_space=pltpu.SMEM),
            pl.BlockSpec(memory_space=pltpu.SMEM),
            pl.BlockSpec((rows, width), lambda g: (0, 0)),
        ]
        + [own] * 3
        + [by_group]
        + [own]
        + [pl.BlockSpec((1, 8, rows), lambda g: (0, 0, 0))],
        out_specs=[own] * 3
        + [
            pl.BlockSpec((BLOCKS // 2, 3, size, cols), lambda g: (0, 0, 0, 0)),
            pl.BlockSpec((BLOCKS // 2, 3, size, cols), lambda g: (0, 0, 0, 0)),
            pl.BlockSpec((8, cols), lambda g: (0, 0)),
        ],
        out_shape=[low] * 3
        + [
            jax.ShapeDtypeStruct((BLOCKS // 2, 3, size, cols), bf16),
            jax.ShapeDtypeStruct((BLOCKS // 2, 3, size, cols), bf16),
            jax.ShapeDtypeStruct((8, cols), f32),
        ],
        scratch_shapes=[
            pltpu.VMEM((width, rows), bf16),
            pltpu.VMEM((heads, rows, 128), bf16),
            pltpu.VMEM((heads, rows, 128), bf16),
            pltpu.VMEM((heads, 128, rows), bf16),
            pltpu.VMEM((heads, 128, rows), bf16),
            pltpu.VMEM((heads, rows, 128), bf16),
            pltpu.VMEM((heads, rows, 128), bf16),
            pltpu.VMEM((cols, rows), bf16),
            pltpu.VMEM((HD, rows), bf16),
            pltpu.VMEM((rows, 128), bf16),
            pltpu.VMEM((cols, BACKWARD_TILE), f32),
            pltpu.VMEM((rows, cols), f32),
            pltpu.VMEM((rows, cols), f32),
            pltpu.VMEM((width, cols), f32),
        ],
        compiler_params=pltpu.CompilerParams(vmem_limit_bytes=44 << 20),
        cost_estimate=pl.CostEstimate(flops=12 * rows * width * width, bytes_accessed=16 << 20, transcendentals=0),
        name="attend_backward",
    )(lengths, place, tokens, query, keys, values, grad_mixed, mixed, lse)


def token_grad_kernel(gp_ref, *refs):
    *grads, w_ref, out_ref = refs
    total = gp_ref[...]
    cols = grads[0].shape[1]
    for i, grad in enumerate(grads):
        total = total + dot(grad[...], w_ref[:, i * cols : i * cols + cols], NT)
    out_ref[...] = total


def token_grad(grad_one, grads, full_qkv):
    rows, width = grad_one.shape
    cols = grads[0].shape[1]
    by_rows = pl.BlockSpec((TB, width), lambda i: (i, 0))
    return pl.pallas_call(
        token_grad_kernel,
        grid=(rows // TB,),
        in_specs=[by_rows]
        + [pl.BlockSpec((TB, cols), lambda i: (i, 0))] * len(grads)
        + [pl.BlockSpec((width, 3 * width), lambda i: (0, 0), pipeline_mode=pl.Buffered(1))],
        out_specs=by_rows,
        out_shape=jax.ShapeDtypeStruct((rows, width), f32),
        compiler_params=pltpu.CompilerParams(vmem_limit_bytes=28 << 20),
        cost_estimate=pl.CostEstimate(flops=6 * rows * width * width, bytes_accessed=14 << 20, transcendentals=0),
        name="token_grad",
    )(grad_one, *grads, full_qkv)


def assemble_kernel(blocks_ref, near_ref, far_ref, out_ref):
    count = near_ref.shape[0]
    for m in range(count):
        out_ref[blocks_ref[m]] = near_ref[m]
        out_ref[blocks_ref[count + m]] = far_ref[m]


def assemble(blocks_at, near, far):
    rows, cols = near.shape[1:]
    parts = 1
    while cols % (2 * parts * 128) == 0 and cols // parts > 1024:
        parts *= 2
    while cols // parts > 1024 and cols % (3 * parts * 128) == 0:
        parts *= 3
    by_cols = pl.BlockSpec((near.shape[0], rows, cols // parts), lambda i: (0, 0, i))
    return pl.pallas_call(
        assemble_kernel,
        grid=(parts,),
        in_specs=[pl.BlockSpec(memory_space=pltpu.SMEM), by_cols, by_cols],
        out_specs=pl.BlockSpec((BLOCKS, rows, cols // parts), lambda i: (0, 0, i)),
        out_shape=jax.ShapeDtypeStruct((BLOCKS, rows, cols), near.dtype),
        compiler_params=pltpu.CompilerParams(vmem_limit_bytes=20 << 20),
        cost_estimate=pl.CostEstimate(flops=0, bytes_accessed=4 * near.size * 2, transcendentals=0),
        name="assemble",
    )(blocks_at, near, far)


CORE, X, Y, Z_LOW, Z_HIGH = 1, 2, 4, 8, 16


def relative_places():
    places = np.zeros((32, 32), np.int32)
    for i in range(32):
        for b in range(32):
            bits = i ^ b
            x, y = int(bits & X > 0), int(bits & Y > 0)
            first, second = (y, x) if b & CORE else (x, y)
            low, high = int(bits & Z_LOW > 0), int(bits & Z_HIGH > 0)
            places[i, b] = 16 * (bits & CORE) + 8 * first + 4 * second + 2 * low + high
    return places


def exchange(values, even, odd):
    return lax.ppermute(
        values, "dp", [(i, i ^ (odd if i & CORE else even)) for i in range(32)]
    )


def added(a, b):
    return (a.astype(f32) + b.astype(f32)).astype(bf16)


def after(values, *earlier):
    return lax.optimization_barrier((values, *earlier))[0]


GATHER_HOPS = ((Z_HIGH, Z_HIGH), (Z_LOW, Z_LOW), (Y, X), (X, Y), (CORE, CORE))


def gather_blocks(*own):
    held = [part[None] for part in own]
    earlier = yield
    for hop in GATHER_HOPS:
        if earlier is not None:
            held[0] = after(held[0], *earlier)
        near, got = held[0], [exchange(part, *hop) for part in held]
        if hop[0] != CORE:
            held = [jnp.concatenate([jnp.concatenate(held, axis=2), jnp.concatenate(got, axis=2)], axis=0)]
        earlier = yield got[0], near


def fold(pairs):
    half = pairs[0][0].shape[0] // 2

    def joined(rows):
        return jnp.concatenate([added(kept[rows], got[rows]) for kept, got in pairs], axis=1)

    return joined(slice(half, 2 * half)), joined(slice(0, half))


def meet(parts):
    return [(near, exchange(far, CORE, CORE)) for near, far in parts]


def hop(state, even, odd):
    send, keep = state
    return keep, exchange(send, even, odd)


def total(pair):
    return pair[0][0].astype(f32) + pair[1][0].astype(f32)


def body(
    tokens, cotangent, lengths, w_qkv, w_out, w_up, w_down, bias_q, bias_v, bias_out,
    gain_one, shift_one, bias_up, bias_down, gain_two, shift_two,
):
    count = lax.axis_size("dp")
    index = lax.axis_index("dp")
    width = tokens.shape[1]
    units = w_up.shape[1]
    shard = w_qkv.shape[0]
    ratio = units // width
    small = jnp.concatenate(
        [bias_q, bias_v, bias_out, gain_one, shift_one, bias_down, gain_two, shift_two]
    )
    small = jnp.concatenate([small.reshape(8, shard).T, bias_up.reshape(shard, ratio)], axis=1)
    small = jnp.pad(small, ((0, 0), (0, 128 - small.shape[1])))
    up_out_shard = jnp.concatenate([w_up, w_out], axis=1)
    if count == BLOCKS:
        table = relative_places()
        core = np.arange(BLOCKS)[:, None] & CORE
        place = jnp.asarray(np.concatenate([table, core], axis=1).astype(np.int32))[index]
        blocks_at = jnp.asarray(np.argsort(table, axis=1).astype(np.int32))[index]
        first, second = gather_blocks(w_qkv, small), gather_blocks(up_out_shard)
        next(first)
        next(second)
        full_down = lax.all_gather(w_down, "dp", axis=0, tiled=True)
        hops = [first.send(None) for _ in range(5)]
        far, near = hops[4]
        full_qkv = assemble(blocks_at, near, far).reshape(width, -1)
        arrived = [second.send([hops[3][0]])[0], second.send([far])[0]]
    else:
        place = jnp.arange(BLOCKS, dtype=jnp.int32) // 2
        place = jnp.append(place, 0)
        full_qkv, full_up_out, full_down = (
            lax.all_gather(part, "dp", axis=0, tiled=True)
            for part in (jnp.concatenate([w_qkv, small], axis=1), up_out_shard, w_down)
        )
    vectors = full_qkv[:, 3 * width :]
    full_bias_up = vectors[:, 8 : 8 + ratio].reshape(1, units)

    forward = []
    for g in range(width // COLS):
        held = tokens
        if count == BLOCKS:
            held = after(tokens, arrived[g])
            if g:
                arrived.append(second.send([forward[-1][3]])[0])
        forward.append(attend_forward(g, lengths, held, full_qkv))
    if count == BLOCKS:
        far, near = second.send([part[3] for part in forward])
        full_up_out = assemble(blocks_at, near, far).reshape(width, -1)
    (
        output, grad_one, grad_attn, grad_mixed, hidden_low, grad_branch, mixed, active, grad_up,
        gvec, gbu,
    ) = feed_forward(
        lengths, tokens, [part[3] for part in forward], cotangent, full_up_out, full_down,
        full_qkv, full_bias_up,
    )
    part_down = weight_grad_tall(place, active, grad_branch)
    part_up = weight_grad_wide(place, after(hidden_low, part_down[0]), grad_up, width)
    part_out = weight_grad_wide(place, after(mixed, part_up[0]), grad_attn, COLS)
    milestones = []

    def backward(g):
        held = after(grad_mixed, *milestones)
        query, keys, values, own_mixed, lse = forward[g]
        return attend_backward(g, lengths, place, tokens, query, keys, values, held, own_mixed, lse)

    if count != BLOCKS:
        groups = [backward(g) for g in range(width // COLS)]
        grad_tokens = token_grad(
            grad_one, [group[s] for s in range(3) for group in groups], full_qkv
        )
        gbias = jnp.concatenate([group[5] for group in groups], axis=1)
        def scattered(part):
            return lax.psum_scatter(part, "dp", scatter_dimension=0, tiled=True).astype(f32)

        def lined(halves):
            part = jnp.stack(halves, axis=1).reshape(BLOCKS, *halves[0].shape[1:])
            return part.transpose(0, 2, 1, 3).reshape(width, -1)

        part_qkv = [jnp.concatenate([group[h] for group in groups], axis=3) for h in (3, 4)]
        tall_down = jnp.stack(part_down, axis=1).reshape(units, width)
        return (
            output, grad_tokens, scattered(lined(part_qkv)), scattered(lined(part_out)),
            scattered(lined(part_up)), scattered(tall_down),
            scattered(gbias[0]), scattered(gbias[1]), scattered(gvec[5]), scattered(gvec[3]),
            scattered(gvec[4]), scattered(gbu[0]), scattered(gvec[2]), scattered(gvec[0]),
            scattered(gvec[1]),
        )

    def small_part(lines, width):
        line = jnp.concatenate(
            [
                part.reshape(part.shape[0], BLOCKS, -1).transpose(1, 0, 2).reshape(BLOCKS, -1)
                for part in lines
            ],
            axis=1,
        )
        line = jnp.pad(line.astype(bf16), ((0, 0), (0, width - line.shape[1])))
        line = jnp.pad(line[blocks_at][:, None, :], ((0, 0), (0, 7), (0, 0)))
        return line[: BLOCKS // 2], line[BLOCKS // 2 :]

    def rows_of(halves):
        return [half.reshape(half.shape[0], -1, half.shape[-1]) for half in halves]

    small_mlp = small_part([gvec[:6], gbu], width)
    down = fold(meet([part_down, small_mlp]))
    down_first = hop(down, X, Y)
    up_met = meet([rows_of(part_up)])
    out_met = meet([rows_of(part_out)])
    up = fold(up_met)
    milestones += [part_out[0], up[0]]
    groups = [backward(0)]
    up_first = hop(up, X, Y)
    milestones[:] = [groups[0][0]]
    mlp = fold([down_first, up_first])
    milestones += [mlp[0]]
    groups.append(backward(1))
    mlp = fold([hop(mlp, Y, X)])
    early = fold(out_met + meet([rows_of(groups[0][3:5])]))
    milestones[:] = [groups[1][0], mlp[0], early[0]]
    groups.append(backward(2))
    mlp = fold([hop(mlp, Z_LOW, Z_LOW)])
    early_first = hop(early, X, Y)
    gbias = jnp.concatenate([group[5] for group in groups], axis=1)
    small_attn = small_part([gbias[:2]], COLS)
    late = fold(meet([rows_of(groups[1][3:5]), rows_of(groups[2][3:5]), small_attn]))
    late_first = hop(late, X, Y)
    grad_tokens = token_grad(
        grad_one, [group[s] for s in range(3) for group in groups], full_qkv
    )
    mlp = total(hop(mlp, Z_HIGH, Z_HIGH))
    attn = fold([early_first, late_first])
    attn = fold([hop(attn, Y, X)])
    attn = fold([hop(attn, Z_LOW, Z_LOW)])
    attn = total(hop(attn, Z_HIGH, Z_HIGH))

    def wide_of(rows):
        return rows.reshape(-1, shard, width).transpose(1, 0, 2).reshape(shard, -1)

    tall = ratio * shard
    line = mlp[tall]
    attn = [attn[i * shard : i * shard + shard] for i in range(12)] + [attn[12 * shard]]
    line_attn = attn[12]
    grad_out_weight = jnp.concatenate(attn[:3], axis=1)
    grad_qkv = jnp.concatenate([attn[3 + 3 * g + s] for s in range(3) for g in range(3)], axis=1)

    def piece(line, i):
        return line[i * shard : i * shard + shard]

    return (
        output, grad_tokens, grad_qkv, grad_out_weight,
        wide_of(mlp[tall + 8 :]), mlp[:tall],
        piece(line_attn, 0), piece(line_attn, 1), piece(line, 5), piece(line, 3), piece(line, 4),
        line[6 * shard : 6 * shard + tall], piece(line, 2), piece(line, 0), piece(line, 1),
    )


def solution(mesh):
    rows, vector = P("dp", None), P("dp")
    return jax.shard_map(
        body, mesh=mesh, in_specs=(rows,) * 7 + (vector,) * 9, out_specs=(rows,) * 6 + (vector,) * 9,
        check_vma=False,
    )
```

time: 476 us -> 348 us (0.73)
  waiting for transfers between devices: 170 us -> 107 us
  local copies, waits for them, and re-layouts: 63.6 us -> 31.9 us
  Pallas kernels: 180 us -> 149 us
    all_gather x2 -> x1, waiting for transfers between devices: 88.7 us -> 0.01 us  [body(): full_down = lax.all_gather(w_down, 'dp', axis=0, tiled=True)]
    pallas_call x2 -> x8, Pallas kernels: 115 us -> 78.7 us  [the longest x3 43.5 us: attend_backward(): pl.pallas_call(attend_backward_kernel, grid=(1,), in_specs=[pl.BlockSpec(...]
    ppermute x14 -> x29, waiting for transfers between devices: 80.9 us -> 107 us  [exchange(): lax.ppermute(values, 'dp', [(i, i ^ (odd if i & CORE else even)) for i in...]
    slice x16 -> x9, local copies, waits for them, and re-layouts: 23.4 us -> 0.38 us  [the longest x5 0.31 us: joined(): kept[rows]]
    reshape x3 -> x5, local copies, waits for them, and re-layouts: 10.3 us -> 1.11 us  [the longest x1 0.75 us: body(): bias_up.reshape(shard, ratio)]
    another operation x19 -> x1, local copies, waits for them, and re-layouts: 6.9 us -> 0.09 us  [small_part(): part.reshape(part.shape[0], BLOCKS, -1).transpose(1, 0, 2)]
    concatenate x2 -> x3, local copies, waits for them, and re-layouts: 0.2 us -> 5.55 us  [the longest x1 5.43 us: body(): jnp.concatenate([bias_q, bias_v, bias_out, gain_one, shift_one, bias_down...]
    unnamed x51 -> x132, local copies, waits for them, and re-layouts: 13.7 us -> 17.4 us
  transfers between devices with their start and end apart: 16 -> 30, of which waited for: 10 -> 16; matrix products, arithmetic and copies ran while one was open for 8% -> 9% of each run, Pallas kernels for 28% -> 28%
where the time goes in v2:
time: 348 us; the launch traced here: 345 us
  Pallas kernels  149 us (43%)
  waiting for transfers between devices  107 us (31%)
  local copies, waits for them, and re-layouts  31.9 us (9%)
  starting transfers between devices  23.9 us (7%)
  other arithmetic  18.4 us (5%)
  between operations  15.6 us (4%)
    ppermute x29, waiting for transfers between devices, exchange(): lax.ppermute(values, 'dp', [(i, i ^ (odd if i & CORE else even)) for i in...  107 us
    pallas_call x1, Pallas kernels, feed_forward(): pl.pallas_call(feed_forward_kernel, grid=(rows // TB,), in_specs=[pl.Bloc...  43.7 us
    pallas_call x3, Pallas kernels, attend_backward(): pl.pallas_call(attend_backward_kernel, grid=(1,), in_specs=[pl.BlockSpec(...  43.5 us
    pallas_call x3, Pallas kernels, attend_forward(): pl.pallas_call(functools.partial(attend_forward_kernel, group), grid=(1,)...  29.2 us
    ppermute x29, starting transfers between devices, exchange(): lax.ppermute(values, 'dp', [(i, i ^ (odd if i & CORE else even)) for i in...  23.9 us
    unnamed x132, local copies, waits for them, and re-layouts  17.4 us
    convert_element_type x16, other arithmetic, added(): return (a.astype(f32) + b.astype(f32)).astype(bf16)  12.1 us
    pallas_call x2, Pallas kernels, weight_grad_wide(): pl.pallas_call(weight_grad_kernel, grid=(groups,), in_specs=[pl.BlockSpec...  12 us
  transfers between devices with their start and end apart: 30, of which 16 were waited for; matrix products, arithmetic and copies ran while one was open for 9% of the time, Pallas kernels for 28%

profile of v2, /device:TPU:0, one launch (start us, length us, event | category | flops | bytes accessed | tf_op | source)
XLA Modules:
  0.0 344.9 jit_solution(5688152216034254729)
XLA Ops:
  11.3 5.4 %concatenate.87 = bf16[192]{0:T(256)(128)(2,1)S(1)} concatenate(bf16[24]{0:T(256)(128)(2,1)} %param.25, bf16[24]{0:T(256)(128)(2,1)} %param.26, bf16[24]{0:T(256)(128)(2,1)} %param.27, bf16[24]{0:T(256)(128)(2,1)} %param.28, bf16[24]{0:T(256)(128)(2,1)} %param.29, bf16[24]{0:T(256)(128)(2,1)} %param.31, bf16[24]{0:T(256)(128)(2,1)} %param.32, bf16[24]{0:T(256)(128)(2,1)} %param.33), dimensions={0} | concatenate | bytes 768 | tf_op jit(solution)/shard_map/concatenate | solution.py:689
  24.9 4.5 %collective-permute-done.2 = bf16[2,24,2432]{2,1,0:T(8,128)(2,1)S(1)} collective-permute-done((bf16[2,24,2432]{2,1,0:T(8,128)(2,1)S(1)}, bf16[2,24,2432]{2,1,0:T(8,128)(2,1)S(1)}, u32[]{:S(2)}, u32[]{:S(2)}) %collective-permute-start.2) | collective-permute-done | bytes 233504 | tf_op jit(solution)/shard_map/ppermute | solution.py:629
  31.9 7.8 %collective-permute-done.3 = bf16[4,24,2432]{2,1,0:T(8,128)(2,1)S(1)} collective-permute-done((bf16[4,24,2432]{2,1,0:T(8,128)(2,1)S(1)}, bf16[4,24,2432]{2,1,0:T(8,128)(2,1)S(1)}, u32[]{:S(2)}, u32[]{:S(2)}) %collective-permute-start.3) | collective-permute-done | bytes 466976 | tf_op jit(solution)/shard_map/ppermute | solution.py:629
  41.5 12.0 %collective-permute-done.4 = bf16[8,24,2432]{2,1,0:T(8,128)(2,1)S(1)} collective-permute-done((bf16[8,24,2432]{2,1,0:T(8,128)(2,1)S(1)}, bf16[8,24,2432]{2,1,0:T(8,128)(2,1)S(1)}, u32[]{:S(2)}, u32[]{:S(2)}) %collective-permute-start.4) | collective-permute-done | bytes 933920 | tf_op jit(solution)/shard_map/ppermute | solution.py:629
  54.5 11.4 %collective-permute-done.5 = bf16[1,24,3840]{2,1,0:T(8,128)(2,1)S(1)} collective-permute-done((bf16[1,24,3840]{2,1,0:T(8,128)(2,1)S(1)}, bf16[1,24,3840]{2,1,0:T(8,128)(2,1)S(1)}, u32[]{:S(2)}, u32[]{:S(2)}) %collective-permute-start.5) | collective-permute-done | bytes 184352 | tf_op jit(solution)/shard_map/ppermute | solution.py:629
  68.0 10.1 %attend_forward.3 = (bf16[1024,256]{1,0:T(8,128)(2,1)S(1)}, bf16[1024,256]{1,0:T(8,128)(2,1)S(1)}, bf16[1024,256]{1,0:T(8,128)(2,1)S(1)}, bf16[1024,256]{1,0:T(8,128)(2,1)S(1)}, f32[1,8,1024]{2,1,0:T(8,128)S(1)}) custom-call(s32[1,8]{1,0:T(1,128)S(1)} %copy-done.16, bf16[1024,768]{1,0:T(8,128)(2,1)S(1)} %copy-done.14, bf16[768,2432]{1,0:T(8,128)(2,1)S(1)} %bitcast.128, ...), custom_call_target="tpu_custom_call" | custom-call | flops 7247757312 | bytes 12582912 | tf_op jit(solution)/shard_map/attend_forward/pallas_call | solution.py:172
  82.1 9.6 %attend_forward.4 = (bf16[1024,256]{1,0:T(8,128)(2,1)S(1)}, bf16[1024,256]{1,0:T(8,128)(2,1)S(1)}, bf16[1024,256]{1,0:T(8,128)(2,1)S(1)}, bf16[1024,256]{1,0:T(8,128)(2,1)S(1)}, f32[1,8,1024]{2,1,0:T(8,128)S(1)}) custom-call(s32[1,8]{1,0:T(1,128)S(1)} %copy-done.16, bf16[1024,768]{1,0:T(8,128)(2,1)S(1)} %copy-done.14, bf16[768,2432]{1,0:T(8,128)(2,1)S(1)} %bitcast.132, ...), custom_call_target="tpu_custom_call" | custom-call | flops 7247757312 | bytes 12582912 | tf_op jit(solution)/shard_map/attend_forward/pallas_call | solution.py:172
  94.5 9.6 %attend_forward.5 = (bf16[1024,256]{1,0:T(8,128)(2,1)S(1)}, bf16[1024,256]{1,0:T(8,128)(2,1)S(1)}, bf16[1024,256]{1,0:T(8,128)(2,1)S(1)}, bf16[1024,256]{1,0:T(8,128)(2,1)S(1)}, f32[1,8,1024]{2,1,0:T(8,128)S(1)}) custom-call(s32[1,8]{1,0:T(1,128)S(1)} %copy-done.16, bf16[1024,768]{1,0:T(8,128)(2,1)S(1)} %copy-done.14, bf16[768,2432]{1,0:T(8,128)(2,1)S(1)} %bitcast.136, ...), custom_call_target="tpu_custom_call" | custom-call | flops 7247757312 | bytes 12582912 | tf_op jit(solution)/shard_map/attend_forward/pallas_call | solution.py:172
  104.1 16.7 %collective-permute-done.9 = bf16[8,24,3840]{2,1,0:T(8,128)(2,1)S(1)} collective-permute-done((bf16[8,24,3840]{2,1,0:T(8,128)(2,1)S(1)}, bf16[8,24,3840]{2,1,0:T(8,128)(2,1)S(1)}, u32[]{:S(2)}, u32[]{:S(2)}) %collective-permute-start.9) | collective-permute-done | bytes 1474592 | tf_op jit(solution)/shard_map/ppermute | solution.py:629
  123.0 4.1 %collective-permute-done.10.far_ref = bf16[16,24,3840]{2,1,0:T(8,128)(2,1)} collective-permute-done((bf16[16,24,3840]{2,1,0:T(8,128)(2,1)S(1)}, bf16[16,24,3840]{2,1,0:T(8,128)(2,1)}, u32[]{:S(2)}, u32[]{:S(2)}) %collective-permute-start.10) | collective-permute-done | bytes 2949152 | tf_op jit(solution)/shard_map/ppermute | solution.py:629
  127.1 4.1 %assemble.3 = bf16[32,24,3840]{2,1,0:T(8,128)(2,1)S(1)} custom-call(s32[32]{0:T(128)S(1)} %fusion.19.blocks_ref, bf16[16,24,3840]{2,1,0:T(8,128)(2,1)S(1)} %pad_maximum_fusion.near_ref, bf16[16,24,3840]{2,1,0:T(8,128)(2,1)} %collective-permute-done.10.far_ref), custom_call_target="tpu_custom_call" | custom-call | bytes 11796480 | tf_op jit(solution)/shard_map/assemble/pallas_call | solution.py:601
  133.7 43.7 %feed_forward.1 = (bf16[1024,768]{1,0:T(8,128)(2,1)}, f32[1024,768]{1,0:T(8,128)}, bf16[1024,768]{1,0:T(8,128)(2,1)}, bf16[1024,768]{1,0:T(8,128)(2,1)}, bf16[10...) custom-call(s32[1,8]{1,0:T(1,128)} %len_ref.13, ...), custom_call_target="tpu_custom_call" | custom-call | flops 21743271936 | bytes 41943040 | tf_op jit(solution)/shard_map/feed_forward/pallas_call | solution.py:301
  181.7 8.6 %weight_grad_tall.1 = (bf16[16,96,768]{2,1,0:T(8,128)(2,1)S(1)}, bf16[16,96,768]{2,1,0:T(8,128)(2,1)}) custom-call(s32[33]{0:T(128)S(1)} %dynamic-slice_bitcast_fusion.place_ref, bf16[1024,3072]{1,0:T(8,128)(2,1)S(1)} %copy-done.21, bf16[1024,768]{1,0:T(8,128)(2,1)S(1)} %copy-done.23), custom_call_target="tpu_custom_call" | custom-call | flops 4831838208 | bytes 12582912 | tf_op jit(solution)/shard_map/weight_grad_tall/pallas_call | solution.py:370
  190.6 8.7 %weight_grad_wide.2 = (bf16[16,4,24,768]{3,2,1,0:T(8,128)(2,1)S(1)}, bf16[16,4,24,768]{3,2,1,0:T(8,128)(2,1)}) custom-call(s32[33]{0:T(128)S(1)} %dynamic-slice_bitcast_fusion.place_ref, bf16[1024,768]{1,0:T(8,128)(2,1)S(1)} %copy-done.22, bf16[1024,3072]{1,0:T(8,128)(2,1)S(1)} %copy-done.20), custom_call_target="tpu_custom_call" | custom-call | flops 4831838208 | bytes 12582912 | tf_op jit(solution)/shard_map/weight_grad_wide/pallas_call | solution.py:343
  218.0 14.1 %attend_backward.3 = (bf16[1024,256]{1,0:T(8,128)(2,1)S(1)}, bf16[1024,256]{1,0:T(8,128)(2,1)S(1)}, bf16[1024,256]{1,0:T(8,128)(2,1)S(1)}, bf16[16,3,24,256]{3,2...) custom-call(s32[1,8]{1,0:T(1,128)S(1)} %copy-done.17, ...), custom_call_target="tpu_custom_call" | custom-call | flops 7247757312 | bytes 16777216 | tf_op jit(solution)/shard_map/attend_backward/pallas_call | solution.py:513
  232.3 10.0 %collective-permute-done.15 = bf16[8,96,768]{2,1,0:T(8,128)(2,1)S(1)} collective-permute-done((bf16[8,96,768]{2,1,0:T(8,128)(2,1)S(1)}, bf16[8,96,768]{2,1,0:T(8,128)(2,1)S(1)}, u32[]{:S(2)}, u32[]{:S(2)}) %collective-permute-start.15) | collective-permute-done | bytes 1179680 | tf_op jit(solution)/shard_map/ppermute | solution.py:629
  244.7 14.4 %attend_backward.4 = (bf16[1024,256]{1,0:T(8,128)(2,1)S(1)}, bf16[1024,256]{1,0:T(8,128)(2,1)S(1)}, bf16[1024,256]{1,0:T(8,128)(2,1)S(1)}, bf16[16,3,24,256]{3,2...) custom-call(s32[1,8]{1,0:T(1,128)S(1)} %copy-done.17, ...), custom_call_target="tpu_custom_call" | custom-call | flops 7247757312 | bytes 16777216 | tf_op jit(solution)/shard_map/attend_backward/pallas_call | solution.py:513
  264.1 15.0 %attend_backward.5 = (bf16[1024,256]{1,0:T(8,128)(2,1)S(1)}, bf16[1024,256]{1,0:T(8,128)(2,1)S(1)}, bf16[1024,256]{1,0:T(8,128)(2,1)S(1)}, bf16[16,3,24,256]{3,2...) custom-call(s32[1,8]{1,0:T(1,128)S(1)} %copy-done.17, ...), custom_call_target="tpu_custom_call" | custom-call | flops 7247757312 | bytes 16777216 | tf_op jit(solution)/shard_map/attend_backward/pallas_call | solution.py:513
  289.7 6.0 %collective-permute-done.23 = bf16[8,152,256]{2,1,0:T(8,128)(2,1)S(1)} collective-permute-done((bf16[8,152,256]{2,1,0:T(8,128)(2,1)S(1)}, bf16[8,152,256]{2,1,0:T(8,128)(2,1)S(1)}, u32[]{:S(2)}, u32[]{:S(2)}) %collective-permute-start.23) | collective-permute-done | bytes 622624 | tf_op jit(solution)/shard_map/ppermute | solution.py:629
  296.0 5.7 %collective-permute-done.27 = bf16[2,200,768]{2,1,0:T(8,128)(2,1)S(1)} collective-permute-done((bf16[2,200,768]{2,1,0:T(8,128)(2,1)S(1)}, bf16[2,200,768]{2,1,0:T(8,128)(2,1)S(1)}, u32[]{:S(2)}, u32[]{:S(2)}) %collective-permute-start.27) | collective-permute-done | bytes 614432 | tf_op jit(solution)/shard_map/ppermute | solution.py:629
  304.7 5.7 %token_grad.1 = f32[1024,768]{1,0:T(8,128)} custom-call(f32[1024,768]{1,0:T(8,128)S(1)} %copy-done.3, bf16[1024,256]{1,0:T(8,128)(2,1)S(1)} %get-tuple-element.109.refs_0_, bf16[1024,256]{1,0:T(8,128)(2,1)S(1)} %get-tuple-element.118.refs_1_, bf16[1024,256]{1,0:T(8,128)(2,1)S(1)} %copy-done.9, bf16[1024,256]{1,0:T(8,128)(2,1)S(1)} %get-tuple-element.128.refs_3_, ...), custom_call_target="tpu_custom_call" | custom-call | flops 3623878656 | bytes 14680064 | tf_op jit(solution)/shard_map/token_grad/pallas_call | solution.py:572
  310.3 7.1 %collective-permute-done.28 = bf16[1,200,768]{2,1,0:T(8,128)(2,1)S(1)} collective-permute-done((bf16[1,200,768]{2,1,0:T(8,128)(2,1)S(1)}, bf16[1,200,768]{2,1,0:T(8,128)(2,1)S(1)}, u32[]{:S(2)}, u32[]{:S(2)}) %collective-permute-start.28) | collective-permute-done | bytes 307232 | tf_op jit(solution)/shard_map/ppermute | solution.py:629
  319.9 7.0 %collective-permute-done.25 = bf16[2,296,256]{2,1,0:T(8,128)(2,1)S(1)} collective-permute-done((bf16[2,296,256]{2,1,0:T(8,128)(2,1)S(1)}, bf16[2,296,256]{2,1,0:T(8,128)(2,1)S(1)}, u32[]{:S(2)}, u32[]{:S(2)}) %collective-permute-start.25) | collective-permute-done | bytes 303136 | tf_op jit(solution)/shard_map/ppermute | solution.py:629
  327.6 8.6 %collective-permute-done.26 = bf16[1,296,256]{2,1,0:T(8,128)(2,1)S(1)} collective-permute-done((bf16[1,296,256]{2,1,0:T(8,128)(2,1)S(1)}, bf16[1,296,256]{2,1,0:T(8,128)(2,1)S(1)}, u32[]{:S(2)}, u32[]{:S(2)}) %collective-permute-start.26) | collective-permute-done | bytes 151584 | tf_op jit(solution)/shard_map/ppermute | solution.py:629
  (263 shorter events, 79.6 us)
Async XLA Ops:
  7.2 126.5 %all-gather.2.cloned.1.call-start = ((), (), s32[]{:S(2)}) async-start(), calls=%async_computation | async-start | bytes 4866048 | tf_op jit(solution)/shard_map/all_gather | solution.py:703
  7.2 11.5 %collective-permute-start = (bf16[1,24,2304]{2,1,0:T(8,128)(2,1)}, bf16[1,24,2304]{2,1,0:T(8,128)(2,1)S(1)}, u32[]{:S(2)}, u32[]{:S(2)}) collective-permute-start(bf16[1,24,2304]{2,1,0:T(8,128)(2,1)} %bitcast.150), channel_id=1, source_target_pairs={{0,16},{1,17},{2,18},{3,19},{4,20},{5,21},{6,22},{7,23},{8,24},{9,... | collective-permute-start | bytes 331784 | tf_op jit(solution)/shard_map/ppermute | solution.py:629
  30.3 9.4 %collective-permute-start.3 = (bf16[4,24,2432]{2,1,0:T(8,128)(2,1)S(1)}, bf16[4,24,2432]{2,1,0:T(8,128)(2,1)S(1)}, u32[]{:S(2)}, u32[]{:S(2)}) collective-permute-start(bf16[4,24,2432]{2,1,0:T(8,128)(2,1)S(1)} %pad_maximum_fusion.12), channel_id=1, source_target_pairs={{0,4},{1,3},{2,6},{3,1},{4,0},{5,7},{6,2},{7,5},{8,12},{9,11},{10,... | collective-permute-start | bytes 1400840 | tf_op jit(solution)/shard_map/ppermute | solution.py:629
  39.8 13.6 %collective-permute-start.4 = (bf16[8,24,2432]{2,1,0:T(8,128)(2,1)S(1)}, bf16[8,24,2432]{2,1,0:T(8,128)(2,1)S(1)}, u32[]{:S(2)}, u32[]{:S(2)}) collective-permute-start(bf16[8,24,2432]{2,1,0:T(8,128)(2,1)S(1)} %pad_maximum_fusion.4), channel_id=1, source_target_pairs={{0,2},{1,5},{2,0},{3,7},{4,6},{5,1},{6,4},{7,3},{8,10},{9,13},{10,... | collective-permute-start | bytes 2801672 | tf_op jit(solution)/shard_map/ppermute | solution.py:629
  53.6 12.4 %collective-permute-start.6 = (bf16[16,24,2432]{2,1,0:T(8,128)(2,1)S(1)}, bf16[16,24,2432]{2,1,0:T(8,128)(2,1)}, u32[]{:S(2)}, u32[]{:S(2)}) collective-permute-start(bf16[16,24,2432]{2,1,0:T(8,128)(2,1)S(1)} %constant_dynamic-update-slice_fusion.2.near_ref), channel_id=1, source_target_pairs={{0,1},{1,0},{2,3},{3,2},{4,5},{5,4},{6,7},{7,6},{8,9},{9,8},{10,11... | collective-permute-start | bytes 5603336 | tf_op jit(solution)/shard_map/ppermute | solution.py:629
  53.7 12.1 %collective-permute-start.5 = (bf16[1,24,3840]{2,1,0:T(8,128)(2,1)S(1)}, bf16[1,24,3840]{2,1,0:T(8,128)(2,1)S(1)}, u32[]{:S(2)}, u32[]{:S(2)}) collective-permute-start(bf16[1,24,3840]{2,1,0:T(8,128)(2,1)S(1)} %maximum_bitcast_fusion), channel_id=1, source_target_pairs={{0,16},{1,17},{2,18},{3,19},{4,20},{5,21},{6,22},{7,23},{8,24},{9,... | collective-permute-start | bytes 552968 | tf_op jit(solution)/shard_map/ppermute | solution.py:629
  66.0 13.6 %collective-permute-start.7 = (bf16[2,24,3840]{2,1,0:T(8,128)(2,1)S(1)}, bf16[2,24,3840]{2,1,0:T(8,128)(2,1)S(1)}, u32[]{:S(2)}, u32[]{:S(2)}) collective-permute-start(bf16[2,24,3840]{2,1,0:T(8,128)(2,1)S(1)} %pad_maximum_fusion.13), channel_id=1, source_target_pairs={{0,8},{1,9},{2,10},{3,11},{4,12},{5,13},{6,14},{7,15},{8,0},{9,1},... | collective-permute-start | bytes 1105928 | tf_op jit(solution)/shard_map/ppermute | solution.py:629
  80.5 11.5 %collective-permute-start.8 = (bf16[4,24,3840]{2,1,0:T(8,128)(2,1)S(1)}, bf16[4,24,3840]{2,1,0:T(8,128)(2,1)S(1)}, u32[]{:S(2)}, u32[]{:S(2)}) collective-permute-start(bf16[4,24,3840]{2,1,0:T(8,128)(2,1)S(1)} %pad_maximum_fusion.5), channel_id=1, source_target_pairs={{0,4},{1,3},{2,6},{3,1},{4,0},{5,7},{6,2},{7,5},{8,12},{9,11},{10,... | collective-permute-start | bytes 2211848 | tf_op jit(solution)/shard_map/ppermute | solution.py:629
  93.0 27.8 %collective-permute-start.9 = (bf16[8,24,3840]{2,1,0:T(8,128)(2,1)S(1)}, bf16[8,24,3840]{2,1,0:T(8,128)(2,1)S(1)}, u32[]{:S(2)}, u32[]{:S(2)}) collective-permute-start(bf16[8,24,3840]{2,1,0:T(8,128)(2,1)S(1)} %pad_maximum_fusion.1), channel_id=1, source_target_pairs={{0,2},{1,5},{2,0},{3,7},{4,6},{5,1},{6,4},{7,3},{8,10},{9,13},{10,... | collective-permute-start | bytes 4423688 | tf_op jit(solution)/shard_map/ppermute | solution.py:629
  190.2 19.7 %collective-permute-start.12 = (bf16[16,96,768]{2,1,0:T(8,128)(2,1)}, bf16[16,96,768]{2,1,0:T(8,128)(2,1)}, u32[]{:S(2)}, u32[]{:S(2)}) collective-permute-start(bf16[16,96,768]{2,1,0:T(8,128)(2,1)} %get-tuple-element.113), channel_id=1, source_target_pairs={{0,1},{1,0},{2,3},{3,2},{4,5},{5,4},{6,7},{7,6},{8,9},{9,8},{10,11... | collective-permute-start | bytes 7077896 | tf_op jit(solution)/shard_map/ppermute | solution.py:629
  200.7 12.8 %collective-permute-start.11 = (bf16[16,96,768]{2,1,0:T(8,128)(2,1)}, bf16[16,96,768]{2,1,0:T(8,128)(2,1)}, u32[]{:S(2)}, u32[]{:S(2)}) collective-permute-start(bf16[16,96,768]{2,1,0:T(8,128)(2,1)} %bitcast.9), channel_id=1, source_target_pairs={{0,1},{1,0},{2,3},{3,2},{4,5},{5,4},{6,7},{7,6},{8,9},{9,8},{10,11... | collective-permute-start | bytes 7077896 | tf_op jit(solution)/shard_map/ppermute | solution.py:629
  202.9 7.0 %collective-permute-start.13 = (bf16[16,8,768]{2,1,0:T(8,128)(2,1)S(1)}, bf16[16,8,768]{2,1,0:T(8,128)(2,1)S(1)}, u32[]{:S(2)}, u32[]{:S(2)}) collective-permute-start(bf16[16,8,768]{2,1,0:T(8,128)(2,1)S(1)} %pad_slice_fusion.7), channel_id=1, source_target_pairs={{0,1},{1,0},{2,3},{3,2},{4,5},{5,4},{6,7},{7,6},{8,9},{9,8},{10,11... | collective-permute-start | bytes 589832 | tf_op jit(solution)/shard_map/ppermute | solution.py:629
  209.4 7.6 %collective-permute-start.17 = (bf16[16,72,256]{2,1,0:T(8,128)(2,1)S(1)}, bf16[16,72,256]{2,1,0:T(8,128)(2,1)S(1)}, u32[]{:S(2)}, u32[]{:S(2)}) collective-permute-start(bf16[16,72,256]{2,1,0:T(8,128)(2,1)S(1)} %bitcast.146), channel_id=1, source_target_pairs={{0,1},{1,0},{2,3},{3,2},{4,5},{5,4},{6,7},{7,6},{8,9},{9,8},{10,11... | collective-permute-start | bytes 1769480 | tf_op jit(solution)/shard_map/ppermute | solution.py:629
  212.4 30.3 %collective-permute-start.14 = (bf16[8,104,768]{2,1,0:T(8,128)(2,1)S(1)}, bf16[8,104,768]{2,1,0:T(8,128)(2,1)S(1)}, u32[]{:S(2)}, u32[]{:S(2)}) collective-permute-start(bf16[8,104,768]{2,1,0:T(8,128)(2,1)S(1)} %pad_maximum_fusion.2), channel_id=1, source_target_pairs={{0,2},{1,5},{2,0},{3,7},{4,6},{5,1},{6,4},{7,3},{8,10},{9,13},{10,... | collective-permute-start | bytes 3833864 | tf_op jit(solution)/shard_map/ppermute | solution.py:629
  216.1 26.2 %collective-permute-start.15 = (bf16[8,96,768]{2,1,0:T(8,128)(2,1)S(1)}, bf16[8,96,768]{2,1,0:T(8,128)(2,1)S(1)}, u32[]{:S(2)}, u32[]{:S(2)}) collective-permute-start(bf16[8,96,768]{2,1,0:T(8,128)(2,1)S(1)} %get-tuple-element.150), channel_id=1, source_target_pairs={{0,2},{1,5},{2,0},{3,7},{4,6},{5,1},{6,4},{7,3},{8,10},{9,13},{10,... | collective-permute-start | bytes 3538952 | tf_op jit(solution)/shard_map/ppermute | solution.py:629
  232.1 27.0 %collective-permute-start.18 = (bf16[16,72,256]{2,1,0:T(8,128)(2,1)S(1)}, bf16[16,72,256]{2,1,0:T(8,128)(2,1)S(1)}, u32[]{:S(2)}, u32[]{:S(2)}) collective-permute-start(bf16[16,72,256]{2,1,0:T(8,128)(2,1)S(1)} %bitcast.145), channel_id=1, source_target_pairs={{0,1},{1,0},{2,3},{3,2},{4,5},{5,4},{6,7},{7,6},{8,9},{9,8},{10,11... | collective-permute-start | bytes 1769480 | tf_op jit(solution)/shard_map/ppermute | solution.py:629
  243.1 19.0 %collective-permute-start.16 = (bf16[4,200,768]{2,1,0:T(8,128)(2,1)S(1)}, bf16[4,200,768]{2,1,0:T(8,128)(2,1)S(1)}, u32[]{:S(2)}, u32[]{:S(2)}) collective-permute-start(bf16[4,200,768]{2,1,0:T(8,128)(2,1)S(1)} %pad_maximum_fusion.3), channel_id=1, source_target_pairs={{0,4},{1,3},{2,6},{3,1},{4,0},{5,7},{6,2},{7,5},{8,12},{9,11},{10,... | collective-permute-start | bytes 3686408 | tf_op jit(solution)/shard_map/ppermute | solution.py:629
  260.2 28.0 %collective-permute-start.19 = (bf16[8,144,256]{2,1,0:T(8,128)(2,1)}, bf16[8,144,256]{2,1,0:T(8,128)(2,1)}, u32[]{:S(2)}, u32[]{:S(2)}) collective-permute-start(bf16[8,144,256]{2,1,0:T(8,128)(2,1)} %pad_maximum_fusion.11), channel_id=1, source_target_pairs={{0,2},{1,5},{2,0},{3,7},{4,6},{5,1},{6,4},{7,3},{8,10},{9,13},{10,... | collective-permute-start | bytes 1769480 | tf_op jit(solution)/shard_map/ppermute | solution.py:629
  285.4 10.3 %collective-permute-start.23 = (bf16[8,152,256]{2,1,0:T(8,128)(2,1)S(1)}, bf16[8,152,256]{2,1,0:T(8,128)(2,1)S(1)}, u32[]{:S(2)}, u32[]{:S(2)}) collective-permute-start(bf16[8,152,256]{2,1,0:T(8,128)(2,1)S(1)} %pad_maximum_fusion.8), channel_id=1, source_target_pairs={{0,2},{1,5},{2,0},{3,7},{4,6},{5,1},{6,4},{7,3},{8,10},{9,13},{10,... | collective-permute-start | bytes 1867784 | tf_op jit(solution)/shard_map/ppermute | solution.py:629
  285.5 16.2 %collective-permute-start.27 = (bf16[2,200,768]{2,1,0:T(8,128)(2,1)S(1)}, bf16[2,200,768]{2,1,0:T(8,128)(2,1)S(1)}, u32[]{:S(2)}, u32[]{:S(2)}) collective-permute-start(bf16[2,200,768]{2,1,0:T(8,128)(2,1)S(1)} %copy-done.54), channel_id=1, source_target_pairs={{0,8},{1,9},{2,10},{3,11},{4,12},{5,13},{6,14},{7,15},{8,0},{9,1},... | collective-permute-start | bytes 1843208 | tf_op jit(solution)/shard_map/ppermute | solution.py:629
  295.9 21.7 %collective-permute-start.24 = (bf16[4,296,256]{2,1,0:T(8,128)(2,1)S(1)}, bf16[4,296,256]{2,1,0:T(8,128)(2,1)S(1)}, u32[]{:S(2)}, u32[]{:S(2)}) collective-permute-start(bf16[4,296,256]{2,1,0:T(8,128)(2,1)S(1)} %pad_maximum_fusion.10), channel_id=1, source_target_pairs={{0,4},{1,3},{2,6},{3,1},{4,0},{5,7},{6,2},{7,5},{8,12},{9,11},{10,... | collective-permute-start | bytes 1818632 | tf_op jit(solution)/shard_map/ppermute | solution.py:629
  301.7 15.7 %collective-permute-start.28 = (bf16[1,200,768]{2,1,0:T(8,128)(2,1)S(1)}, bf16[1,200,768]{2,1,0:T(8,128)(2,1)S(1)}, u32[]{:S(2)}, u32[]{:S(2)}) collective-permute-start(bf16[1,200,768]{2,1,0:T(8,128)(2,1)S(1)} %add_convert_fusion.10), channel_id=1, source_target_pairs={{0,16},{1,17},{2,18},{3,19},{4,20},{5,21},{6,22},{7,23},{8,24},{9,... | collective-permute-start | bytes 921608 | tf_op jit(solution)/shard_map/ppermute | solution.py:629
  317.7 9.2 %collective-permute-start.25 = (bf16[2,296,256]{2,1,0:T(8,128)(2,1)S(1)}, bf16[2,296,256]{2,1,0:T(8,128)(2,1)S(1)}, u32[]{:S(2)}, u32[]{:S(2)}) collective-permute-start(bf16[2,296,256]{2,1,0:T(8,128)(2,1)S(1)} %get-tuple-element.156), channel_id=1, source_target_pairs={{0,8},{1,9},{2,10},{3,11},{4,12},{5,13},{6,14},{7,15},{8,0},{9,1},... | collective-permute-start | bytes 909320 | tf_op jit(solution)/shard_map/ppermute | solution.py:629
  326.9 9.2 %collective-permute-start.26 = (bf16[1,296,256]{2,1,0:T(8,128)(2,1)S(1)}, bf16[1,296,256]{2,1,0:T(8,128)(2,1)S(1)}, u32[]{:S(2)}, u32[]{:S(2)}) collective-permute-start(bf16[1,296,256]{2,1,0:T(8,128)(2,1)S(1)} %add_convert_fusion.16), channel_id=1, source_target_pairs={{0,16},{1,17},{2,18},{3,19},{4,20},{5,21},{6,22},{7,23},{8,24},{9,... | collective-permute-start | bytes 454664 | tf_op jit(solution)/shard_map/ppermute | solution.py:629
  (66 other events, 449.7 us)
Sparse Core Ops, SparseCore 0:
  53.8 72.9 all-gather.1

commit v3 on v2

--- a/solution.py
+++ b/solution.py
@@ -192,7 +192,7 @@
             pltpu.VMEM((8, FORWARD_TILE), f32),
             pltpu.VMEM((8, width), f32),
         ],
-        compiler_params=pltpu.CompilerParams(vmem_limit_bytes=44 << 20),
+        compiler_params=pltpu.CompilerParams(vmem_limit_bytes=60 << 20),
         cost_estimate=pl.CostEstimate(flops=12 * rows * width * width, bytes_accessed=12 << 20, transcendentals=0),
         name="attend_forward",
     )(lengths, tokens, full_qkv, full_qkv, full_qkv, full_qkv)
@@ -243,9 +243,12 @@
     hidden_low = hidden.astype(bf16)
     hl_ref[...] = hidden_low
     branch = jnp.zeros((rows, width), f32)
-    for f in range(hidden_units // FB):
-        part = slice(f * FB, f * FB + FB)
-        up = dot(hidden_low, wu_ref[:, part]) + bu_ref[:, part].astype(f32)
+    parts = [slice(f * FB, f * FB + FB) for f in range(hidden_units // FB)]
+    ahead = dot(hidden_low, wu_ref[:, parts[0]])
+    for f, part in enumerate(parts):
+        up = ahead + bu_ref[:, part].astype(f32)
+        if f + 1 < len(parts):
+            ahead = dot(hidden_low, wu_ref[:, parts[f + 1]])
         bell = jnp.exp(up * up * -0.5)
         t = 1.0 / (1.0 + (0.3275911 * math.sqrt(0.5)) * jnp.abs(up))
         poly = 0.5 * 1.061405429 * t - 0.5 * 1.453152027
@@ -268,9 +271,11 @@
     gb_ref[...] = grad_branch
     add_vec(2, grad_branch.astype(f32))
     grad_hidden = grad_two
-    for f in range(hidden_units // FB):
-        part = slice(f * FB, f * FB + FB)
-        grad_up = (dot(grad_branch, wd_ref[part, :], NT) * slope_ref[:, part]).astype(bf16)
+    ahead = dot(grad_branch, wd_ref[parts[0], :], NT)
+    for f, part in enumerate(parts):
+        grad_up = (ahead * slope_ref[:, part]).astype(bf16)
+        if f + 1 < len(parts):
+            ahead = dot(grad_branch, wd_ref[parts[f + 1], :], NT)
         gu_ref[:, part] = grad_up
         gbu_ref[:, part] += jnp.sum(grad_up.astype(f32), axis=0, keepdims=True)
         grad_hidden = grad_hidden + dot(grad_up, wu_ref[:, part], NT)
@@ -701,10 +706,11 @@
         next(first)
         next(second)
         full_down = lax.all_gather(w_down, "dp", axis=0, tiled=True)
-        hops = [first.send(None) for _ in range(5)]
-        far, near = hops[4]
+        hops = [first.send(None) for _ in range(4)]
+        behind = [second.send([hops[1][0]])[0]]
+        far, near = first.send([behind[0]])
         full_qkv = assemble(blocks_at, near, far).reshape(width, -1)
-        arrived = [second.send([hops[3][0]])[0], second.send([far])[0]]
+        behind.append(second.send([far])[0])
     else:
         place = jnp.arange(BLOCKS, dtype=jnp.int32) // 2
         place = jnp.append(place, 0)
@@ -718,13 +724,13 @@
     forward = []
     for g in range(width // COLS):
         held = tokens
-        if count == BLOCKS:
-            held = after(tokens, arrived[g])
-            if g:
-                arrived.append(second.send([forward[-1][3]])[0])
+        if count == BLOCKS and g:
+            held = after(tokens, behind[g], forward[-1][3], *[full_down][: g - 1])
         forward.append(attend_forward(g, lengths, held, full_qkv))
+        if count == BLOCKS and g < 2:
+            behind.append(second.send([forward[-1][3], *[full_down][:g]])[0])
     if count == BLOCKS:
-        far, near = second.send([part[3] for part in forward])
+        far, near = second.send([forward[-1][3]])
         full_up_out = assemble(blocks_at, near, far).reshape(width, -1)
     (
         output, grad_one, grad_attn, grad_mixed, hidden_low, grad_branch, mixed, active, grad_up,
@@ -735,7 +741,11 @@
     )
     part_down = weight_grad_tall(place, active, grad_branch)
     part_up = weight_grad_wide(place, after(hidden_low, part_down[0]), grad_up, width)
-    part_out = weight_grad_wide(place, after(mixed, part_up[0]), grad_attn, COLS)
+    held = after(mixed, part_up[0])
+    if count == BLOCKS:
+        down = fold(meet([part_down]))
+        held = after(held, down[0])
+    part_out = weight_grad_wide(place, held, grad_attn, COLS)
     milestones = []
 
     def backward(g):
@@ -766,23 +776,24 @@
             scattered(gvec[1]),
         )
 
-    def small_part(lines, width):
-        line = jnp.concatenate(
-            [
-                part.reshape(part.shape[0], BLOCKS, -1).transpose(1, 0, 2).reshape(BLOCKS, -1)
-                for part in lines
-            ],
-            axis=1,
-        )
-        line = jnp.pad(line.astype(bf16), ((0, 0), (0, width - line.shape[1])))
-        line = jnp.pad(line[blocks_at][:, None, :], ((0, 0), (0, 7), (0, 0)))
-        return line[: BLOCKS // 2], line[BLOCKS // 2 :]
+    def small_part(*all_lines):
+        rows = []
+        for lines in all_lines:
+            line = jnp.concatenate(
+                [
+                    part.reshape(part.shape[0], BLOCKS, -1).transpose(1, 0, 2).reshape(BLOCKS, -1)
+                    for part in lines
+                ],
+                axis=1,
+            )
+            rows.append(jnp.pad(line.astype(bf16), ((0, 0), (0, COLS - line.shape[1])))[:, None])
+        rows = jnp.concatenate(rows, axis=1)[blocks_at]
+        rows = jnp.pad(rows, ((0, 0), (0, 8 - rows.shape[1]), (0, 0)))
+        return rows[: BLOCKS // 2], rows[BLOCKS // 2 :]
 
     def rows_of(halves):
         return [half.reshape(half.shape[0], -1, half.shape[-1]) for half in halves]
 
-    small_mlp = small_part([gvec[:6], gbu], width)
-    down = fold(meet([part_down, small_mlp]))
     down_first = hop(down, X, Y)
     up_met = meet([rows_of(part_up)])
     out_met = meet([rows_of(part_out)])
@@ -801,14 +812,15 @@
     mlp = fold([hop(mlp, Z_LOW, Z_LOW)])
     early_first = hop(early, X, Y)
     gbias = jnp.concatenate([group[5] for group in groups], axis=1)
-    small_attn = small_part([gbias[:2]], COLS)
+    small_attn = small_part([gvec[:6], gbu], [gbias[:2]])
     late = fold(meet([rows_of(groups[1][3:5]), rows_of(groups[2][3:5]), small_attn]))
-    late_first = hop(late, X, Y)
+    late_first = hop((after(late[0], mlp[0]), late[1]), X, Y)
     grad_tokens = token_grad(
         grad_one, [group[s] for s in range(3) for group in groups], full_qkv
     )
     mlp = total(hop(mlp, Z_HIGH, Z_HIGH))
     attn = fold([early_first, late_first])
+    attn = after(attn[0], mlp), attn[1]
     attn = fold([hop(attn, Y, X)])
     attn = fold([hop(attn, Z_LOW, Z_LOW)])
     attn = total(hop(attn, Z_HIGH, Z_HIGH))
@@ -817,9 +829,11 @@
         return rows.reshape(-1, shard, width).transpose(1, 0, 2).reshape(shard, -1)
 
     tall = ratio * shard
-    line = mlp[tall]
-    attn = [attn[i * shard : i * shard + shard] for i in range(12)] + [attn[12 * shard]]
-    line_attn = attn[12]
+    attn = [attn[i * shard : i * shard + shard] for i in range(12)] + [
+        attn[12 * shard],
+        attn[12 * shard + 1],
+    ]
+    line, line_attn = attn[12:]
     grad_out_weight = jnp.concatenate(attn[:3], axis=1)
     grad_qkv = jnp.concatenate([attn[3 + 3 * g + s] for s in range(3) for g in range(3)], axis=1)
 
@@ -828,7 +842,7 @@
 
     return (
         output, grad_tokens, grad_qkv, grad_out_weight,
-        wide_of(mlp[tall + 8 :]), mlp[:tall],
+        wide_of(mlp[tall:]), mlp[:tall],
         piece(line_attn, 0), piece(line_attn, 1), piece(line, 5), piece(line, 3), piece(line, 4),
         line[6 * shard : 6 * shard + tall], piece(line, 2), piece(line, 0), piece(line, 1),
     )

time: 348 us -> 337 us (0.968)
  waiting for transfers between devices: 107 us -> 82.4 us
  other arithmetic: 18.4 us -> 25.3 us
  Pallas kernels: 149 us -> 155 us
    ppermute x29 -> x28, waiting for transfers between devices: 107 us -> 81.7 us  [exchange(): lax.ppermute(values, 'dp', [(i, i ^ (odd if i & CORE else even)) for i in...]
    pallas_call x3, Pallas kernels: 29.2 us -> 36.1 us  [attend_forward(): pl.pallas_call(functools.partial(attend_forward_kernel, group), grid=(1,)...]
    unnamed x132 -> x107, local copies, waits for them, and re-layouts: 17.4 us -> 13.8 us
    convert_element_type x16 -> x15, other arithmetic: 12.1 us -> 14.9 us  [added(): return (a.astype(f32) + b.astype(f32)).astype(bf16)]
    ppermute x29 -> x28, starting transfers between devices: 23.9 us -> 22.3 us  [exchange(): lax.ppermute(values, 'dp', [(i, i ^ (odd if i & CORE else even)) for i in...]
  transfers between devices with their start and end apart: 30 -> 29, of which waited for: 16 -> 14; matrix products, arithmetic and copies ran while one was open for 9% -> 12% of each run, Pallas kernels for 28% -> 30%
where the time goes in v3:
time: 337 us; the launch traced here: 332 us
  Pallas kernels  155 us (46%)
  waiting for transfers between devices  82.4 us (24%)
  local copies, waits for them, and re-layouts  32.4 us (10%)
  other arithmetic  25.3 us (8%)
  starting transfers between devices  22.3 us (7%)
  between operations  15.2 us (5%)
    ppermute x28, waiting for transfers between devices, exchange(): lax.ppermute(values, 'dp', [(i, i ^ (odd if i & CORE else even)) for i in...  81.7 us
    pallas_call x3, Pallas kernels, attend_backward(): pl.pallas_call(attend_backward_kernel, grid=(1,), in_specs=[pl.BlockSpec(...  43.3 us
    pallas_call x1, Pallas kernels, feed_forward(): pl.pallas_call(feed_forward_kernel, grid=(rows // TB,), in_specs=[pl.Bloc...  43.1 us
    pallas_call x3, Pallas kernels, attend_forward(): pl.pallas_call(functools.partial(attend_forward_kernel, group), grid=(1,)...  36.1 us
    ppermute x28, starting transfers between devices, exchange(): lax.ppermute(values, 'dp', [(i, i ^ (odd if i & CORE else even)) for i in...  22.3 us
    convert_element_type x15, other arithmetic, added(): return (a.astype(f32) + b.astype(f32)).astype(bf16)  14.9 us
    unnamed x107, local copies, waits for them, and re-layouts  13.8 us
    pallas_call x2, Pallas kernels, weight_grad_wide(): pl.pallas_call(weight_grad_kernel, grid=(groups,), in_specs=[pl.BlockSpec...  12.2 us
  transfers between devices with their start and end apart: 29, of which 14 were waited for; matrix products, arithmetic and copies ran while one was open for 12% of the time, Pallas kernels for 30%

profile of v3, /device:TPU:0, one launch (start us, length us, event | category | flops | bytes accessed | tf_op | source)
XLA Modules:
  0.0 332.4 jit_solution(6064571030723103244)
XLA Ops:
  7.9 4.1 %collective-permute-start = (bf16[1,24,2304]{2,1,0:T(8,128)(2,1)}, bf16[1,24,2304]{2,1,0:T(8,128)(2,1)S(1)}, u32[]{:S(2)}, u32[]{:S(2)}) collective-permute-start(bf16[1,24,2304]{2,1,0:T(8,128)(2,1)} %bitcast.147), channel_id=1, source_target_pairs={{0,16},{1,17},{2,18},{3,19},{4,20},{5,21},{6,22},{7,23},{8,24},{9,... | collective-permute-start | bytes 331784 | tf_op jit(solution)/shard_map/ppermute | solution.py:634
  12.0 5.4 %concatenate.83 = bf16[192]{0:T(256)(128)(2,1)S(1)} concatenate(bf16[24]{0:T(256)(128)(2,1)} %param.25, bf16[24]{0:T(256)(128)(2,1)} %param.26, bf16[24]{0:T(256)(128)(2,1)} %param.27, bf16[24]{0:T(256)(128)(2,1)} %param.28, bf16[24]{0:T(256)(128)(2,1)} %param.29, bf16[24]{0:T(256)(128)(2,1)} %param.31, bf16[24]{0:T(256)(128)(2,1)} %param.32, bf16[24]{0:T(256)(128)(2,1)} %param.33), dimensions={0} | concatenate | bytes 768 | tf_op jit(solution)/shard_map/concatenate | solution.py:694
  19.5 3.6 %collective-permute-done.1 = bf16[1,24,128]{2,1,0:T(8,128)(2,1)S(1)} collective-permute-done((bf16[1,24,128]{2,1,0:T(8,128)(2,1)S(1)}, bf16[1,24,128]{2,1,0:T(8,128)(2,1)S(1)}, u32[]{:S(2)}, u32[]{:S(2)}) %collective-permute-start.1) | collective-permute-done | bytes 6176 | tf_op jit(solution)/shard_map/ppermute | solution.py:634
  25.6 6.8 %collective-permute-done.2 = bf16[2,24,2432]{2,1,0:T(8,128)(2,1)S(1)} collective-permute-done((bf16[2,24,2432]{2,1,0:T(8,128)(2,1)S(1)}, bf16[2,24,2432]{2,1,0:T(8,128)(2,1)S(1)}, u32[]{:S(2)}, u32[]{:S(2)}) %collective-permute-start.2) | collective-permute-done | bytes 233504 | tf_op jit(solution)/shard_map/ppermute | solution.py:634
  35.0 9.8 %collective-permute-done.3 = bf16[4,24,2432]{2,1,0:T(8,128)(2,1)S(1)} collective-permute-done((bf16[4,24,2432]{2,1,0:T(8,128)(2,1)S(1)}, bf16[4,24,2432]{2,1,0:T(8,128)(2,1)S(1)}, u32[]{:S(2)}, u32[]{:S(2)}) %collective-permute-start.3) | collective-permute-done | bytes 466976 | tf_op jit(solution)/shard_map/ppermute | solution.py:634
  47.1 11.4 %collective-permute-done.4 = bf16[8,24,2432]{2,1,0:T(8,128)(2,1)S(1)} collective-permute-done((bf16[8,24,2432]{2,1,0:T(8,128)(2,1)S(1)}, bf16[8,24,2432]{2,1,0:T(8,128)(2,1)S(1)}, u32[]{:S(2)}, u32[]{:S(2)}) %collective-permute-start.4) | collective-permute-done | bytes 933920 | tf_op jit(solution)/shard_map/ppermute | solution.py:634
  66.7 12.2 %attend_forward.3 = (bf16[1024,256]{1,0:T(8,128)(2,1)}, bf16[1024,256]{1,0:T(8,128)(2,1)}, bf16[1024,256]{1,0:T(8,128)(2,1)}, bf16[1024,256]{1,0:T(8,128)(2,1)}, f32[1,8,1024]{2,1,0:T(8,128)}) custom-call(s32[1,8]{1,0:T(1,128)} %len_ref.13, bf16[1024,768]{1,0:T(8,128)(2,1)} %x_ref.11, bf16[768,2432]{1,0:T(8,128)(2,1)} %bitcast.127, ...), custom_call_target="tpu_custom_call" | custom-call | flops 7247757312 | bytes 12582912 | tf_op jit(solution)/shard_map/attend_forward/pallas_call | solution.py:172
  85.0 12.0 %attend_forward.4 = (bf16[1024,256]{1,0:T(8,128)(2,1)}, bf16[1024,256]{1,0:T(8,128)(2,1)}, bf16[1024,256]{1,0:T(8,128)(2,1)}, bf16[1024,256]{1,0:T(8,128)(2,1)}, f32[1,8,1024]{2,1,0:T(8,128)}) custom-call(s32[1,8]{1,0:T(1,128)} %len_ref.13, bf16[1024,768]{1,0:T(8,128)(2,1)} %x_ref.11, bf16[768,2432]{1,0:T(8,128)(2,1)} %bitcast.131, ...), custom_call_target="tpu_custom_call" | custom-call | flops 7247757312 | bytes 12582912 | tf_op jit(solution)/shard_map/attend_forward/pallas_call | solution.py:172
  98.9 12.0 %attend_forward.5 = (bf16[1024,256]{1,0:T(8,128)(2,1)}, bf16[1024,256]{1,0:T(8,128)(2,1)}, bf16[1024,256]{1,0:T(8,128)(2,1)}, bf16[1024,256]{1,0:T(8,128)(2,1)}, f32[1,8,1024]{2,1,0:T(8,128)}) custom-call(s32[1,8]{1,0:T(1,128)} %len_ref.13, bf16[1024,768]{1,0:T(8,128)(2,1)} %x_ref.11, bf16[768,2432]{1,0:T(8,128)(2,1)} %bitcast.135, ...), custom_call_target="tpu_custom_call" | custom-call | flops 7247757312 | bytes 12582912 | tf_op jit(solution)/shard_map/attend_forward/pallas_call | solution.py:172
  110.9 5.8 %collective-permute-done.9 = bf16[8,24,3840]{2,1,0:T(8,128)(2,1)} collective-permute-done((bf16[8,24,3840]{2,1,0:T(8,128)(2,1)S(1)}, bf16[8,24,3840]{2,1,0:T(8,128)(2,1)}, u32[]{:S(2)}, u32[]{:S(2)}) %collective-permute-start.9) | collective-permute-done | bytes 1474592 | tf_op jit(solution)/shard_map/ppermute | solution.py:634
  124.4 4.1 %assemble.3 = bf16[32,24,3840]{2,1,0:T(8,128)(2,1)S(1)} custom-call(s32[32]{0:T(128)S(1)} %fusion.22.blocks_ref, bf16[16,24,3840]{2,1,0:T(8,128)(2,1)S(1)} %pad_maximum_fusion.near_ref, bf16[16,24,3840]{2,1,0:T(8,128)(2,1)} %collective-permute-done.10.far_ref), custom_call_target="tpu_custom_call" | custom-call | bytes 11796480 | tf_op jit(solution)/shard_map/assemble/pallas_call | solution.py:606
  131.0 43.1 %feed_forward.1 = (bf16[1024,768]{1,0:T(8,128)(2,1)}, f32[1024,768]{1,0:T(8,128)}, bf16[1024,768]{1,0:T(8,128)(2,1)}, bf16[1024,768]{1,0:T(8,128)(2,1)}, bf16[10...) custom-call(s32[1,8]{1,0:T(1,128)} %len_ref.13, ...), custom_call_target="tpu_custom_call" | custom-call | flops 21743271936 | bytes 41943040 | tf_op jit(solution)/shard_map/feed_forward/pallas_call | solution.py:306
  178.3 8.5 %weight_grad_tall.1 = (bf16[16,96,768]{2,1,0:T(8,128)(2,1)S(1)}, bf16[16,96,768]{2,1,0:T(8,128)(2,1)}) custom-call(s32[33]{0:T(128)S(1)} %dynamic-slice_bitcast_fusion.place_ref, bf16[1024,3072]{1,0:T(8,128)(2,1)S(1)} %copy-done.18, bf16[1024,768]{1,0:T(8,128)(2,1)S(1)} %copy-done.20), custom_call_target="tpu_custom_call" | custom-call | flops 4831838208 | bytes 12582912 | tf_op jit(solution)/shard_map/weight_grad_tall/pallas_call | solution.py:375
  186.9 8.9 %weight_grad_wide.2 = (bf16[16,4,24,768]{3,2,1,0:T(8,128)(2,1)S(1)}, bf16[16,4,24,768]{3,2,1,0:T(8,128)(2,1)}) custom-call(s32[33]{0:T(128)S(1)} %dynamic-slice_bitcast_fusion.place_ref, bf16[1024,768]{1,0:T(8,128)(2,1)S(1)} %copy-done.19, bf16[1024,3072]{1,0:T(8,128)(2,1)S(1)} %copy-done.17), custom_call_target="tpu_custom_call" | custom-call | flops 4831838208 | bytes 12582912 | tf_op jit(solution)/shard_map/weight_grad_wide/pallas_call | solution.py:348
  206.2 3.5 %fusion = (bf16[8,96,768]{2,1,0:T(8,128)(2,1)S(1)}, bf16[8,96,768]{2,1,0:T(8,128)(2,1)}) fusion(bf16[16,96,768]{2,1,0:T(8,128)(2,1)} %collective-permute-done.12, bf16[8,4,24,768]{3,2,1,0:T(8,128)(2,1)S(1)} %get-tuple-element.155, bf16[8,4,24,768]{3,2,1,0:T(8,128)(2,1)S(1)} %get-tuple-element.156), kind=kLoop, calls=%fused_computation.3 | loop fusion | flops 4718592 | bytes 7077888 | tf_op jit(solution)/shard_map/convert_element_type | solution.py:640
  213.6 14.1 %attend_backward.3 = (bf16[1024,256]{1,0:T(8,128)(2,1)S(1)}, bf16[1024,256]{1,0:T(8,128)(2,1)S(1)}, bf16[1024,256]{1,0:T(8,128)(2,1)S(1)}, bf16[16,3,24,256]{3,2...) custom-call(s32[1,8]{1,0:T(1,128)S(1)} %copy-done.14, ...), custom_call_target="tpu_custom_call" | custom-call | flops 7247757312 | bytes 16777216 | tf_op jit(solution)/shard_map/attend_backward/pallas_call | solution.py:518
  228.5 5.2 %collective-permute-done.14 = bf16[8,96,768]{2,1,0:T(8,128)(2,1)S(1)} collective-permute-done((bf16[8,96,768]{2,1,0:T(8,128)(2,1)}, bf16[8,96,768]{2,1,0:T(8,128)(2,1)S(1)}, u32[]{:S(2)}, u32[]{:S(2)}) %collective-permute-start.14) | collective-permute-done | bytes 1179680 | tf_op jit(solution)/shard_map/ppermute | solution.py:634
  235.4 14.2 %attend_backward.4 = (bf16[1024,256]{1,0:T(8,128)(2,1)S(1)}, bf16[1024,256]{1,0:T(8,128)(2,1)S(1)}, bf16[1024,256]{1,0:T(8,128)(2,1)S(1)}, bf16[16,3,24,256]{3,2...) custom-call(s32[1,8]{1,0:T(1,128)S(1)} %copy-done.14, ...), custom_call_target="tpu_custom_call" | custom-call | flops 7247757312 | bytes 16777216 | tf_op jit(solution)/shard_map/attend_backward/pallas_call | solution.py:518
  255.3 15.0 %attend_backward.5 = (bf16[1024,256]{1,0:T(8,128)(2,1)S(1)}, bf16[1024,256]{1,0:T(8,128)(2,1)S(1)}, bf16[1024,256]{1,0:T(8,128)(2,1)S(1)}, bf16[16,3,24,256]{3,2...) custom-call(s32[1,8]{1,0:T(1,128)S(1)} %copy-done.14, ...), custom_call_target="tpu_custom_call" | custom-call | flops 7247757312 | bytes 16777216 | tf_op jit(solution)/shard_map/attend_backward/pallas_call | solution.py:518
  282.9 8.8 %collective-permute-done.23 = bf16[8,152,256]{2,1,0:T(8,128)(2,1)S(1)} collective-permute-done((bf16[8,152,256]{2,1,0:T(8,128)(2,1)S(1)}, bf16[8,152,256]{2,1,0:T(8,128)(2,1)S(1)}, u32[]{:S(2)}, u32[]{:S(2)}) %collective-permute-start.23) | collective-permute-done | bytes 622624 | tf_op jit(solution)/shard_map/ppermute | solution.py:634
  293.3 8.8 %collective-permute-done.24 = bf16[4,296,256]{2,1,0:T(8,128)(2,1)S(1)} collective-permute-done((bf16[4,296,256]{2,1,0:T(8,128)(2,1)S(1)}, bf16[4,296,256]{2,1,0:T(8,128)(2,1)S(1)}, u32[]{:S(2)}, u32[]{:S(2)}) %collective-permute-start.24) | collective-permute-done | bytes 606240 | tf_op jit(solution)/shard_map/ppermute | solution.py:634
  303.3 5.6 %token_grad.1 = f32[1024,768]{1,0:T(8,128)} custom-call(f32[1024,768]{1,0:T(8,128)S(1)} %copy-done.3, bf16[1024,256]{1,0:T(8,128)(2,1)S(1)} %get-tuple-element.113.refs_0_, bf16[1024,256]{1,0:T(8,128)(2,1)S(1)} %get-tuple-element.119.refs_1_, bf16[1024,256]{1,0:T(8,128)(2,1)S(1)} %copy-done.8, bf16[1024,256]{1,0:T(8,128)(2,1)S(1)} %get-tuple-element.129.refs_3_, ...), custom_call_target="tpu_custom_call" | custom-call | flops 3623878656 | bytes 14680064 | tf_op jit(solution)/shard_map/token_grad/pallas_call | solution.py:577
  310.1 4.1 %collective-permute-done.25 = bf16[2,296,256]{2,1,0:T(8,128)(2,1)S(1)} collective-permute-done((bf16[2,296,256]{2,1,0:T(8,128)(2,1)S(1)}, bf16[2,296,256]{2,1,0:T(8,128)(2,1)S(1)}, u32[]{:S(2)}, u32[]{:S(2)}) %collective-permute-start.25) | collective-permute-done | bytes 303136 | tf_op jit(solution)/shard_map/ppermute | solution.py:634
  315.8 7.5 %collective-permute-done.26 = bf16[1,296,256]{2,1,0:T(8,128)(2,1)S(1)} collective-permute-done((bf16[1,296,256]{2,1,0:T(8,128)(2,1)S(1)}, bf16[1,296,256]{2,1,0:T(8,128)(2,1)S(1)}, u32[]{:S(2)}, u32[]{:S(2)}) %collective-permute-start.26) | collective-permute-done | bytes 151584 | tf_op jit(solution)/shard_map/ppermute | solution.py:634
  (230 shorter events, 82.7 us)
Async XLA Ops:
  7.2 90.0 %all-gather.2.cloned.1.call-start = ((), (), s32[]{:S(2)}) async-start(), calls=%async_computation | async-start | bytes 4866048 | tf_op jit(solution)/shard_map/all_gather | solution.py:708
  7.9 11.5 %collective-permute-start = (bf16[1,24,2304]{2,1,0:T(8,128)(2,1)}, bf16[1,24,2304]{2,1,0:T(8,128)(2,1)S(1)}, u32[]{:S(2)}, u32[]{:S(2)}) collective-permute-start(bf16[1,24,2304]{2,1,0:T(8,128)(2,1)} %bitcast.147), channel_id=1, source_target_pairs={{0,16},{1,17},{2,18},{3,19},{4,20},{5,21},{6,22},{7,23},{8,24},{9,... | collective-permute-start | bytes 331784 | tf_op jit(solution)/shard_map/ppermute | solution.py:634
  24.0 8.5 %collective-permute-start.2 = (bf16[2,24,2432]{2,1,0:T(8,128)(2,1)S(1)}, bf16[2,24,2432]{2,1,0:T(8,128)(2,1)S(1)}, u32[]{:S(2)}, u32[]{:S(2)}) collective-permute-start(bf16[2,24,2432]{2,1,0:T(8,128)(2,1)S(1)} %pad_maximum_fusion.14), channel_id=1, source_target_pairs={{0,8},{1,9},{2,10},{3,11},{4,12},{5,13},{6,14},{7,15},{8,0},{9,1},... | collective-permute-start | bytes 700424 | tf_op jit(solution)/shard_map/ppermute | solution.py:634
  33.4 11.4 %collective-permute-start.3 = (bf16[4,24,2432]{2,1,0:T(8,128)(2,1)S(1)}, bf16[4,24,2432]{2,1,0:T(8,128)(2,1)S(1)}, u32[]{:S(2)}, u32[]{:S(2)}) collective-permute-start(bf16[4,24,2432]{2,1,0:T(8,128)(2,1)S(1)} %pad_maximum_fusion.10), channel_id=1, source_target_pairs={{0,4},{1,3},{2,6},{3,1},{4,0},{5,7},{6,2},{7,5},{8,12},{9,11},{10,... | collective-permute-start | bytes 1400840 | tf_op jit(solution)/shard_map/ppermute | solution.py:634
  44.8 13.6 %collective-permute-start.4 = (bf16[8,24,2432]{2,1,0:T(8,128)(2,1)S(1)}, bf16[8,24,2432]{2,1,0:T(8,128)(2,1)S(1)}, u32[]{:S(2)}, u32[]{:S(2)}) collective-permute-start(bf16[8,24,2432]{2,1,0:T(8,128)(2,1)S(1)} %pad_maximum_fusion.3), channel_id=1, source_target_pairs={{0,2},{1,5},{2,0},{3,7},{4,6},{5,1},{6,4},{7,3},{8,10},{9,13},{10,... | collective-permute-start | bytes 2801672 | tf_op jit(solution)/shard_map/ppermute | solution.py:634
  46.9 11.7 %collective-permute-start.5 = (bf16[1,24,3840]{2,1,0:T(8,128)(2,1)S(1)}, bf16[1,24,3840]{2,1,0:T(8,128)(2,1)S(1)}, u32[]{:S(2)}, u32[]{:S(2)}) collective-permute-start(bf16[1,24,3840]{2,1,0:T(8,128)(2,1)S(1)} %maximum_bitcast_fusion), channel_id=1, source_target_pairs={{0,16},{1,17},{2,18},{3,19},{4,20},{5,21},{6,22},{7,23},{8,24},{9,... | collective-permute-start | bytes 552968 | tf_op jit(solution)/shard_map/ppermute | solution.py:634
  62.6 19.2 %collective-permute-start.7 = (bf16[2,24,3840]{2,1,0:T(8,128)(2,1)S(1)}, bf16[2,24,3840]{2,1,0:T(8,128)(2,1)S(1)}, u32[]{:S(2)}, u32[]{:S(2)}) collective-permute-start(bf16[2,24,3840]{2,1,0:T(8,128)(2,1)S(1)} %pad_maximum_fusion.11), channel_id=1, source_target_pairs={{0,8},{1,9},{2,10},{3,11},{4,12},{5,13},{6,14},{7,15},{8,0},{9,1},... | collective-permute-start | bytes 1105928 | tf_op jit(solution)/shard_map/ppermute | solution.py:634
  81.9 15.1 %collective-permute-start.8 = (bf16[4,24,3840]{2,1,0:T(8,128)(2,1)S(1)}, bf16[4,24,3840]{2,1,0:T(8,128)(2,1)S(1)}, u32[]{:S(2)}, u32[]{:S(2)}) collective-permute-start(bf16[4,24,3840]{2,1,0:T(8,128)(2,1)S(1)} %pad_maximum_fusion.4), channel_id=1, source_target_pairs={{0,4},{1,3},{2,6},{3,1},{4,0},{5,7},{6,2},{7,5},{8,12},{9,11},{10,... | collective-permute-start | bytes 2211848 | tf_op jit(solution)/shard_map/ppermute | solution.py:634
  97.2 19.5 %collective-permute-start.9 = (bf16[8,24,3840]{2,1,0:T(8,128)(2,1)S(1)}, bf16[8,24,3840]{2,1,0:T(8,128)(2,1)}, u32[]{:S(2)}, u32[]{:S(2)}) collective-permute-start(bf16[8,24,3840]{2,1,0:T(8,128)(2,1)S(1)} %pad_maximum_fusion.1), channel_id=1, source_target_pairs={{0,2},{1,5},{2,0},{3,7},{4,6},{5,1},{6,4},{7,3},{8,10},{9,13},{10,... | collective-permute-start | bytes 4423688 | tf_op jit(solution)/shard_map/ppermute | solution.py:634
  186.8 14.5 %collective-permute-start.11 = (bf16[16,96,768]{2,1,0:T(8,128)(2,1)}, bf16[16,96,768]{2,1,0:T(8,128)(2,1)}, u32[]{:S(2)}, u32[]{:S(2)}) collective-permute-start(bf16[16,96,768]{2,1,0:T(8,128)(2,1)} %get-tuple-element.106), channel_id=1, source_target_pairs={{0,1},{1,0},{2,3},{3,2},{4,5},{5,4},{6,7},{7,6},{8,9},{9,8},{10,11... | collective-permute-start | bytes 7077896 | tf_op jit(solution)/shard_map/ppermute | solution.py:634
  197.2 9.0 %collective-permute-start.12 = (bf16[16,96,768]{2,1,0:T(8,128)(2,1)}, bf16[16,96,768]{2,1,0:T(8,128)(2,1)}, u32[]{:S(2)}, u32[]{:S(2)}) collective-permute-start(bf16[16,96,768]{2,1,0:T(8,128)(2,1)} %bitcast.9), channel_id=1, source_target_pairs={{0,1},{1,0},{2,3},{3,2},{4,5},{5,4},{6,7},{7,6},{8,9},{9,8},{10,11... | collective-permute-start | bytes 7077896 | tf_op jit(solution)/shard_map/ppermute | solution.py:634
  204.6 23.6 %collective-permute-start.13 = (bf16[8,96,768]{2,1,0:T(8,128)(2,1)}, bf16[8,96,768]{2,1,0:T(8,128)(2,1)S(1)}, u32[]{:S(2)}, u32[]{:S(2)}) collective-permute-start(bf16[8,96,768]{2,1,0:T(8,128)(2,1)} %get-tuple-element.146), channel_id=1, source_target_pairs={{0,2},{1,5},{2,0},{3,7},{4,6},{5,1},{6,4},{7,3},{8,10},{9,13},{10,... | collective-permute-start | bytes 3538952 | tf_op jit(solution)/shard_map/ppermute | solution.py:634
  209.7 23.9 %collective-permute-start.14 = (bf16[8,96,768]{2,1,0:T(8,128)(2,1)}, bf16[8,96,768]{2,1,0:T(8,128)(2,1)S(1)}, u32[]{:S(2)}, u32[]{:S(2)}) collective-permute-start(bf16[8,96,768]{2,1,0:T(8,128)(2,1)} %get-tuple-element.154), channel_id=1, source_target_pairs={{0,2},{1,5},{2,0},{3,7},{4,6},{5,1},{6,4},{7,3},{8,10},{9,13},{10,... | collective-permute-start | bytes 3538952 | tf_op jit(solution)/shard_map/ppermute | solution.py:634
  213.5 14.4 %collective-permute-start.16 = (bf16[16,72,256]{2,1,0:T(8,128)(2,1)S(1)}, bf16[16,72,256]{2,1,0:T(8,128)(2,1)S(1)}, u32[]{:S(2)}, u32[]{:S(2)}) collective-permute-start(bf16[16,72,256]{2,1,0:T(8,128)(2,1)S(1)} %bitcast.146), channel_id=1, source_target_pairs={{0,1},{1,0},{2,3},{3,2},{4,5},{5,4},{6,7},{7,6},{8,9},{9,8},{10,11... | collective-permute-start | bytes 1769480 | tf_op jit(solution)/shard_map/ppermute | solution.py:634
  227.7 22.0 %collective-permute-start.17 = (bf16[16,72,256]{2,1,0:T(8,128)(2,1)S(1)}, bf16[16,72,256]{2,1,0:T(8,128)(2,1)S(1)}, u32[]{:S(2)}, u32[]{:S(2)}) collective-permute-start(bf16[16,72,256]{2,1,0:T(8,128)(2,1)S(1)} %bitcast.144), channel_id=1, source_target_pairs={{0,1},{1,0},{2,3},{3,2},{4,5},{5,4},{6,7},{7,6},{8,9},{9,8},{10,11... | collective-permute-start | bytes 1769480 | tf_op jit(solution)/shard_map/ppermute | solution.py:634
  234.0 18.7 %collective-permute-start.15 = (bf16[4,192,768]{2,1,0:T(8,128)(2,1)S(1)}, bf16[4,192,768]{2,1,0:T(8,128)(2,1)S(1)}, u32[]{:S(2)}, u32[]{:S(2)}) collective-permute-start(bf16[4,192,768]{2,1,0:T(8,128)(2,1)S(1)} %pad_maximum_fusion.2), channel_id=1, source_target_pairs={{0,4},{1,3},{2,6},{3,1},{4,0},{5,7},{6,2},{7,5},{8,12},{9,11},{10,... | collective-permute-start | bytes 3538952 | tf_op jit(solution)/shard_map/ppermute | solution.py:634
  251.5 29.9 %collective-permute-start.18 = (bf16[8,144,256]{2,1,0:T(8,128)(2,1)}, bf16[8,144,256]{2,1,0:T(8,128)(2,1)}, u32[]{:S(2)}, u32[]{:S(2)}) collective-permute-start(bf16[8,144,256]{2,1,0:T(8,128)(2,1)} %pad_maximum_fusion.9), channel_id=1, source_target_pairs={{0,2},{1,5},{2,0},{3,7},{4,6},{5,1},{6,4},{7,3},{8,10},{9,13},{10,... | collective-permute-start | bytes 1769480 | tf_op jit(solution)/shard_map/ppermute | solution.py:634
  254.1 26.1 %collective-permute-start.22 = (bf16[2,192,768]{2,1,0:T(8,128)(2,1)}, bf16[2,192,768]{2,1,0:T(8,128)(2,1)}, u32[]{:S(2)}, u32[]{:S(2)}) collective-permute-start(bf16[2,192,768]{2,1,0:T(8,128)(2,1)} %get-tuple-element.148), channel_id=1, source_target_pairs={{0,8},{1,9},{2,10},{3,11},{4,12},{5,13},{6,14},{7,15},{8,0},{9,1},... | collective-permute-start | bytes 1769480 | tf_op jit(solution)/shard_map/ppermute | solution.py:634
  272.7 6.2 %collective-permute-start.20 = (bf16[16,72,256]{2,1,0:T(8,128)(2,1)}, bf16[16,72,256]{2,1,0:T(8,128)(2,1)}, u32[]{:S(2)}, u32[]{:S(2)}) collective-permute-start(bf16[16,72,256]{2,1,0:T(8,128)(2,1)} %bitcast.20), channel_id=1, source_target_pairs={{0,1},{1,0},{2,3},{3,2},{4,5},{5,4},{6,7},{7,6},{8,9},{9,8},{10,11... | collective-permute-start | bytes 1769480 | tf_op jit(solution)/shard_map/ppermute | solution.py:634
  281.4 10.3 %collective-permute-start.23 = (bf16[8,152,256]{2,1,0:T(8,128)(2,1)S(1)}, bf16[8,152,256]{2,1,0:T(8,128)(2,1)S(1)}, u32[]{:S(2)}, u32[]{:S(2)}) collective-permute-start(bf16[8,152,256]{2,1,0:T(8,128)(2,1)S(1)} %pad_maximum_fusion.6), channel_id=1, source_target_pairs={{0,2},{1,5},{2,0},{3,7},{4,6},{5,1},{6,4},{7,3},{8,10},{9,13},{10,... | collective-permute-start | bytes 1867784 | tf_op jit(solution)/shard_map/ppermute | solution.py:634
  291.9 10.1 %collective-permute-start.24 = (bf16[4,296,256]{2,1,0:T(8,128)(2,1)S(1)}, bf16[4,296,256]{2,1,0:T(8,128)(2,1)S(1)}, u32[]{:S(2)}, u32[]{:S(2)}) collective-permute-start(bf16[4,296,256]{2,1,0:T(8,128)(2,1)S(1)} %pad_maximum_fusion.7), channel_id=1, source_target_pairs={{0,4},{1,3},{2,6},{3,1},{4,0},{5,7},{6,2},{7,5},{8,12},{9,11},{10,... | collective-permute-start | bytes 1818632 | tf_op jit(solution)/shard_map/ppermute | solution.py:634
  293.3 15.7 %collective-permute-start.27 = (bf16[1,192,768]{2,1,0:T(8,128)(2,1)S(1)}, bf16[1,192,768]{2,1,0:T(8,128)(2,1)S(1)}, u32[]{:S(2)}, u32[]{:S(2)}) collective-permute-start(bf16[1,192,768]{2,1,0:T(8,128)(2,1)S(1)} %add_convert_fusion.14), channel_id=1, source_target_pairs={{0,16},{1,17},{2,18},{3,19},{4,20},{5,21},{6,22},{7,23},{8,24},{9,... | collective-permute-start | bytes 884744 | tf_op jit(solution)/shard_map/ppermute | solution.py:634
  302.2 12.0 %collective-permute-start.25 = (bf16[2,296,256]{2,1,0:T(8,128)(2,1)S(1)}, bf16[2,296,256]{2,1,0:T(8,128)(2,1)S(1)}, u32[]{:S(2)}, u32[]{:S(2)}) collective-permute-start(bf16[2,296,256]{2,1,0:T(8,128)(2,1)S(1)} %get-tuple-element.160), channel_id=1, source_target_pairs={{0,8},{1,9},{2,10},{3,11},{4,12},{5,13},{6,14},{7,15},{8,0},{9,1},... | collective-permute-start | bytes 909320 | tf_op jit(solution)/shard_map/ppermute | solution.py:634
  314.2 9.1 %collective-permute-start.26 = (bf16[1,296,256]{2,1,0:T(8,128)(2,1)S(1)}, bf16[1,296,256]{2,1,0:T(8,128)(2,1)S(1)}, u32[]{:S(2)}, u32[]{:S(2)}) collective-permute-start(bf16[1,296,256]{2,1,0:T(8,128)(2,1)S(1)} %add_convert_fusion.16), channel_id=1, source_target_pairs={{0,16},{1,17},{2,18},{3,19},{4,20},{5,21},{6,22},{7,23},{8,24},{9,... | collective-permute-start | bytes 454664 | tf_op jit(solution)/shard_map/ppermute | solution.py:634
  (53 other events, 339.2 us)
Sparse Core Ops, SparseCore 0:
  10.9 74.1 all-gather.1
